TPU v7x, 32 devices: a whole 2x2x4 slice. The times are simulated.
32 devices in a mesh: rep: 1, ep: 32 (over z, y, x, core).
Axes of the slice: x: 2, y: 2, z: 4, core: 2. Of those that a mesh axis runs over, the one named last changes fastest.
Arguments:
- tokens: bfloat16 [4096, 3584], P(('rep', 'ep')), may hold values from -6 to 6
- route_token: int32 [2048], P(('rep', 'ep')), may hold values from 0 to 127
- route_expert: int32 [2048, 1], P(('rep', 'ep')), may hold values from 0 to 3; in each aligned block of 64 rows (0 to 63, 64 to 127, ...) at most 24 rows name the same one
- route_gate: float32 [2048], P(('rep', 'ep')), may hold values from 0.25 to 2.5
- w_in: bfloat16 [32, 3584, 256], P('ep'), may hold values from -0.09375 to 0.09375
- w_out: bfloat16 [32, 128, 3584], P('ep'), may hold values from -0.1875 to 0.1875
- swap_pairs: int32 [16], replicated, may hold values 0 or 1
Outputs:
- mixed: bfloat16 [4096, 3584], P(('rep', 'ep'))
- saved_hidden: bfloat16 [32, 768, 128], P(('rep', 'ep'))
Inputs may be any that keep to these rules, and one draw needn't show every extreme that they name: `route_expert`: in each block of 64 rows (the rows of one device) no expert is named by more than 24 rows, and some block names an expert exactly 24 times.
All inputs are finite; a program needn't handle non-finite values.
Results may differ from a plain program's by a relative error of at most 0.0057.
Values may be sent and summed in bfloat16 or wider, within the bound.
No kernel may reach another device: no remote copies, remote signals or barrier semaphores. Data moves between devices by JAX's collectives and lax.ppermute only.
A program may use at most 64 MiB of HBM per device.

v0:
```python
import jax
import jax.numpy as jnp
from jax import lax
from jax.sharding import PartitionSpec as P

SLICES = 8


def from_behind(value, axis, steps):
    count = lax.axis_size(axis)
    pairs = [(source, (source + steps) % count) for source in range(count)]
    return lax.ppermute(value, axis, pairs)


def shards(tokens, route_token, route_expert, route_gate, w_in, w_out, swap_pairs):
    devices = lax.axis_size("ep")
    half_axis = devices // 2
    feature_width = tokens.shape[1]
    slice_units = w_out.shape[1]
    rows_dev = route_token.shape[0]
    tok_count = tokens.shape[0]
    experts = devices // SLICES
    capacity = min(rows_dev, 3 * rows_dev // (2 * experts))
    own_index = lax.axis_index("ep")
    flag_mine = swap_pairs[own_index % half_axis]
    device_ids = jnp.arange(devices, dtype=jnp.int32)
    expert_ids = route_expert[:, 0]
    expert_range = jnp.arange(experts, dtype=jnp.int32)
    expert_hits = (expert_ids[:, None] == expert_range[None, :]).astype(jnp.int32)
    slot_index = jnp.sum((jnp.cumsum(expert_hits, axis=0) - 1) * expert_hits, axis=1)
    slot_table = (expert_ids[None, None, :] == expert_range[:, None, None]) & (
        slot_index[None, None, :] == jnp.arange(capacity, dtype=jnp.int32)[None, :, None]
    )
    picked = jnp.take(tokens, route_token, axis=0)
    expert_buf = jnp.einsum(
        "ecr,rd->ecd", slot_table.astype(jnp.bfloat16), picked, preferred_element_type=jnp.float32
    ).astype(jnp.bfloat16)
    served_in = w_in[0]
    served_out = w_out[0]
    served_expert = device_ids // SLICES
    outgoing = jnp.take(expert_buf, served_expert, axis=0)
    arrived = lax.all_to_all(outgoing, "ep", split_axis=0, concat_axis=0, tiled=True)
    item_count = arrived.shape[1]
    flat_rows = arrived.reshape(-1, feature_width)
    gate_up = jnp.dot(flat_rows, served_in, preferred_element_type=jnp.float32)
    hidden = (jax.nn.silu(gate_up[:, :slice_units]) * gate_up[:, slice_units:]).astype(jnp.bfloat16)
    partial_value = jnp.dot(hidden, served_out, preferred_element_type=jnp.float32).astype(
        jnp.bfloat16
    )
    returned = lax.all_to_all(
        partial_value.reshape(devices, item_count, feature_width),
        "ep",
        split_axis=0,
        concat_axis=0,
        tiled=True,
    )
    returned, hidden_rows = (returned, hidden.reshape(devices, item_count, slice_units))
    owner_table = (served_expert[:, None] == expert_range[None, :]).astype(jnp.bfloat16)
    combined = jnp.einsum("je,jcd->ecd", owner_table, returned, preferred_element_type=jnp.float32)
    row_values = jnp.einsum(
        "ecr,ecd->rd", slot_table.astype(jnp.float32), combined, precision=lax.Precision.HIGHEST
    )
    token_table = (jnp.arange(tok_count, dtype=jnp.int32)[:, None] == route_token[None, :]).astype(
        jnp.float32
    )
    token_table = token_table * route_gate[None, :]
    mixed = jnp.dot(token_table, row_values, precision=lax.Precision.HIGHEST).astype(jnp.bfloat16)
    moved_hidden = from_behind(hidden_rows, "ep", half_axis)
    saved_rows = jnp.where(flag_mine == 1, moved_hidden, hidden_rows)
    return (mixed, saved_rows.reshape(1, devices * capacity, slice_units))


def solution(mesh):
    return jax.shard_map(
        shards,
        mesh=mesh,
        in_specs=(
            P(("rep", "ep"), None),
            P(("rep", "ep")),
            P(("rep", "ep"), None),
            P(("rep", "ep")),
            P("ep", None, None),
            P("ep", None, None),
            P(),
        ),
        out_specs=(P(("rep", "ep"), None), P(("rep", "ep"), None, None)),
        check_vma=False,
    )
```

profile of v0, /device:TPU:0, one launch (start us, length us, event | category | flops | bytes accessed | tf_op | source)
XLA Modules:
  0.0 294.6 jit_solution(460362654003883774)
XLA Ops:
  0.6 0.0 copy-start
  0.6 0.9 fusion.14
  1.5 0.7 iota_compare_fusion.5
  2.2 0.7 compare_select_fusion.1
  2.8 0.7 compare_and_fusion
  3.5 0.1 reduce_window_sum.11
  3.6 0.8 select_reduce_fusion
  4.5 2.6 gather_fusion
  7.1 0.4 convolution_convert_fusion.2
  7.5 3.3 %gather_fusion.1 = bf16[32,24,3584]{2,1,0:T(8,128)(2,1)} fusion(bf16[4,24,3584]{2,1,0:T(8,128)(2,1)S(1)} %convolution_convert_fusion.2, s32[1024]{0:T(1024)S(1)} %pad_clamp_fusion), kind=kCustom, calls=%fused_computation.1 | custom fusion | bytes 11010176 | tf_op jit(solution)/shard_map/jit(_take)/gather | solution.py:41
  10.8 3.1 %broadcast_select_fusion = bf16[32,24,3584]{2,1,0:T(8,128)(2,1)S(1)} fusion(bf16[32,24,3584]{2,1,0:T(8,128)(2,1)} %gather_fusion.1, pred[32]{0:T(512)(128)(4,1)S(1)} %compare_and_fusion.1), kind=kLoop, calls=%fused_computation.5 | loop fusion | flops 2752512 | bytes 11010080 | tf_op jit(solution)/shard_map/jit(_take)/select_n | solution.py:41
  13.9 130.2 %all_to_all.10 = bf16[32,24,3584]{2,1,0:T(8,128)(2,1)S(1)} all-to-all(bf16[32,24,3584]{2,1,0:T(8,128)(2,1)S(1)} %broadcast_select_fusion), channel_id=1, replica_groups=mesh['rep'=1,'ep'=32] {'ep'}, dimensions={0} | all-to-all | bytes 11010048 | tf_op jit(solution)/shard_map/all_to_all | solution.py:42
  144.2 1.6 fusion.2
  145.7 0.1 fusion.9
  145.9 4.0 %convolution_convert_fusion = bf16[768,3584]{1,0:T(8,128)(2,1)} fusion(bf16[768,128]{1,0:T(8,128)(2,1)S(1)} %fusion.9, bf16[1,128,3584]{2,1,0:T(8,128)(2,1)S(1)} %copy-done.1), kind=kOutput, calls=%fused_computation.2 | convolution fusion | flops 707395584 | bytes 6619136 | tf_op jit(solution)/shard_map/dot_general | solution.py:47
  149.9 3.7 %all-to-all-start.1 = ((bf16[32,24,3584]{2,1,0:T(8,128)(2,1)}), bf16[32,24,3584]{2,1,0:T(8,128)(2,1)}, u32[]{:S(2)}, u32[]{:S(2)}) async-start(bf16[32,24,3584]{2,1,0:T(8,128)(2,1)} %bitcast.25), calls=%async_computation.1 | async-start | bytes 11010048 | tf_op jit(solution)/shard_map/all_to_all | solution.py:50
  153.6 0.0 copy-start.2
  153.7 2.7 collective-permute-start
  156.3 0.6 dynamic_slice.3
  157.6 126.9 %collective-permute-done = bf16[32,24,128]{2,1,0:T(8,128)(2,1)S(1)} collective-permute-done((bf16[32,24,128]{2,1,0:T(8,128)(2,1)S(1)}, bf16[32,24,128]{2,1,0:T(8,128)(2,1)S(1)}, u32[]{:S(2)}, u32[]{:S(2)}) %collective-permute-start) | collective-permute-done | bytes 196640 | tf_op jit(solution)/shard_map/ppermute | solution.py:12
  284.5 0.7 broadcast_select_fusion.1
  285.2 5.7 %fusion = f32[4,24,3584]{2,0,1:T(4,128)S(1)} fusion(bf16[32,24,3584]{2,1,0:T(8,128)(2,1)} %all-to-all-done.1, s32[32]{0:T(128)S(1)} %and_select_fusion.1), kind=kOutput, calls=%fused_computation.3 | convolution fusion | flops 22020224 | bytes 6881408 | tf_op jit(solution)/shard_map/je,jcd->ecd/dot_general | solution.py:59
  291.0 1.1 convolution_bitcast_fusion
  292.1 2.5 convolution_convert_fusion.1
  (15 shorter events, 0.1 us)
Async XLA Ops:
  0.6 143.5 %copy-start = (bf16[1,3584,256]{2,1,0:T(8,128)(2,1)S(1)}, bf16[1,3584,256]{2,1,0:T(8,128)(2,1)}, u32[]{:S(2)}) copy-start(bf16[1,3584,256]{2,1,0:T(8,128)(2,1)} %param.11) | copy-start | bytes 5505028
  144.2 1.7 copy-start.1
  149.9 6.4 %copy-start.4 = (s32[16]{0:T(128)S(1)}, s32[16]{0:T(128)}, u32[]{:S(2)}) copy-start(s32[16]{0:T(128)} %param.13) | copy-start | bytes 196
  149.9 135.3 %all-to-all-start.1 = ((bf16[32,24,3584]{2,1,0:T(8,128)(2,1)}), bf16[32,24,3584]{2,1,0:T(8,128)(2,1)}, u32[]{:S(2)}, u32[]{:S(2)}) async-start(bf16[32,24,3584]{2,1,0:T(8,128)(2,1)} %bitcast.25), calls=%async_computation.1 | async-start | bytes 11010048 | tf_op jit(solution)/shard_map/all_to_all | solution.py:50
  153.6 138.4 %copy-start.2 = (s32[64]{0:T(128)S(1)}, s32[64]{0:T(128)}, u32[]{:S(2)}) copy-start(s32[64]{0:T(128)} %param.8) | copy-start | bytes 772
  153.7 138.4 %copy-start.3 = (f32[64]{0:T(128)S(1)}, f32[64]{0:T(128)}, u32[]{:S(2)}) copy-start(f32[64]{0:T(128)} %param.10) | copy-start | bytes 772
  153.7 130.8 %collective-permute-start = (bf16[32,24,128]{2,1,0:T(8,128)(2,1)S(1)}, bf16[32,24,128]{2,1,0:T(8,128)(2,1)S(1)}, u32[]{:S(2)}, u32[]{:S(2)}) collective-permute-start(bf16[32,24,128]{2,1,0:T(8,128)(2,1)S(1)} %bitcast.27), channel_id=1, source_target_pairs={{0,16},{1,17},{2,18},{3,19},{4,20},{5,21},{6,22},{7,23},{8,24},{9,... | collective-permute-start | bytes 589832 | tf_op jit(solution)/shard_map/ppermute | solution.py:12
where the time goes:
time: 295 us
  blocking collectives  130 us (44%)
  waiting for transfers between devices  127 us (43%)
  matrix products  15.3 us (5%)
  other arithmetic  7.77 us (3%)
  local copies, waits for them, and re-layouts  6.48 us (2%)
  starting transfers between devices  6.37 us (2%)
    all_to_all x1, blocking collectives, shards(): lax.all_to_all(outgoing, 'ep', split_axis=0, concat_axis=0, tiled=True)  130 us
    ppermute x1, waiting for transfers between devices, from_behind(): return lax.ppermute(value, axis, pairs)  127 us
  transfers between devices with their start and end apart: 2, of which 1 were waited for; matrix products, arithmetic and copies ran while one was open for 0% of the time, Pallas kernels for 0%

commit v1 on v0

v1 whole, which is shorter than its diff:
```python
import functools

import jax
import jax.numpy as jnp
from jax import lax
from jax.experimental import pallas as pl
from jax.experimental.pallas import tpu as pltpu
from jax.sharding import PartitionSpec as P

SLICES = 8
CORE, FIRST, SECOND = 1, 2, 4
VMEM = pl.BlockSpec(memory_space=pltpu.VMEM)
SMEM = pl.BlockSpec(memory_space=pltpu.SMEM)
VMEM_LIMIT = 48 * 1024 * 1024


def swap(value, mask_of):
    count = lax.axis_size("ep")
    return lax.ppermute(value, "ep", [(i, i ^ mask_of(i)) for i in range(count)])


def lane(i):
    return FIRST if i & CORE == 0 else SECOND


def cross(i):
    return SECOND if i & CORE == 0 else FIRST


def column_tile(width):
    return next(t for t in (512, 256, 128, width) if width % t == 0)


def route_kernel(experts, capacity, layer_ref, expert_ref, token_ref, gate_ref, tok_ref, *outs):
    bufs, (hi_ref, lo_ref) = outs[:experts], outs[experts:]
    rows = expert_ref.shape[1]
    tok_count, width = tok_ref.shape
    places = experts * capacity
    relative = expert_ref[...] ^ layer_ref[0]
    ranks = -(-experts // 8) * 8
    hits = (lax.broadcasted_iota(jnp.int32, (ranks, rows), 0) == relative).astype(jnp.float32)
    earlier = lax.broadcasted_iota(jnp.int32, (rows, rows), 0) < lax.broadcasted_iota(
        jnp.int32, (rows, rows), 1
    )
    before = jnp.dot(
        hits.astype(jnp.bfloat16),
        earlier.astype(jnp.float32).astype(jnp.bfloat16),
        preferred_element_type=jnp.float32,
    )
    slot = jnp.sum(hits * before, axis=0, keepdims=True).astype(jnp.int32)
    target = relative * capacity + slot
    place_hot = (lax.broadcasted_iota(jnp.int32, (places, rows), 0) == target).astype(jnp.float32)
    token_hot = (lax.broadcasted_iota(jnp.int32, (tok_count, rows), 0) == token_ref[...]).astype(
        jnp.float32
    )
    place_hot = place_hot.astype(jnp.bfloat16)
    gate = gate_ref[...]
    gate_hi = gate.astype(jnp.bfloat16).astype(jnp.float32)
    gate_lo = gate - gate_hi
    contract = (((1,), (1,)), ((), ()))
    for part, ref in ((gate_hi, hi_ref), (gate_lo, lo_ref)):
        ref[...] = lax.dot_general(
            (token_hot * part).astype(jnp.bfloat16),
            place_hot,
            contract,
            preferred_element_type=jnp.float32,
        ).astype(jnp.bfloat16)
    pick = lax.dot_general(
        place_hot, token_hot.astype(jnp.bfloat16), contract, preferred_element_type=jnp.float32
    ).astype(jnp.bfloat16)
    tile = column_tile(width)
    for at in range(0, width, tile):
        picked = jnp.dot(pick, tok_ref[:, at : at + tile], preferred_element_type=jnp.float32)
        for s in range(experts):
            bufs[s][:, at : at + tile] = picked[s * capacity : (s + 1) * capacity].astype(
                jnp.bfloat16
            )


def expert_kernel(count, place_ref, *refs):
    pieces = refs[:count]
    win_a, win_b, wout_a, wout_b = refs[count : count + 4]
    outs = refs[count + 4 : 2 * count + 4]
    hid_a, hid_b = refs[2 * count + 4 : 2 * count + 6]
    rows_ref, acc_ref, hidden_ref, wout_ref = refs[2 * count + 6 :]
    capacity, width = pieces[0].shape
    units = wout_a.shape[0]
    tile = column_tile(width)
    wout_ref[:units] = wout_a[...]
    wout_ref[units:] = wout_b[...]
    acc_ref[...] = jnp.zeros_like(acc_ref)

    @pl.loop(0, width // tile)
    def _(k):
        cols = pl.ds(pl.multiple_of(k * tile, tile), tile)
        rows_ref[...] = jnp.concatenate(
            [piece[:, cols].astype(jnp.float32) for piece in pieces], axis=0
        ).astype(jnp.bfloat16)
        rows = rows_ref[...]
        acc_ref[:, : 2 * units] += jnp.dot(
            rows, win_a[cols, :], preferred_element_type=jnp.float32
        )
        acc_ref[:, 2 * units :] += jnp.dot(
            rows, win_b[cols, :], preferred_element_type=jnp.float32
        )

    for half, hid in ((0, hid_a), (1, hid_b)):
        base = 2 * units * half
        gate, up = acc_ref[:, base : base + units], acc_ref[:, base + units : base + 2 * units]
        value = gate / (1.0 + jnp.exp(-gate)) * up
        hidden_ref[:, units * half : units * (half + 1)] = value.astype(jnp.bfloat16)
        for i in range(count):
            hid[place_ref[i]] = value[i * capacity : (i + 1) * capacity].astype(jnp.bfloat16)

    @pl.loop(0, width // tile)
    def _(k):
        cols = pl.ds(pl.multiple_of(k * tile, tile), tile)
        out = jnp.dot(hidden_ref[...], wout_ref[:, cols], preferred_element_type=jnp.float32)
        for i in range(count):
            outs[i][:, cols] = out[i * capacity : (i + 1) * capacity].astype(jnp.bfloat16)


def mix_kernel(experts, hi_ref, lo_ref, *refs):
    own, came = refs[:3], refs[3 : 2 + experts]
    mixed_ref = refs[2 + experts]
    capacity, width = own[0].shape
    tile = column_tile(width)
    for at in range(0, width, tile):
        cols = slice(at, at + tile)
        local = sum(r[:, cols].astype(jnp.float32) for r in own).astype(jnp.bfloat16)
        values = [local.astype(jnp.float32)] + [r[:, cols].astype(jnp.float32) for r in came]
        rows = jnp.concatenate(values, axis=0).astype(jnp.bfloat16)
        total = jnp.dot(hi_ref[...], rows, preferred_element_type=jnp.float32)
        total += jnp.dot(lo_ref[...], rows, preferred_element_type=jnp.float32)
        mixed_ref[:, cols] = total.astype(jnp.bfloat16)


def shards(tokens, route_token, route_expert, route_gate, w_in, w_out, swap_pairs):
    devices = lax.axis_size("ep")
    half_axis = devices // 2
    tok_count, width = tokens.shape
    units = w_out.shape[1]
    rows_dev = route_token.shape[0]
    experts = devices // SLICES
    capacity = min(rows_dev, 3 * rows_dev // (2 * experts))
    places = experts * capacity
    me = lax.axis_index("ep")
    layer = me // SLICES
    flag = swap_pairs[me % half_axis]
    params = pltpu.CompilerParams(vmem_limit_bytes=VMEM_LIMIT)
    block = jax.ShapeDtypeStruct((capacity, width), jnp.bfloat16)

    win_b = swap(w_in[0], lambda i: CORE)
    wout_b = swap(w_out[0], lambda i: CORE)

    mix_shape = jax.ShapeDtypeStruct((tok_count, places), jnp.bfloat16)
    *bufs, gate_hi, gate_lo = pl.pallas_call(
        functools.partial(route_kernel, experts, capacity),
        out_shape=[block] * experts + [mix_shape] * 2,
        in_specs=[SMEM] + [VMEM] * 4,
        out_specs=[VMEM] * (experts + 2),
        compiler_params=params,
    )(
        layer.reshape(1),
        route_expert.reshape(1, rows_dev),
        route_token.reshape(1, rows_dev),
        route_gate.reshape(1, rows_dev),
        tokens,
    )

    pieces, spots = [], []
    chip = (me % SLICES) // 2
    lane_mask = jnp.where(me % 2 == 0, FIRST, SECOND) // 2
    cross_mask = jnp.where(me % 2 == 0, SECOND, FIRST) // 2
    for s in range(experts):
        mine = bufs[s] if s == 0 else swap(bufs[s], lambda i: SLICES * s)
        beside = swap(mine, lane)
        across = swap(mine, cross)
        corner = swap(beside, cross)
        pieces += [mine, beside, across, corner]
        row = (layer ^ s) * (SLICES // 2)
        spots += [
            row + chip,
            row + (chip ^ lane_mask),
            row + (chip ^ cross_mask),
            row + (chip ^ lane_mask ^ cross_mask),
        ]
    count = len(pieces)
    hid_shape = jax.ShapeDtypeStruct((count, capacity, units), jnp.bfloat16)
    flops = 2 * count * capacity * width * units * 6
    *outs, hid_a, hid_b = pl.pallas_call(
        functools.partial(expert_kernel, count),
        out_shape=[block] * count + [hid_shape] * 2,
        in_specs=[SMEM] + [VMEM] * (count + 4),
        out_specs=[VMEM] * (count + 2),
        scratch_shapes=[
            pltpu.VMEM((count * capacity, column_tile(width)), jnp.bfloat16),
            pltpu.VMEM((count * capacity, 4 * units), jnp.float32),
            pltpu.VMEM((count * capacity, 2 * units), jnp.bfloat16),
            pltpu.VMEM((2 * units, width), jnp.bfloat16),
        ],
        compiler_params=params,
        cost_estimate=pl.CostEstimate(
            flops=flops, bytes_accessed=20 * 1024 * 1024, transcendentals=0
        ),
    )(jnp.stack(spots).astype(jnp.int32), *pieces, w_in[0], win_b, w_out[0], wout_b)

    own, came = None, []
    for s in reversed(range(experts)):
        mine, beside, across, corner = outs[4 * s : 4 * s + 4]
        relay = beside.astype(jnp.float32) + swap(corner, cross).astype(jnp.float32)
        from_lane = swap(relay.astype(jnp.bfloat16), lane)
        from_cross = swap(across, cross)
        if s == 0:
            own = [mine, from_lane, from_cross]
        else:
            total = sum(v.astype(jnp.float32) for v in (mine, from_lane, from_cross))
            came.insert(0, swap(total.astype(jnp.bfloat16), lambda i: SLICES * s))

    mixed = pl.pallas_call(
        functools.partial(mix_kernel, experts),
        out_shape=jax.ShapeDtypeStruct((tok_count, width), jnp.bfloat16),
        in_specs=[VMEM] * (4 + experts),
        out_specs=VMEM,
        compiler_params=params,
    )(gate_hi, gate_lo, *own, *came)

    other = swap(hid_b, lambda i: CORE)
    far_own = swap(hid_a, lambda i: half_axis)
    far_other = swap(hid_b, lambda i: half_axis ^ CORE)
    kept = jnp.where(flag == 1, far_own, hid_a)
    rest = jnp.where(flag == 1, far_other, other)
    even = me % 2 == 0
    saved = jnp.stack([jnp.where(even, kept, rest), jnp.where(even, rest, kept)], axis=1)
    return (mixed, saved.reshape(1, devices * capacity, units))


def solution(mesh):
    return jax.shard_map(
        shards,
        mesh=mesh,
        in_specs=(
            P(("rep", "ep"), None),
            P(("rep", "ep")),
            P(("rep", "ep"), None),
            P(("rep", "ep")),
            P("ep", None, None),
            P("ep", None, None),
            P(),
        ),
        out_specs=(P(("rep", "ep"), None), P(("rep", "ep"), None, None)),
        check_vma=False,
    )
```

time: 295 us -> 125 us (0.42)
  blocking collectives: 130 us -> 0 us
  waiting for transfers between devices: 127 us -> 56 us
  starting transfers between devices: 6.37 us -> 40.3 us
  matrix products: 15.3 us -> 0 us
  local copies, waits for them, and re-layouts: 6.48 us -> 16.7 us
  Pallas kernels: 0 us -> 10.1 us
  other arithmetic: 7.77 us -> 0.44 us
    all_to_all x1 -> x0, blocking collectives: 130 us -> none  [shards(): lax.all_to_all(outgoing, 'ep', split_axis=0, concat_axis=0, tiled=True)]
    ppermute x1 -> x35, waiting for transfers between devices: 127 us -> 56 us  [swap(): lax.ppermute(value, 'ep', [(i, i ^ mask_of(i)) for i in range(count)])]
    ppermute x1 -> x35, starting transfers between devices: 2.65 us -> 40.3 us  [swap(): lax.ppermute(value, 'ep', [(i, i ^ mask_of(i)) for i in range(count)])]
    dot_general x6 -> x0, matrix products: 15.3 us -> none  [the longest x1 5.75 us: shards(): jnp.einsum('je,jcd->ecd', owner_table, returned, preferred_element_type=j...]
    unnamed x10 -> x56, local copies, waits for them, and re-layouts: 0.03 us -> 15.3 us
    pallas_call x0 -> x3, Pallas kernels: none -> 10.1 us  [the longest x1 7.91 us: shards(): pl.pallas_call(functools.partial(expert_kernel, count), out_shape=[block]...]
    gather x2 -> x0, local copies, waits for them, and re-layouts: 5.87 us -> none  [the longest x1 3.29 us: shards(): outgoing = jnp.take(expert_buf, served_expert, axis=0)]
    select_n x5 -> x0, other arithmetic: 4.52 us -> none  [the longest x2 3.16 us: shards(): outgoing = jnp.take(expert_buf, served_expert, axis=0)]
  transfers between devices with their start and end apart: 2 -> 35, of which waited for: 1 -> 19; matrix products, arithmetic and copies ran while one was open for 0% -> 1% of each run, Pallas kernels for 0% -> 1%
where the time goes in v1:
time: 125 us
  waiting for transfers between devices  56 us (45%)
  starting transfers between devices  40.3 us (32%)
  local copies, waits for them, and re-layouts  16.7 us (13%)
  Pallas kernels  10.1 us (8%)
  between operations  1.47 us (1%)
    ppermute x35, waiting for transfers between devices, swap(): lax.ppermute(value, 'ep', [(i, i ^ mask_of(i)) for i in range(count)])  56 us
    ppermute x35, starting transfers between devices, swap(): lax.ppermute(value, 'ep', [(i, i ^ mask_of(i)) for i in range(count)])  40.3 us
    unnamed x56, local copies, waits for them, and re-layouts  15.3 us
    pallas_call x1, Pallas kernels, shards(): pl.pallas_call(functools.partial(expert_kernel, count), out_shape=[block]...  7.91 us
  transfers between devices with their start and end apart: 35, of which 19 were waited for; matrix products, arithmetic and copies ran while one was open for 1% of the time, Pallas kernels for 1%

profile of v1, /device:TPU:0, one launch (start us, length us, event | category | flops | bytes accessed | tf_op | source)
XLA Modules:
  0.0 125.1 jit_solution(18075721153027410823)
XLA Ops:
  6.2 3.0 %collective-permute-start.3 = (bf16[24,3584]{1,0:T(8,128)(2,1)S(1)}, bf16[24,3584]{1,0:T(8,128)(2,1)S(1)}, u32[]{:S(2)}, u32[]{:S(2)}) collective-permute-start(bf16[24,3584]{1,0:T(8,128)(2,1)S(1)} %get-tuple-element.29), channel_id=1, source_target_pairs={{0,8},{1,9},{2,10},{3,11},{4,12},{5,13},{6,14},{7,15},{8,0},{9,1},... | collective-permute-start | bytes 516104 | tf_op jit(solution)/shard_map/ppermute | solution.py:19
  9.2 2.6 %collective-permute-start.7 = (bf16[24,3584]{1,0:T(8,128)(2,1)S(1)}, bf16[24,3584]{1,0:T(8,128)(2,1)S(1)}, u32[]{:S(2)}, u32[]{:S(2)}) collective-permute-start(bf16[24,3584]{1,0:T(8,128)(2,1)S(1)} %get-tuple-element.30), channel_id=1, source_target_pairs={{0,16},{1,17},{2,18},{3,19},{4,20},{5,21},{6,22},{7,23},{8,24},{9,... | collective-permute-start | bytes 516104 | tf_op jit(solution)/shard_map/ppermute | solution.py:19
  11.8 5.0 %collective-permute-done.3.refs_4_ = bf16[24,3584]{1,0:T(8,128)(2,1)S(1)} collective-permute-done((bf16[24,3584]{1,0:T(8,128)(2,1)S(1)}, bf16[24,3584]{1,0:T(8,128)(2,1)S(1)}, u32[]{:S(2)}, u32[]{:S(2)}) %collective-permute-start.3) | collective-permute-done | bytes 172064 | tf_op jit(solution)/shard_map/ppermute | solution.py:19
  16.8 1.8 %collective-permute-start.1 = (bf16[24,3584]{1,0:T(8,128)(2,1)S(1)}, bf16[24,3584]{1,0:T(8,128)(2,1)S(1)}, u32[]{:S(2)}, u32[]{:S(2)}) collective-permute-start(bf16[24,3584]{1,0:T(8,128)(2,1)S(1)} %get-tuple-element.28.refs_0_), channel_id=1, source_target_pairs={{0,4},{1,3},{2,6},{3,1},{4,0},{5,7},{6,2},{7,5},{8,12},{9,11},{10,... | collective-permute-start | bytes 516104 | tf_op jit(solution)/shard_map/ppermute | solution.py:19
  18.6 6.2 %collective-permute-done.7.refs_8_ = bf16[24,3584]{1,0:T(8,128)(2,1)S(1)} collective-permute-done((bf16[24,3584]{1,0:T(8,128)(2,1)S(1)}, bf16[24,3584]{1,0:T(8,128)(2,1)S(1)}, u32[]{:S(2)}, u32[]{:S(2)}) %collective-permute-start.7) | collective-permute-done | bytes 172064 | tf_op jit(solution)/shard_map/ppermute | solution.py:19
  28.3 3.7 %collective-permute-done.refs_1_ = bf16[24,3584]{1,0:T(8,128)(2,1)S(1)} collective-permute-done((bf16[24,3584]{1,0:T(8,128)(2,1)S(1)}, bf16[24,3584]{1,0:T(8,128)(2,1)S(1)}, u32[]{:S(2)}, u32[]{:S(2)}) %collective-permute-start) | collective-permute-done | bytes 172064 | tf_op jit(solution)/shard_map/ppermute | solution.py:19
  38.2 2.3 %collective-permute-done.8.refs_9_ = bf16[24,3584]{1,0:T(8,128)(2,1)S(1)} collective-permute-done((bf16[24,3584]{1,0:T(8,128)(2,1)S(1)}, bf16[24,3584]{1,0:T(8,128)(2,1)S(1)}, u32[]{:S(2)}, u32[]{:S(2)}) %collective-permute-start.8) | collective-permute-done | bytes 172064 | tf_op jit(solution)/shard_map/ppermute | solution.py:19
  40.5 1.8 %collective-permute-start.2 = (bf16[24,3584]{1,0:T(8,128)(2,1)S(1)}, bf16[24,3584]{1,0:T(8,128)(2,1)S(1)}, u32[]{:S(2)}, u32[]{:S(2)}) collective-permute-start(bf16[24,3584]{1,0:T(8,128)(2,1)S(1)} %collective-permute-done.refs_1_), channel_id=1, source_target_pairs={{0,4},{1,3},{2,6},{3,1},{4,0},{5,7},{6,2},{7,5},{8,12},{9,11},{10,... | collective-permute-start | bytes 516104 | tf_op jit(solution)/shard_map/ppermute | solution.py:19
  42.5 2.2 %collective-permute-done.12.refs_13_ = bf16[24,3584]{1,0:T(8,128)(2,1)S(1)} collective-permute-done((bf16[24,3584]{1,0:T(8,128)(2,1)S(1)}, bf16[24,3584]{1,0:T(8,128)(2,1)S(1)}, u32[]{:S(2)}, u32[]{:S(2)}) %collective-permute-start.12) | collective-permute-done | bytes 172064 | tf_op jit(solution)/shard_map/ppermute | solution.py:19
  56.3 7.9 %shard_map.87 = (bf16[24,3584]{1,0:T(8,128)(2,1)S(1)}, bf16[24,3584]{1,0:T(8,128)(2,1)S(1)}, bf16[24,3584]{1,0:T(8,128)(2,1)S(1)}, bf16[24,3584]{1,0:T(8,128)(2,...) custom-call(s32[16]{0:T(128)S(1)} %stack.76.place_ref, ...), custom_call_target="tpu_custom_call" | custom-call | flops 2113929216 | bytes 20971520 | tf_op jit(solution)/shard_map/pallas_call | solution.py:191
  72.2 2.5 %collective-permute-start.33 = (bf16[16,24,128]{2,1,0:T(8,128)(2,1)}, bf16[16,24,128]{2,1,0:T(8,128)(2,1)S(1)}, u32[]{:S(2)}, u32[]{:S(2)}) collective-permute-start(bf16[16,24,128]{2,1,0:T(8,128)(2,1)} %copy-done.26), channel_id=1, source_target_pairs={{0,17},{1,16},{2,19},{3,18},{4,21},{5,20},{6,23},{7,22},{8,25},{9,... | collective-permute-start | bytes 294920 | tf_op jit(solution)/shard_map/ppermute | solution.py:19
  77.3 3.5 %collective-permute-done.20 = bf16[24,3584]{1,0:T(8,128)(2,1)S(1)} collective-permute-done((bf16[24,3584]{1,0:T(8,128)(2,1)}, bf16[24,3584]{1,0:T(8,128)(2,1)S(1)}, u32[]{:S(2)}, u32[]{:S(2)}) %collective-permute-start.20) | collective-permute-done | bytes 172064 | tf_op jit(solution)/shard_map/ppermute | solution.py:19
  81.6 4.8 %collective-permute-done.24 = bf16[24,3584]{1,0:T(8,128)(2,1)S(1)} collective-permute-done((bf16[24,3584]{1,0:T(8,128)(2,1)}, bf16[24,3584]{1,0:T(8,128)(2,1)S(1)}, u32[]{:S(2)}, u32[]{:S(2)}) %collective-permute-start.24) | collective-permute-done | bytes 172064 | tf_op jit(solution)/shard_map/ppermute | solution.py:19
  87.2 5.3 %collective-permute-done.28 = bf16[24,3584]{1,0:T(8,128)(2,1)S(1)} collective-permute-done((bf16[24,3584]{1,0:T(8,128)(2,1)}, bf16[24,3584]{1,0:T(8,128)(2,1)S(1)}, u32[]{:S(2)}, u32[]{:S(2)}) %collective-permute-start.28) | collective-permute-done | bytes 172064 | tf_op jit(solution)/shard_map/ppermute | solution.py:19
  92.5 1.8 %collective-permute-start.21 = (bf16[24,3584]{1,0:T(8,128)(2,1)S(1)}, bf16[24,3584]{1,0:T(8,128)(2,1)S(1)}, u32[]{:S(2)}, u32[]{:S(2)}) collective-permute-start(bf16[24,3584]{1,0:T(8,128)(2,1)S(1)} %add_convert_fusion.5), channel_id=1, source_target_pairs={{0,2},{1,5},{2,0},{3,7},{4,6},{5,1},{6,4},{7,3},{8,10},{9,13},{10,... | collective-permute-start | bytes 516104 | tf_op jit(solution)/shard_map/ppermute | solution.py:19
  94.5 4.4 %collective-permute-done.21 = bf16[24,3584]{1,0:T(8,128)(2,1)S(1)} collective-permute-done((bf16[24,3584]{1,0:T(8,128)(2,1)S(1)}, bf16[24,3584]{1,0:T(8,128)(2,1)S(1)}, u32[]{:S(2)}, u32[]{:S(2)}) %collective-permute-start.21) | collective-permute-done | bytes 172064 | tf_op jit(solution)/shard_map/ppermute | solution.py:19
  98.9 2.4 %collective-permute-start.25 = (bf16[24,3584]{1,0:T(8,128)(2,1)S(1)}, bf16[24,3584]{1,0:T(8,128)(2,1)S(1)}, u32[]{:S(2)}, u32[]{:S(2)}) collective-permute-start(bf16[24,3584]{1,0:T(8,128)(2,1)S(1)} %add_convert_fusion.3), channel_id=1, source_target_pairs={{0,2},{1,5},{2,0},{3,7},{4,6},{5,1},{6,4},{7,3},{8,10},{9,13},{10,... | collective-permute-start | bytes 516104 | tf_op jit(solution)/shard_map/ppermute | solution.py:19
  101.5 4.6 %collective-permute-done.25 = bf16[24,3584]{1,0:T(8,128)(2,1)S(1)} collective-permute-done((bf16[24,3584]{1,0:T(8,128)(2,1)S(1)}, bf16[24,3584]{1,0:T(8,128)(2,1)S(1)}, u32[]{:S(2)}, u32[]{:S(2)}) %collective-permute-start.25) | collective-permute-done | bytes 172064 | tf_op jit(solution)/shard_map/ppermute | solution.py:19
  106.1 1.7 %collective-permute-start.29 = (bf16[24,3584]{1,0:T(8,128)(2,1)S(1)}, bf16[24,3584]{1,0:T(8,128)(2,1)S(1)}, u32[]{:S(2)}, u32[]{:S(2)}) collective-permute-start(bf16[24,3584]{1,0:T(8,128)(2,1)S(1)} %add_convert_fusion.1), channel_id=1, source_target_pairs={{0,2},{1,5},{2,0},{3,7},{4,6},{5,1},{6,4},{7,3},{8,10},{9,13},{10,... | collective-permute-start | bytes 516104 | tf_op jit(solution)/shard_map/ppermute | solution.py:19
  108.5 3.0 %collective-permute-done.29 = bf16[24,3584]{1,0:T(8,128)(2,1)S(1)} collective-permute-done((bf16[24,3584]{1,0:T(8,128)(2,1)S(1)}, bf16[24,3584]{1,0:T(8,128)(2,1)S(1)}, u32[]{:S(2)}, u32[]{:S(2)}) %collective-permute-start.29) | collective-permute-done | bytes 172064 | tf_op jit(solution)/shard_map/ppermute | solution.py:19
  113.4 2.4 %collective-permute-start.27 = (bf16[24,3584]{1,0:T(8,128)(2,1)S(1)}, bf16[24,3584]{1,0:T(8,128)(2,1)S(1)}, u32[]{:S(2)}, u32[]{:S(2)}) collective-permute-start(bf16[24,3584]{1,0:T(8,128)(2,1)S(1)} %add_convert_fusion.2), channel_id=1, source_target_pairs={{0,16},{1,17},{2,18},{3,19},{4,20},{5,21},{6,22},{7,23},{8,24},{9,... | collective-permute-start | bytes 516104 | tf_op jit(solution)/shard_map/ppermute | solution.py:19
  115.9 1.9 %collective-permute-start.31 = (bf16[24,3584]{1,0:T(8,128)(2,1)S(1)}, bf16[24,3584]{1,0:T(8,128)(2,1)S(1)}, u32[]{:S(2)}, u32[]{:S(2)}) collective-permute-start(bf16[24,3584]{1,0:T(8,128)(2,1)S(1)} %add_convert_fusion), channel_id=1, source_target_pairs={{0,24},{1,25},{2,26},{3,27},{4,28},{5,29},{6,30},{7,31},{8,16},{9,... | collective-permute-start | bytes 516104 | tf_op jit(solution)/shard_map/ppermute | solution.py:19
  118.6 2.0 %collective-permute-done.23.refs_3_ = bf16[24,3584]{1,0:T(8,128)(2,1)S(1)} collective-permute-done((bf16[24,3584]{1,0:T(8,128)(2,1)S(1)}, bf16[24,3584]{1,0:T(8,128)(2,1)S(1)}, u32[]{:S(2)}, u32[]{:S(2)}) %collective-permute-start.23) | collective-permute-done | bytes 172064 | tf_op jit(solution)/shard_map/ppermute | solution.py:19
  120.6 3.0 %collective-permute-done.27.refs_4_ = bf16[24,3584]{1,0:T(8,128)(2,1)S(1)} collective-permute-done((bf16[24,3584]{1,0:T(8,128)(2,1)S(1)}, bf16[24,3584]{1,0:T(8,128)(2,1)S(1)}, u32[]{:S(2)}, u32[]{:S(2)}) %collective-permute-start.27) | collective-permute-done | bytes 172064 | tf_op jit(solution)/shard_map/ppermute | solution.py:19
  (117 shorter events, 43.7 us)
Async XLA Ops:
  0.6 52.0 %collective-permute-start.15 = (bf16[3584,256]{1,0:T(8,128)(2,1)}, bf16[3584,256]{1,0:T(8,128)(2,1)}, u32[]{:S(2)}, u32[]{:S(2)}) collective-permute-start(bf16[3584,256]{1,0:T(8,128)(2,1)} %bitcast.31), channel_id=1, source_target_pairs={{0,1},{1,0},{2,3},{3,2},{4,5},{5,4},{6,7},{7,6},{8,9},{9,8},{10,11... | collective-permute-start | bytes 5505032 | tf_op jit(solution)/shard_map/ppermute | solution.py:19
  1.1 51.5 %collective-permute-start.16 = (bf16[128,3584]{1,0:T(8,128)(2,1)}, bf16[128,3584]{1,0:T(8,128)(2,1)}, u32[]{:S(2)}, u32[]{:S(2)}) collective-permute-start(bf16[128,3584]{1,0:T(8,128)(2,1)} %bitcast.33), channel_id=1, source_target_pairs={{0,1},{1,0},{2,3},{3,2},{4,5},{5,4},{6,7},{7,6},{8,9},{9,8},{10,11... | collective-permute-start | bytes 2752520 | tf_op jit(solution)/shard_map/ppermute | solution.py:19
  6.2 10.6 %collective-permute-start.3 = (bf16[24,3584]{1,0:T(8,128)(2,1)S(1)}, bf16[24,3584]{1,0:T(8,128)(2,1)S(1)}, u32[]{:S(2)}, u32[]{:S(2)}) collective-permute-start(bf16[24,3584]{1,0:T(8,128)(2,1)S(1)} %get-tuple-element.29), channel_id=1, source_target_pairs={{0,8},{1,9},{2,10},{3,11},{4,12},{5,13},{6,14},{7,15},{8,0},{9,1},... | collective-permute-start | bytes 516104 | tf_op jit(solution)/shard_map/ppermute | solution.py:19
  9.2 15.5 %collective-permute-start.7 = (bf16[24,3584]{1,0:T(8,128)(2,1)S(1)}, bf16[24,3584]{1,0:T(8,128)(2,1)S(1)}, u32[]{:S(2)}, u32[]{:S(2)}) collective-permute-start(bf16[24,3584]{1,0:T(8,128)(2,1)S(1)} %get-tuple-element.30), channel_id=1, source_target_pairs={{0,16},{1,17},{2,18},{3,19},{4,20},{5,21},{6,22},{7,23},{8,24},{9,... | collective-permute-start | bytes 516104 | tf_op jit(solution)/shard_map/ppermute | solution.py:19
  11.8 14.4 %collective-permute-start.11 = (bf16[24,3584]{1,0:T(8,128)(2,1)S(1)}, bf16[24,3584]{1,0:T(8,128)(2,1)S(1)}, u32[]{:S(2)}, u32[]{:S(2)}) collective-permute-start(bf16[24,3584]{1,0:T(8,128)(2,1)S(1)} %get-tuple-element.31), channel_id=1, source_target_pairs={{0,24},{1,25},{2,26},{3,27},{4,28},{5,29},{6,30},{7,31},{8,16},{9,... | collective-permute-start | bytes 516104 | tf_op jit(solution)/shard_map/ppermute | solution.py:19
  16.8 11.0 %collective-permute-start.1 = (bf16[24,3584]{1,0:T(8,128)(2,1)S(1)}, bf16[24,3584]{1,0:T(8,128)(2,1)S(1)}, u32[]{:S(2)}, u32[]{:S(2)}) collective-permute-start(bf16[24,3584]{1,0:T(8,128)(2,1)S(1)} %get-tuple-element.28.refs_0_), channel_id=1, source_target_pairs={{0,4},{1,3},{2,6},{3,1},{4,0},{5,7},{6,2},{7,5},{8,12},{9,11},{10,... | collective-permute-start | bytes 516104 | tf_op jit(solution)/shard_map/ppermute | solution.py:19
  24.8 7.2 %collective-permute-start = (bf16[24,3584]{1,0:T(8,128)(2,1)S(1)}, bf16[24,3584]{1,0:T(8,128)(2,1)S(1)}, u32[]{:S(2)}, u32[]{:S(2)}) collective-permute-start(bf16[24,3584]{1,0:T(8,128)(2,1)S(1)} %get-tuple-element.28.refs_0_), channel_id=1, source_target_pairs={{0,2},{1,5},{2,0},{3,7},{4,6},{5,1},{6,4},{7,3},{8,10},{9,13},{10,... | collective-permute-start | bytes 516104 | tf_op jit(solution)/shard_map/ppermute | solution.py:19
  26.3 7.0 %collective-permute-start.5 = (bf16[24,3584]{1,0:T(8,128)(2,1)S(1)}, bf16[24,3584]{1,0:T(8,128)(2,1)S(1)}, u32[]{:S(2)}, u32[]{:S(2)}) collective-permute-start(bf16[24,3584]{1,0:T(8,128)(2,1)S(1)} %collective-permute-done.3.refs_4_), channel_id=1, source_target_pairs={{0,4},{1,3},{2,6},{3,1},{4,0},{5,7},{6,2},{7,5},{8,12},{9,11},{10,... | collective-permute-start | bytes 516104 | tf_op jit(solution)/shard_map/ppermute | solution.py:19
  27.8 7.3 %collective-permute-start.4 = (bf16[24,3584]{1,0:T(8,128)(2,1)S(1)}, bf16[24,3584]{1,0:T(8,128)(2,1)S(1)}, u32[]{:S(2)}, u32[]{:S(2)}) collective-permute-start(bf16[24,3584]{1,0:T(8,128)(2,1)S(1)} %collective-permute-done.3.refs_4_), channel_id=1, source_target_pairs={{0,2},{1,5},{2,0},{3,7},{4,6},{5,1},{6,4},{7,3},{8,10},{9,13},{10,... | collective-permute-start | bytes 516104 | tf_op jit(solution)/shard_map/ppermute | solution.py:19
  33.2 7.3 %collective-permute-start.8 = (bf16[24,3584]{1,0:T(8,128)(2,1)S(1)}, bf16[24,3584]{1,0:T(8,128)(2,1)S(1)}, u32[]{:S(2)}, u32[]{:S(2)}) collective-permute-start(bf16[24,3584]{1,0:T(8,128)(2,1)S(1)} %collective-permute-done.7.refs_8_), channel_id=1, source_target_pairs={{0,2},{1,5},{2,0},{3,7},{4,6},{5,1},{6,4},{7,3},{8,10},{9,13},{10,... | collective-permute-start | bytes 516104 | tf_op jit(solution)/shard_map/ppermute | solution.py:19
  35.1 7.2 %collective-permute-start.13 = (bf16[24,3584]{1,0:T(8,128)(2,1)S(1)}, bf16[24,3584]{1,0:T(8,128)(2,1)S(1)}, u32[]{:S(2)}, u32[]{:S(2)}) collective-permute-start(bf16[24,3584]{1,0:T(8,128)(2,1)S(1)} %collective-permute-done.11.refs_12_), channel_id=1, source_target_pairs={{0,4},{1,3},{2,6},{3,1},{4,0},{5,7},{6,2},{7,5},{8,12},{9,11},{10,... | collective-permute-start | bytes 516104 | tf_op jit(solution)/shard_map/ppermute | solution.py:19
  37.4 7.3 %collective-permute-start.12 = (bf16[24,3584]{1,0:T(8,128)(2,1)S(1)}, bf16[24,3584]{1,0:T(8,128)(2,1)S(1)}, u32[]{:S(2)}, u32[]{:S(2)}) collective-permute-start(bf16[24,3584]{1,0:T(8,128)(2,1)S(1)} %collective-permute-done.11.refs_12_), channel_id=1, source_target_pairs={{0,2},{1,5},{2,0},{3,7},{4,6},{5,1},{6,4},{7,3},{8,10},{9,13},{10,... | collective-permute-start | bytes 516104 | tf_op jit(solution)/shard_map/ppermute | solution.py:19
  72.1 41.4 %collective-permute-start.34 = (bf16[16,24,128]{2,1,0:T(8,128)(2,1)}, bf16[16,24,128]{2,1,0:T(8,128)(2,1)S(1)}, u32[]{:S(2)}, u32[]{:S(2)}) collective-permute-start(bf16[16,24,128]{2,1,0:T(8,128)(2,1)} %copy-done.26), channel_id=1, source_target_pairs={{0,1},{1,0},{2,3},{3,2},{4,5},{5,4},{6,7},{7,6},{8,9},{9,8},{10,11... | collective-permute-start | bytes 294920 | tf_op jit(solution)/shard_map/ppermute | solution.py:19
  72.2 43.7 %collective-permute-start.33 = (bf16[16,24,128]{2,1,0:T(8,128)(2,1)}, bf16[16,24,128]{2,1,0:T(8,128)(2,1)S(1)}, u32[]{:S(2)}, u32[]{:S(2)}) collective-permute-start(bf16[16,24,128]{2,1,0:T(8,128)(2,1)} %copy-done.26), channel_id=1, source_target_pairs={{0,17},{1,16},{2,19},{3,18},{4,21},{5,20},{6,23},{7,22},{8,25},{9,... | collective-permute-start | bytes 294920 | tf_op jit(solution)/shard_map/ppermute | solution.py:19
  74.7 38.7 %collective-permute-start.32 = (bf16[16,24,128]{2,1,0:T(8,128)(2,1)S(1)}, bf16[16,24,128]{2,1,0:T(8,128)(2,1)S(1)}, u32[]{:S(2)}, u32[]{:S(2)}) collective-permute-start(bf16[16,24,128]{2,1,0:T(8,128)(2,1)S(1)} %get-tuple-element.48), channel_id=1, source_target_pairs={{0,16},{1,17},{2,18},{3,19},{4,20},{5,21},{6,22},{7,23},{8,24},{9,... | collective-permute-start | bytes 294920 | tf_op jit(solution)/shard_map/ppermute | solution.py:19
  75.9 18.4 %collective-permute-start.22 = (bf16[24,3584]{1,0:T(8,128)(2,1)}, bf16[24,3584]{1,0:T(8,128)(2,1)S(1)}, u32[]{:S(2)}, u32[]{:S(2)}) collective-permute-start(bf16[24,3584]{1,0:T(8,128)(2,1)} %copy-done.22), channel_id=1, source_target_pairs={{0,4},{1,3},{2,6},{3,1},{4,0},{5,7},{6,2},{7,5},{8,12},{9,11},{10,... | collective-permute-start | bytes 516104 | tf_op jit(solution)/shard_map/ppermute | solution.py:19
  94.3 7.1 %collective-permute-start.26 = (bf16[24,3584]{1,0:T(8,128)(2,1)S(1)}, bf16[24,3584]{1,0:T(8,128)(2,1)S(1)}, u32[]{:S(2)}, u32[]{:S(2)}) collective-permute-start(bf16[24,3584]{1,0:T(8,128)(2,1)S(1)} %copy-done.21), channel_id=1, source_target_pairs={{0,4},{1,3},{2,6},{3,1},{4,0},{5,7},{6,2},{7,5},{8,12},{9,11},{10,... | collective-permute-start | bytes 516104 | tf_op jit(solution)/shard_map/ppermute | solution.py:19
  98.9 7.2 %collective-permute-start.25 = (bf16[24,3584]{1,0:T(8,128)(2,1)S(1)}, bf16[24,3584]{1,0:T(8,128)(2,1)S(1)}, u32[]{:S(2)}, u32[]{:S(2)}) collective-permute-start(bf16[24,3584]{1,0:T(8,128)(2,1)S(1)} %add_convert_fusion.3), channel_id=1, source_target_pairs={{0,2},{1,5},{2,0},{3,7},{4,6},{5,1},{6,4},{7,3},{8,10},{9,13},{10,... | collective-permute-start | bytes 516104 | tf_op jit(solution)/shard_map/ppermute | solution.py:19
  101.4 7.1 %collective-permute-start.30 = (bf16[24,3584]{1,0:T(8,128)(2,1)S(1)}, bf16[24,3584]{1,0:T(8,128)(2,1)S(1)}, u32[]{:S(2)}, u32[]{:S(2)}) collective-permute-start(bf16[24,3584]{1,0:T(8,128)(2,1)S(1)} %copy-done.19), channel_id=1, source_target_pairs={{0,4},{1,3},{2,6},{3,1},{4,0},{5,7},{6,2},{7,5},{8,12},{9,11},{10,... | collective-permute-start | bytes 516104 | tf_op jit(solution)/shard_map/ppermute | solution.py:19
  108.5 10.0 %collective-permute-start.19 = (bf16[24,3584]{1,0:T(8,128)(2,1)S(1)}, bf16[24,3584]{1,0:T(8,128)(2,1)S(1)}, u32[]{:S(2)}, u32[]{:S(2)}) collective-permute-start(bf16[24,3584]{1,0:T(8,128)(2,1)S(1)} %copy-done.17), channel_id=1, source_target_pairs={{0,4},{1,3},{2,6},{3,1},{4,0},{5,7},{6,2},{7,5},{8,12},{9,11},{10,... | collective-permute-start | bytes 516104 | tf_op jit(solution)/shard_map/ppermute | solution.py:19
  111.5 7.0 %collective-permute-start.18 = (bf16[24,3584]{1,0:T(8,128)(2,1)S(1)}, bf16[24,3584]{1,0:T(8,128)(2,1)S(1)}, u32[]{:S(2)}, u32[]{:S(2)}) collective-permute-start(bf16[24,3584]{1,0:T(8,128)(2,1)S(1)} %add_convert_fusion.6), channel_id=1, source_target_pairs={{0,2},{1,5},{2,0},{3,7},{4,6},{5,1},{6,4},{7,3},{8,10},{9,13},{10,... | collective-permute-start | bytes 516104 | tf_op jit(solution)/shard_map/ppermute | solution.py:19
  113.4 7.2 %collective-permute-start.23 = (bf16[24,3584]{1,0:T(8,128)(2,1)S(1)}, bf16[24,3584]{1,0:T(8,128)(2,1)S(1)}, u32[]{:S(2)}, u32[]{:S(2)}) collective-permute-start(bf16[24,3584]{1,0:T(8,128)(2,1)S(1)} %add_convert_fusion.4), channel_id=1, source_target_pairs={{0,8},{1,9},{2,10},{3,11},{4,12},{5,13},{6,14},{7,15},{8,0},{9,1},... | collective-permute-start | bytes 516104 | tf_op jit(solution)/shard_map/ppermute | solution.py:19
  113.4 10.1 %collective-permute-start.27 = (bf16[24,3584]{1,0:T(8,128)(2,1)S(1)}, bf16[24,3584]{1,0:T(8,128)(2,1)S(1)}, u32[]{:S(2)}, u32[]{:S(2)}) collective-permute-start(bf16[24,3584]{1,0:T(8,128)(2,1)S(1)} %add_convert_fusion.2), channel_id=1, source_target_pairs={{0,16},{1,17},{2,18},{3,19},{4,20},{5,21},{6,22},{7,23},{8,24},{9,... | collective-permute-start | bytes 516104 | tf_op jit(solution)/shard_map/ppermute | solution.py:19
  115.9 7.7 %collective-permute-start.31 = (bf16[24,3584]{1,0:T(8,128)(2,1)S(1)}, bf16[24,3584]{1,0:T(8,128)(2,1)S(1)}, u32[]{:S(2)}, u32[]{:S(2)}) collective-permute-start(bf16[24,3584]{1,0:T(8,128)(2,1)S(1)} %add_convert_fusion), channel_id=1, source_target_pairs={{0,24},{1,25},{2,26},{3,27},{4,28},{5,29},{6,30},{7,31},{8,16},{9,... | collective-permute-start | bytes 516104 | tf_op jit(solution)/shard_map/ppermute | solution.py:19
  (39 other events, 262.4 us)

commit v2 on v0

v2 whole, which is shorter than its diff:
```python
import functools

import jax
import jax.numpy as jnp
from jax import lax
from jax.experimental import pallas as pl
from jax.experimental.pallas import tpu as pltpu
from jax.sharding import PartitionSpec as P

SLICES = 8
CORE, FIRST, SECOND = 1, 2, 4
ANY = pl.BlockSpec(memory_space=pl.ANY)
WHOLE = pl.BlockSpec()
SMEM = pl.BlockSpec(memory_space=pltpu.SMEM)
VMEM_LIMIT = 48 * 1024 * 1024


def swap(value, mask_of):
    count = lax.axis_size("ep")
    return lax.ppermute(value, "ep", [(i, i ^ mask_of(i)) for i in range(count)])


def lane(i):
    return FIRST if i & CORE == 0 else SECOND


def cross(i):
    return SECOND if i & CORE == 0 else FIRST


def column_tile(width):
    return next(t for t in (512, 256, 128, width) if width % t == 0)


def route_kernel(experts, capacity, layer_ref, expert_ref, token_ref, gate_ref, tok_ref, *outs):
    bufs, (hi_ref, lo_ref) = outs[:experts], outs[experts : experts + 2]
    pick_ref = outs[experts + 2]
    rows = expert_ref.shape[1]
    tok_count = tok_ref.shape[0]
    places = experts * capacity

    @pl.when(pl.program_id(0) == 0)
    def _():
        relative = expert_ref[...] ^ layer_ref[0]
        ranks = -(-experts // 8) * 8
        hits = (lax.broadcasted_iota(jnp.int32, (ranks, rows), 0) == relative).astype(jnp.float32)
        earlier = lax.broadcasted_iota(jnp.int32, (rows, rows), 0) < lax.broadcasted_iota(
            jnp.int32, (rows, rows), 1
        )
        before = jnp.dot(
            hits.astype(jnp.bfloat16),
            earlier.astype(jnp.float32).astype(jnp.bfloat16),
            preferred_element_type=jnp.float32,
        )
        slot = jnp.sum(hits * before, axis=0, keepdims=True).astype(jnp.int32)
        target = relative * capacity + slot
        place_hot = lax.broadcasted_iota(jnp.int32, (places, rows), 0) == target
        place_hot = place_hot.astype(jnp.float32).astype(jnp.bfloat16)
        token_hot = lax.broadcasted_iota(jnp.int32, (tok_count, rows), 0) == token_ref[...]
        token_hot = token_hot.astype(jnp.float32)
        gate = gate_ref[...]
        gate_hi = gate.astype(jnp.bfloat16).astype(jnp.float32)
        contract = (((1,), (1,)), ((), ()))
        for part, ref in ((gate_hi, hi_ref), (gate - gate_hi, lo_ref)):
            ref[...] = lax.dot_general(
                (token_hot * part).astype(jnp.bfloat16),
                place_hot,
                contract,
                preferred_element_type=jnp.float32,
            ).astype(jnp.bfloat16)
        pick_ref[...] = lax.dot_general(
            place_hot, token_hot.astype(jnp.bfloat16), contract, preferred_element_type=jnp.float32
        ).astype(jnp.bfloat16)

    picked = jnp.dot(pick_ref[...], tok_ref[...], preferred_element_type=jnp.float32)
    for s in range(experts):
        bufs[s][...] = picked[s * capacity : (s + 1) * capacity].astype(jnp.bfloat16)


def expert_kernel(capacity, place_ref, *refs):
    pieces, (win_a, win_b, wout_a, wout_b) = refs[:4], refs[4:8]
    outs, (hid_a, hid_b) = refs[8:12], refs[12:14]
    rows_ref, win_ref, wout_ref, hidden_ref, out_ref, in_sem, weight_sem, out_sem = refs[14:]
    step, width = pieces[0].shape
    units = wout_a.shape[0]
    tile = column_tile(width)
    tiles = width // tile
    loads, later = [], []
    for k in range(tiles):
        cols = pl.ds(k * tile, tile)
        loads.append(
            [
                pltpu.make_async_copy(
                    piece.at[:, cols], rows_ref.at[pl.ds(i * step, step), cols], in_sem.at[k, i]
                )
                for i, piece in enumerate(pieces)
            ]
            + [
                pltpu.make_async_copy(
                    w.at[cols, :], win_ref.at[cols, pl.ds(2 * units * i, 2 * units)], in_sem.at[k, 4 + i]
                )
                for i, w in enumerate((win_a, win_b))
            ]
        )
    for i, w in enumerate((wout_a, wout_b)):
        later.append(
            pltpu.make_async_copy(w, wout_ref.at[pl.ds(units * i, units), :], weight_sem.at[i])
        )
    for copy in sum(loads, []) + later:
        copy.start()
    total = jnp.zeros((4 * step, 4 * units), jnp.float32)
    for k in range(tiles):
        for copy in loads[k]:
            copy.wait()
        cols = pl.ds(k * tile, tile)
        total += jnp.dot(rows_ref[:, cols], win_ref[cols, :], preferred_element_type=jnp.float32)
    for half, hid in ((0, hid_a), (1, hid_b)):
        base = 2 * units * half
        gate, up = total[:, base : base + units], total[:, base + units : base + 2 * units]
        value = gate / (1.0 + jnp.exp(-gate)) * up
        hidden_ref[:, units * half : units * (half + 1)] = value.astype(jnp.bfloat16)
        for i in range(4 * step // capacity):
            hid[place_ref[i]] = value[i * capacity : (i + 1) * capacity].astype(jnp.bfloat16)
    for copy in later:
        copy.wait()
    stores = []
    for k in range(tiles):
        cols = pl.ds(k * tile, tile)
        out = jnp.dot(hidden_ref[...], wout_ref[:, cols], preferred_element_type=jnp.float32)
        out_ref[:, cols] = out.astype(jnp.bfloat16)
        for i in range(4):
            copy = pltpu.make_async_copy(
                out_ref.at[pl.ds(i * step, step), cols], outs[i].at[:, cols], out_sem.at[k, i]
            )
            copy.start()
            stores.append(copy)
    for copy in stores:
        copy.wait()


def mix_kernel(hi_ref, lo_ref, *refs):
    values = [r[...].astype(jnp.float32) for r in refs[:-1]]
    rows = jnp.concatenate(values, axis=0).astype(jnp.bfloat16)
    total = jnp.dot(hi_ref[...], rows, preferred_element_type=jnp.float32)
    total += jnp.dot(lo_ref[...], rows, preferred_element_type=jnp.float32)
    refs[-1][...] = total.astype(jnp.bfloat16)


def run_expert(capacity, places, pieces, weights):
    step, width = pieces[0].shape
    units = weights[2].shape[0]
    rows = 4 * step
    tile = column_tile(width)
    tiles = width // tile
    block = jax.ShapeDtypeStruct((step, width), jnp.bfloat16)
    hid = jax.ShapeDtypeStruct((rows // capacity, capacity, units), jnp.bfloat16)
    return pl.pallas_call(
        functools.partial(expert_kernel, capacity),
        out_shape=[block] * 4 + [hid] * 2,
        in_specs=[SMEM] + [ANY] * 8,
        out_specs=[ANY] * 4 + [WHOLE] * 2,
        scratch_shapes=[
            pltpu.VMEM((rows, width), jnp.bfloat16),
            pltpu.VMEM((width, 4 * units), jnp.bfloat16),
            pltpu.VMEM((2 * units, width), jnp.bfloat16),
            pltpu.VMEM((rows, 2 * units), jnp.bfloat16),
            pltpu.VMEM((rows, width), jnp.bfloat16),
            pltpu.SemaphoreType.DMA((tiles, 6)),
            pltpu.SemaphoreType.DMA((2,)),
            pltpu.SemaphoreType.DMA((tiles, 4)),
        ],
        compiler_params=pltpu.CompilerParams(vmem_limit_bytes=VMEM_LIMIT),
        cost_estimate=pl.CostEstimate(
            flops=12 * rows * width * units, bytes_accessed=12 * 1024 * 1024, transcendentals=0
        ),
    )(places, *pieces, *weights)


def shards(tokens, route_token, route_expert, route_gate, w_in, w_out, swap_pairs):
    devices = lax.axis_size("ep")
    half_axis = devices // 2
    tok_count, width = tokens.shape
    units = w_out.shape[1]
    rows_dev = route_token.shape[0]
    experts = devices // SLICES
    capacity = min(rows_dev, 3 * rows_dev // (2 * experts))
    places = experts * capacity
    me = lax.axis_index("ep")
    layer = me // SLICES
    flag = swap_pairs[me % half_axis]
    params = pltpu.CompilerParams(vmem_limit_bytes=VMEM_LIMIT)
    block = jax.ShapeDtypeStruct((capacity, width), jnp.bfloat16)
    tile = column_tile(width)

    weights = [
        w_in[0],
        swap(w_in[0], lambda i: CORE),
        w_out[0],
        swap(w_out[0], lambda i: CORE),
    ]
    mix_shape = jax.ShapeDtypeStruct((tok_count, places), jnp.bfloat16)
    fixed = lambda shape: pl.BlockSpec(shape, lambda i: (0, 0))
    moving = lambda rows: pl.BlockSpec((rows, tile), lambda i: (0, i))
    *bufs, gate_hi, gate_lo = pl.pallas_call(
        functools.partial(route_kernel, experts, capacity),
        out_shape=[block] * experts + [mix_shape] * 2,
        grid=(width // tile,),
        in_specs=[SMEM] + [fixed((1, rows_dev))] * 3 + [moving(tok_count)],
        out_specs=[moving(capacity)] * experts + [fixed((tok_count, places))] * 2,
        scratch_shapes=[pltpu.VMEM((places, tok_count), jnp.bfloat16)],
        compiler_params=params,
    )(
        layer.reshape(1),
        route_expert.reshape(1, rows_dev),
        route_token.reshape(1, rows_dev),
        route_gate.reshape(1, rows_dev),
        tokens,
    )

    chip = (me % SLICES) // 2
    lane_mask = jnp.where(me % 2 == 0, FIRST, SECOND) // 2
    cross_mask = jnp.where(me % 2 == 0, SECOND, FIRST) // 2
    chips = [chip, chip ^ lane_mask, chip ^ cross_mask, chip ^ lane_mask ^ cross_mask]
    pairs = experts // 2
    sources = [bufs[0]] + [swap(bufs[s], lambda i: SLICES * s) for s in range(1, experts)]
    runs = []
    for pair in range(pairs):
        mine = jnp.concatenate(sources[2 * pair : 2 * pair + 2], axis=0)
        beside = swap(mine, lane)
        across = swap(mine, cross)
        corner = swap(beside, cross)
        spots = [((layer ^ s) % 2) * (SLICES // 2) + c for c in chips for s in (0, 1)]
        runs.append(
            run_expert(
                capacity, jnp.stack(spots).astype(jnp.int32), [mine, beside, across, corner], weights
            )
        )

    finals = [None] * experts
    for pair in reversed(range(pairs)):
        mine, beside, across, corner = runs[pair][:4]
        relay = beside.astype(jnp.float32) + swap(corner, cross).astype(jnp.float32)
        from_lane = swap(relay.astype(jnp.bfloat16), lane)
        from_cross = swap(across, cross)
        for part in (0, 1):
            s = 2 * pair + part
            rows = slice(part * capacity, (part + 1) * capacity)
            total = sum(v[rows].astype(jnp.float32) for v in (mine, from_lane, from_cross))
            total = total.astype(jnp.bfloat16)
            finals[s] = total if s == 0 else swap(total, lambda i: SLICES * s)

    mixed = pl.pallas_call(
        mix_kernel,
        out_shape=jax.ShapeDtypeStruct((tok_count, width), jnp.bfloat16),
        grid=(width // tile,),
        in_specs=[fixed((tok_count, places))] * 2 + [moving(capacity)] * experts,
        out_specs=moving(tok_count),
        compiler_params=params,
    )(gate_hi, gate_lo, *finals)

    by_pair = [[runs[p][4 + half] for p in range(pairs)] for half in (0, 1)]
    high = layer // 2
    ordered = [
        jnp.concatenate(
            [sum(jnp.where(high ^ p == q, part[q], 0) for q in range(pairs)) for p in range(pairs)],
            axis=0,
        )
        for part in by_pair
    ]
    other = swap(ordered[1], lambda i: CORE)
    even = me % 2 == 0
    full = jnp.stack(
        [jnp.where(even, ordered[0], other), jnp.where(even, other, ordered[0])], axis=1
    ).reshape(1, devices * capacity, units)
    far = swap(full, lambda i: half_axis)
    return (mixed, jnp.where(flag == 1, far, full))


def solution(mesh):
    return jax.shard_map(
        shards,
        mesh=mesh,
        in_specs=(
            P(("rep", "ep"), None),
            P(("rep", "ep")),
            P(("rep", "ep"), None),
            P(("rep", "ep")),
            P("ep", None, None),
            P("ep", None, None),
            P(),
        ),
        out_specs=(P(("rep", "ep"), None), P(("rep", "ep"), None, None)),
        check_vma=False,
    )
```

time: 295 us -> 94.1 us (0.32)
  blocking collectives: 130 us -> 0 us
  waiting for transfers between devices: 127 us -> 31.1 us
  starting transfers between devices: 6.37 us -> 37.9 us
  Pallas kernels: 0 us -> 16.3 us
  matrix products: 15.3 us -> 0 us
  other arithmetic: 7.77 us -> 1.21 us
    all_to_all x1 -> x0, blocking collectives: 130 us -> none  [shards(): lax.all_to_all(outgoing, 'ep', split_axis=0, concat_axis=0, tiled=True)]
    ppermute x1 -> x22, waiting for transfers between devices: 127 us -> 31.1 us  [swap(): lax.ppermute(value, 'ep', [(i, i ^ mask_of(i)) for i in range(count)])]
    ppermute x1 -> x22, starting transfers between devices: 2.65 us -> 37.9 us  [swap(): lax.ppermute(value, 'ep', [(i, i ^ mask_of(i)) for i in range(count)])]
    pallas_call x0 -> x4, Pallas kernels: none -> 16.3 us  [the longest x2 11 us: run_expert(): pl.pallas_call(functools.partial(expert_kernel, capacity), out_shape=[blo...]
    dot_general x6 -> x0, matrix products: 15.3 us -> none  [the longest x1 5.75 us: shards(): jnp.einsum('je,jcd->ecd', owner_table, returned, preferred_element_type=j...]
    gather x2 -> x0, local copies, waits for them, and re-layouts: 5.87 us -> none  [the longest x1 3.29 us: shards(): outgoing = jnp.take(expert_buf, served_expert, axis=0)]
    unnamed x10 -> x22, local copies, waits for them, and re-layouts: 0.03 us -> 3.91 us
    select_n x5 -> x1, other arithmetic: 4.52 us -> 0.7 us  [shards(): return (mixed, jnp.where(flag == 1, far, full))]
  transfers between devices with their start and end apart: 2 -> 22, of which waited for: 1 -> 8; matrix products, arithmetic and copies ran while one was open for 0% -> 3% of each run, Pallas kernels for 0% -> 12%
where the time goes in v2:
time: 94.1 us; the launch traced here: 93.8 us
  starting transfers between devices  37.9 us (40%)
  waiting for transfers between devices  31.1 us (33%)
  Pallas kernels  16.3 us (17%)
  local copies, waits for them, and re-layouts  5.81 us (6%)
  between operations  1.51 us (2%)
  other arithmetic  1.21 us (1%)
    ppermute x22, starting transfers between devices, swap(): lax.ppermute(value, 'ep', [(i, i ^ mask_of(i)) for i in range(count)])  37.9 us
    ppermute x22, waiting for transfers between devices, swap(): lax.ppermute(value, 'ep', [(i, i ^ mask_of(i)) for i in range(count)])  31.1 us
    pallas_call x2, Pallas kernels, run_expert(): pl.pallas_call(functools.partial(expert_kernel, capacity), out_shape=[blo...  11 us
    unnamed x22, local copies, waits for them, and re-layouts  3.91 us
    pallas_call x1, Pallas kernels, shards(): pl.pallas_call(mix_kernel, out_shape=jax.ShapeDtypeStruct((tok_count, wid...  3.56 us
  transfers between devices with their start and end apart: 22, of which 8 were waited for; matrix products, arithmetic and copies ran while one was open for 3% of the time, Pallas kernels for 12%

profile of v2, /device:TPU:0, one launch (start us, length us, event | category | flops | bytes accessed | tf_op | source)
XLA Modules:
  0.0 93.8 jit_solution(13523925341876380945)
XLA Ops:
  3.9 1.7 %shard_map.86 = (bf16[24,3584]{1,0:T(8,128)(2,1)S(1)}, bf16[24,3584]{1,0:T(8,128)(2,1)S(1)}, bf16[24,3584]{1,0:T(8,128)(2,1)S(1)}, bf16[24,3584]{1,0:T(8,128)(2,...) custom-call(s32[1]{0:T(128)} %bitcast.layer_ref, s32[1,64]{1,0:T(1,128)S(1)} %bitcast.23, ...), custom_call_target="tpu_custom_call" | custom-call | tf_op jit(solution)/shard_map/pallas_call | solution.py:204
  5.7 3.1 %collective-permute-start = (bf16[24,3584]{1,0:T(8,128)(2,1)S(1)}, bf16[24,3584]{1,0:T(8,128)(2,1)S(1)}, u32[]{:S(2)}, u32[]{:S(2)}) collective-permute-start(bf16[24,3584]{1,0:T(8,128)(2,1)S(1)} %get-tuple-element.23), channel_id=1, source_target_pairs={{0,8},{1,9},{2,10},{3,11},{4,12},{5,13},{6,14},{7,15},{8,0},{9,1},... | collective-permute-start | bytes 516104 | tf_op jit(solution)/shard_map/ppermute | solution.py:20
  9.3 2.6 %collective-permute-start.10 = (bf16[24,3584]{1,0:T(8,128)(2,1)S(1)}, bf16[24,3584]{1,0:T(8,128)(2,1)S(1)}, u32[]{:S(2)}, u32[]{:S(2)}) collective-permute-start(bf16[24,3584]{1,0:T(8,128)(2,1)S(1)} %get-tuple-element.28), channel_id=1, source_target_pairs={{0,16},{1,17},{2,18},{3,19},{4,20},{5,21},{6,22},{7,23},{8,24},{9,... | collective-permute-start | bytes 516104 | tf_op jit(solution)/shard_map/ppermute | solution.py:20
  11.9 2.9 %collective-permute-done = bf16[24,3584]{1,0:T(8,128)(2,1)S(1)} collective-permute-done((bf16[24,3584]{1,0:T(8,128)(2,1)S(1)}, bf16[24,3584]{1,0:T(8,128)(2,1)S(1)}, u32[]{:S(2)}, u32[]{:S(2)}) %collective-permute-start) | collective-permute-done | bytes 172064 | tf_op jit(solution)/shard_map/ppermute | solution.py:20
  14.8 1.9 %collective-permute-start.1 = (bf16[48,3584]{1,0:T(8,128)(2,1)S(1)}, bf16[48,3584]{1,0:T(8,128)(2,1)S(1)}, u32[]{:S(2)}, u32[]{:S(2)}) collective-permute-start(bf16[48,3584]{1,0:T(8,128)(2,1)S(1)} %constant_dynamic-update-slice_fusion.refs_0_), channel_id=1, source_target_pairs={{0,2},{1,5},{2,0},{3,7},{4,6},{5,1},{6,4},{7,3},{8,10},{9,13},{10,... | collective-permute-start | bytes 1032200 | tf_op jit(solution)/shard_map/ppermute | solution.py:20
  16.7 8.1 %collective-permute-done.10 = bf16[24,3584]{1,0:T(8,128)(2,1)S(1)} collective-permute-done((bf16[24,3584]{1,0:T(8,128)(2,1)S(1)}, bf16[24,3584]{1,0:T(8,128)(2,1)S(1)}, u32[]{:S(2)}, u32[]{:S(2)}) %collective-permute-start.10) | collective-permute-done | bytes 172064 | tf_op jit(solution)/shard_map/ppermute | solution.py:20
  24.8 1.5 %collective-permute-start.2 = (bf16[48,3584]{1,0:T(8,128)(2,1)S(1)}, bf16[48,3584]{1,0:T(8,128)(2,1)S(1)}, u32[]{:S(2)}, u32[]{:S(2)}) collective-permute-start(bf16[48,3584]{1,0:T(8,128)(2,1)S(1)} %constant_dynamic-update-slice_fusion.refs_0_), channel_id=1, source_target_pairs={{0,4},{1,3},{2,6},{3,1},{4,0},{5,7},{6,2},{7,5},{8,12},{9,11},{10,... | collective-permute-start | bytes 1032200 | tf_op jit(solution)/shard_map/ppermute | solution.py:20
  26.4 1.6 %collective-permute-start.12 = (bf16[48,3584]{1,0:T(8,128)(2,1)S(1)}, bf16[48,3584]{1,0:T(8,128)(2,1)S(1)}, u32[]{:S(2)}, u32[]{:S(2)}) collective-permute-start(bf16[48,3584]{1,0:T(8,128)(2,1)S(1)} %constant_dynamic-update-slice_fusion.2.refs_0_), channel_id=1, source_target_pairs={{0,2},{1,5},{2,0},{3,7},{4,6},{5,1},{6,4},{7,3},{8,10},{9,13},{10,... | collective-permute-start | bytes 1032200 | tf_op jit(solution)/shard_map/ppermute | solution.py:20
  28.4 5.9 %collective-permute-done.2.refs_2_ = bf16[48,3584]{1,0:T(8,128)(2,1)S(1)} collective-permute-done((bf16[48,3584]{1,0:T(8,128)(2,1)S(1)}, bf16[48,3584]{1,0:T(8,128)(2,1)S(1)}, u32[]{:S(2)}, u32[]{:S(2)}) %collective-permute-start.2) | collective-permute-done | bytes 344096 | tf_op jit(solution)/shard_map/ppermute | solution.py:20
  34.3 1.5 %collective-permute-start.13 = (bf16[48,3584]{1,0:T(8,128)(2,1)S(1)}, bf16[48,3584]{1,0:T(8,128)(2,1)}, u32[]{:S(2)}, u32[]{:S(2)}) collective-permute-start(bf16[48,3584]{1,0:T(8,128)(2,1)S(1)} %constant_dynamic-update-slice_fusion.2.refs_0_), channel_id=1, source_target_pairs={{0,4},{1,3},{2,6},{3,1},{4,0},{5,7},{6,2},{7,5},{8,12},{9,11},{10,... | collective-permute-start | bytes 1032200 | tf_op jit(solution)/shard_map/ppermute | solution.py:20
  35.8 1.6 %collective-permute-done.12.refs_1_ = bf16[48,3584]{1,0:T(8,128)(2,1)S(1)} collective-permute-done((bf16[48,3584]{1,0:T(8,128)(2,1)S(1)}, bf16[48,3584]{1,0:T(8,128)(2,1)S(1)}, u32[]{:S(2)}, u32[]{:S(2)}) %collective-permute-start.12) | collective-permute-done | bytes 344096 | tf_op jit(solution)/shard_map/ppermute | solution.py:20
  41.1 5.5 %shard_map.87 = (bf16[48,3584]{1,0:T(8,128)(2,1)S(1)}, bf16[48,3584]{1,0:T(8,128)(2,1)S(1)}, bf16[48,3584]{1,0:T(8,128)(2,1)S(1)}, bf16[48,3584]{1,0:T(8,128)(2,...) custom-call(s32[8]{0:T(128)S(1)} %copy-done.6, ...), custom_call_target="tpu_custom_call" | custom-call | flops 1056964608 | bytes 12582912 | tf_op jit(solution)/shard_map/pallas_call | solution.py:157
  46.6 1.6 %collective-permute-start.8 = (bf16[48,3584]{1,0:T(8,128)(2,1)S(1)}, bf16[48,3584]{1,0:T(8,128)(2,1)S(1)}, u32[]{:S(2)}, u32[]{:S(2)}) collective-permute-start(bf16[48,3584]{1,0:T(8,128)(2,1)S(1)} %get-tuple-element.27), channel_id=1, source_target_pairs={{0,4},{1,3},{2,6},{3,1},{4,0},{5,7},{6,2},{7,5},{8,12},{9,11},{10,... | collective-permute-start | bytes 1032200 | tf_op jit(solution)/shard_map/ppermute | solution.py:20
  48.7 5.6 %shard_map.88 = (bf16[48,3584]{1,0:T(8,128)(2,1)S(1)}, bf16[48,3584]{1,0:T(8,128)(2,1)S(1)}, bf16[48,3584]{1,0:T(8,128)(2,1)S(1)}, bf16[48,3584]{1,0:T(8,128)(2,...) custom-call(s32[8]{0:T(128)S(1)} %copy-done.6, ...), custom_call_target="tpu_custom_call" | custom-call | flops 1056964608 | bytes 12582912 | tf_op jit(solution)/shard_map/pallas_call | solution.py:157
  54.3 1.6 %collective-permute-start.17 = (bf16[48,3584]{1,0:T(8,128)(2,1)S(1)}, bf16[48,3584]{1,0:T(8,128)(2,1)S(1)}, u32[]{:S(2)}, u32[]{:S(2)}) collective-permute-start(bf16[48,3584]{1,0:T(8,128)(2,1)S(1)} %get-tuple-element.33), channel_id=1, source_target_pairs={{0,4},{1,3},{2,6},{3,1},{4,0},{5,7},{6,2},{7,5},{8,12},{9,11},{10,... | collective-permute-start | bytes 1032200 | tf_op jit(solution)/shard_map/ppermute | solution.py:20
  57.8 3.8 %collective-permute-start.21 = (bf16[1,768,128]{2,1,0:T(8,128)(2,1)S(1)}, bf16[1,768,128]{2,1,0:T(8,128)(2,1)S(1)}, u32[]{:S(2)}, u32[]{:S(2)}) collective-permute-start(bf16[1,768,128]{2,1,0:T(8,128)(2,1)S(1)} %bitcast.29), channel_id=1, source_target_pairs={{0,16},{1,17},{2,18},{3,19},{4,20},{5,21},{6,22},{7,23},{8,24},{9,... | collective-permute-start | bytes 589832 | tf_op jit(solution)/shard_map/ppermute | solution.py:20
  61.8 1.6 %collective-permute-start.7 = (bf16[48,3584]{1,0:T(8,128)(2,1)S(1)}, bf16[48,3584]{1,0:T(8,128)(2,1)S(1)}, u32[]{:S(2)}, u32[]{:S(2)}) collective-permute-start(bf16[48,3584]{1,0:T(8,128)(2,1)S(1)} %add_convert_fusion.1), channel_id=1, source_target_pairs={{0,2},{1,5},{2,0},{3,7},{4,6},{5,1},{6,4},{7,3},{8,10},{9,13},{10,... | collective-permute-start | bytes 1032200 | tf_op jit(solution)/shard_map/ppermute | solution.py:20
  63.3 3.0 %collective-permute-done.15 = bf16[48,3584]{1,0:T(8,128)(2,1)S(1)} collective-permute-done((bf16[48,3584]{1,0:T(8,128)(2,1)S(1)}, bf16[48,3584]{1,0:T(8,128)(2,1)S(1)}, u32[]{:S(2)}, u32[]{:S(2)}) %collective-permute-start.15) | collective-permute-done | bytes 344096 | tf_op jit(solution)/shard_map/ppermute | solution.py:20
  66.5 1.5 %collective-permute-start.16 = (bf16[48,3584]{1,0:T(8,128)(2,1)S(1)}, bf16[48,3584]{1,0:T(8,128)(2,1)S(1)}, u32[]{:S(2)}, u32[]{:S(2)}) collective-permute-start(bf16[48,3584]{1,0:T(8,128)(2,1)S(1)} %add_convert_fusion), channel_id=1, source_target_pairs={{0,2},{1,5},{2,0},{3,7},{4,6},{5,1},{6,4},{7,3},{8,10},{9,13},{10,... | collective-permute-start | bytes 1032200 | tf_op jit(solution)/shard_map/ppermute | solution.py:20
  69.2 5.0 %collective-permute-start.9 = (bf16[24,3584]{1,0:T(8,128)(2,1)S(1)}, bf16[24,3584]{1,0:T(8,128)(2,1)S(1)}, u32[]{:S(2)}, u32[]{:S(2)}) collective-permute-start(bf16[24,3584]{1,0:T(8,128)(2,1)S(1)} %get-tuple-element.40), channel_id=1, source_target_pairs={{0,8},{1,9},{2,10},{3,11},{4,12},{5,13},{6,14},{7,15},{8,0},{9,1},... | collective-permute-start | bytes 516104 | tf_op jit(solution)/shard_map/ppermute | solution.py:20
  74.4 6.6 %collective-permute-start.18 = (bf16[24,3584]{1,0:T(8,128)(2,1)S(1)}, bf16[24,3584]{1,0:T(8,128)(2,1)S(1)}, u32[]{:S(2)}, u32[]{:S(2)}) collective-permute-start(bf16[24,3584]{1,0:T(8,128)(2,1)S(1)} %get-tuple-element.39), channel_id=1, source_target_pairs={{0,16},{1,17},{2,18},{3,19},{4,20},{5,21},{6,22},{7,23},{8,24},{9,... | collective-permute-start | bytes 516104 | tf_op jit(solution)/shard_map/ppermute | solution.py:20
  81.0 1.4 %collective-permute-start.19 = (bf16[24,3584]{1,0:T(8,128)(2,1)S(1)}, bf16[24,3584]{1,0:T(8,128)(2,1)S(1)}, u32[]{:S(2)}, u32[]{:S(2)}) collective-permute-start(bf16[24,3584]{1,0:T(8,128)(2,1)S(1)} %get-tuple-element.38), channel_id=1, source_target_pairs={{0,24},{1,25},{2,26},{3,27},{4,28},{5,29},{6,30},{7,31},{8,16},{9,... | collective-permute-start | bytes 516104 | tf_op jit(solution)/shard_map/ppermute | solution.py:20
  83.1 7.1 %collective-permute-done.18.refs_2_ = bf16[24,3584]{1,0:T(8,128)(2,1)S(1)} collective-permute-done((bf16[24,3584]{1,0:T(8,128)(2,1)S(1)}, bf16[24,3584]{1,0:T(8,128)(2,1)S(1)}, u32[]{:S(2)}, u32[]{:S(2)}) %collective-permute-start.18) | collective-permute-done | bytes 172064 | tf_op jit(solution)/shard_map/ppermute | solution.py:20
  90.3 3.6 %shard_map.89 = bf16[128,3584]{1,0:T(8,128)(2,1)} custom-call(bf16[128,96]{1,0:T(8,128)(2,1)S(1)} %copy-done.3, bf16[128,96]{1,0:T(8,128)(2,1)S(1)} %copy-done.5, bf16[24,3584]{1,0:T(8,128)(2,1)S(1)} %get-tuple-element.41.refs_0_, bf16[24,3584]{1,0:T(8,128)(2,1)S(1)} %collective-permute-done.9.refs_1_, bf16[24,3584]{1,0:T(8,128)(2,1)S(1)} %collective-permute-done.18.refs_2_, ...), custom_call_target="tpu_custom_call" | custom-call | tf_op jit(solution)/shard_map/pallas_call | solution.py:252
  (61 shorter events, 12.0 us)
Async XLA Ops:
  0.6 39.8 %copy-start = (bf16[1,128,3584]{2,1,0:T(8,128)(2,1)S(1)}, bf16[1,128,3584]{2,1,0:T(8,128)(2,1)}, u32[]{:S(2)}) copy-start(bf16[1,128,3584]{2,1,0:T(8,128)(2,1)} %param.12) | copy-start | bytes 2752516
  5.6 31.8 %copy-start.2 = (bf16[128,96]{1,0:T(8,128)(2,1)}, bf16[128,96]{1,0:T(8,128)(2,1)S(1)}, u32[]{:S(2)}) copy-start(bf16[128,96]{1,0:T(8,128)(2,1)S(1)} %get-tuple-element.20.hi_ref) | copy-start | bytes 73732
  5.7 9.1 %collective-permute-start = (bf16[24,3584]{1,0:T(8,128)(2,1)S(1)}, bf16[24,3584]{1,0:T(8,128)(2,1)S(1)}, u32[]{:S(2)}, u32[]{:S(2)}) collective-permute-start(bf16[24,3584]{1,0:T(8,128)(2,1)S(1)} %get-tuple-element.23), channel_id=1, source_target_pairs={{0,8},{1,9},{2,10},{3,11},{4,12},{5,13},{6,14},{7,15},{8,0},{9,1},... | collective-permute-start | bytes 516104 | tf_op jit(solution)/shard_map/ppermute | solution.py:20
  8.7 31.7 %collective-permute-start.4 = (bf16[3584,256]{1,0:T(8,128)(2,1)}, bf16[3584,256]{1,0:T(8,128)(2,1)}, u32[]{:S(2)}, u32[]{:S(2)}) collective-permute-start(bf16[3584,256]{1,0:T(8,128)(2,1)} %bitcast.26), channel_id=1, source_target_pairs={{0,1},{1,0},{2,3},{3,2},{4,5},{5,4},{6,7},{7,6},{8,9},{9,8},{10,11... | collective-permute-start | bytes 5505032 | tf_op jit(solution)/shard_map/ppermute | solution.py:20
  8.7 31.7 %collective-permute-start.5 = (bf16[128,3584]{1,0:T(8,128)(2,1)}, bf16[128,3584]{1,0:T(8,128)(2,1)S(1)}, u32[]{:S(2)}, u32[]{:S(2)}) collective-permute-start(bf16[128,3584]{1,0:T(8,128)(2,1)} %bitcast.20), channel_id=1, source_target_pairs={{0,1},{1,0},{2,3},{3,2},{4,5},{5,4},{6,7},{7,6},{8,9},{9,8},{10,11... | collective-permute-start | bytes 2752520 | tf_op jit(solution)/shard_map/ppermute | solution.py:20
  9.3 15.6 %collective-permute-start.10 = (bf16[24,3584]{1,0:T(8,128)(2,1)S(1)}, bf16[24,3584]{1,0:T(8,128)(2,1)S(1)}, u32[]{:S(2)}, u32[]{:S(2)}) collective-permute-start(bf16[24,3584]{1,0:T(8,128)(2,1)S(1)} %get-tuple-element.28), channel_id=1, source_target_pairs={{0,16},{1,17},{2,18},{3,19},{4,20},{5,21},{6,22},{7,23},{8,24},{9,... | collective-permute-start | bytes 516104 | tf_op jit(solution)/shard_map/ppermute | solution.py:20
  11.8 14.5 %collective-permute-start.11 = (bf16[24,3584]{1,0:T(8,128)(2,1)S(1)}, bf16[24,3584]{1,0:T(8,128)(2,1)S(1)}, u32[]{:S(2)}, u32[]{:S(2)}) collective-permute-start(bf16[24,3584]{1,0:T(8,128)(2,1)S(1)} %get-tuple-element.29), channel_id=1, source_target_pairs={{0,24},{1,25},{2,26},{3,27},{4,28},{5,29},{6,30},{7,31},{8,16},{9,... | collective-permute-start | bytes 516104 | tf_op jit(solution)/shard_map/ppermute | solution.py:20
  14.8 13.1 %collective-permute-start.1 = (bf16[48,3584]{1,0:T(8,128)(2,1)S(1)}, bf16[48,3584]{1,0:T(8,128)(2,1)S(1)}, u32[]{:S(2)}, u32[]{:S(2)}) collective-permute-start(bf16[48,3584]{1,0:T(8,128)(2,1)S(1)} %constant_dynamic-update-slice_fusion.refs_0_), channel_id=1, source_target_pairs={{0,2},{1,5},{2,0},{3,7},{4,6},{5,1},{6,4},{7,3},{8,10},{9,13},{10,... | collective-permute-start | bytes 1032200 | tf_op jit(solution)/shard_map/ppermute | solution.py:20
  24.8 9.5 %collective-permute-start.2 = (bf16[48,3584]{1,0:T(8,128)(2,1)S(1)}, bf16[48,3584]{1,0:T(8,128)(2,1)S(1)}, u32[]{:S(2)}, u32[]{:S(2)}) collective-permute-start(bf16[48,3584]{1,0:T(8,128)(2,1)S(1)} %constant_dynamic-update-slice_fusion.refs_0_), channel_id=1, source_target_pairs={{0,4},{1,3},{2,6},{3,1},{4,0},{5,7},{6,2},{7,5},{8,12},{9,11},{10,... | collective-permute-start | bytes 1032200 | tf_op jit(solution)/shard_map/ppermute | solution.py:20
  26.4 11.1 %collective-permute-start.12 = (bf16[48,3584]{1,0:T(8,128)(2,1)S(1)}, bf16[48,3584]{1,0:T(8,128)(2,1)S(1)}, u32[]{:S(2)}, u32[]{:S(2)}) collective-permute-start(bf16[48,3584]{1,0:T(8,128)(2,1)S(1)} %constant_dynamic-update-slice_fusion.2.refs_0_), channel_id=1, source_target_pairs={{0,2},{1,5},{2,0},{3,7},{4,6},{5,1},{6,4},{7,3},{8,10},{9,13},{10,... | collective-permute-start | bytes 1032200 | tf_op jit(solution)/shard_map/ppermute | solution.py:20
  27.9 12.5 %collective-permute-start.3 = (bf16[48,3584]{1,0:T(8,128)(2,1)S(1)}, bf16[48,3584]{1,0:T(8,128)(2,1)}, u32[]{:S(2)}, u32[]{:S(2)}) collective-permute-start(bf16[48,3584]{1,0:T(8,128)(2,1)S(1)} %collective-permute-done.1.refs_1_), channel_id=1, source_target_pairs={{0,4},{1,3},{2,6},{3,1},{4,0},{5,7},{6,2},{7,5},{8,12},{9,11},{10,... | collective-permute-start | bytes 1032200 | tf_op jit(solution)/shard_map/ppermute | solution.py:20
  34.3 14.4 %collective-permute-start.13 = (bf16[48,3584]{1,0:T(8,128)(2,1)S(1)}, bf16[48,3584]{1,0:T(8,128)(2,1)}, u32[]{:S(2)}, u32[]{:S(2)}) collective-permute-start(bf16[48,3584]{1,0:T(8,128)(2,1)S(1)} %constant_dynamic-update-slice_fusion.2.refs_0_), channel_id=1, source_target_pairs={{0,4},{1,3},{2,6},{3,1},{4,0},{5,7},{6,2},{7,5},{8,12},{9,11},{10,... | collective-permute-start | bytes 1032200 | tf_op jit(solution)/shard_map/ppermute | solution.py:20
  37.5 11.3 %collective-permute-start.14 = (bf16[48,3584]{1,0:T(8,128)(2,1)S(1)}, bf16[48,3584]{1,0:T(8,128)(2,1)}, u32[]{:S(2)}, u32[]{:S(2)}) collective-permute-start(bf16[48,3584]{1,0:T(8,128)(2,1)S(1)} %collective-permute-done.12.refs_1_), channel_id=1, source_target_pairs={{0,4},{1,3},{2,6},{3,1},{4,0},{5,7},{6,2},{7,5},{8,12},{9,11},{10,... | collective-permute-start | bytes 1032200 | tf_op jit(solution)/shard_map/ppermute | solution.py:20
  46.6 21.4 %collective-permute-start.8 = (bf16[48,3584]{1,0:T(8,128)(2,1)S(1)}, bf16[48,3584]{1,0:T(8,128)(2,1)S(1)}, u32[]{:S(2)}, u32[]{:S(2)}) collective-permute-start(bf16[48,3584]{1,0:T(8,128)(2,1)S(1)} %get-tuple-element.27), channel_id=1, source_target_pairs={{0,4},{1,3},{2,6},{3,1},{4,0},{5,7},{6,2},{7,5},{8,12},{9,11},{10,... | collective-permute-start | bytes 1032200 | tf_op jit(solution)/shard_map/ppermute | solution.py:20
  48.2 13.5 %collective-permute-start.6 = (bf16[48,3584]{1,0:T(8,128)(2,1)S(1)}, bf16[48,3584]{1,0:T(8,128)(2,1)S(1)}, u32[]{:S(2)}, u32[]{:S(2)}) collective-permute-start(bf16[48,3584]{1,0:T(8,128)(2,1)S(1)} %get-tuple-element.26), channel_id=1, source_target_pairs={{0,4},{1,3},{2,6},{3,1},{4,0},{5,7},{6,2},{7,5},{8,12},{9,11},{10,... | collective-permute-start | bytes 1032200 | tf_op jit(solution)/shard_map/ppermute | solution.py:20
  54.3 20.0 %collective-permute-start.17 = (bf16[48,3584]{1,0:T(8,128)(2,1)S(1)}, bf16[48,3584]{1,0:T(8,128)(2,1)S(1)}, u32[]{:S(2)}, u32[]{:S(2)}) collective-permute-start(bf16[48,3584]{1,0:T(8,128)(2,1)S(1)} %get-tuple-element.33), channel_id=1, source_target_pairs={{0,4},{1,3},{2,6},{3,1},{4,0},{5,7},{6,2},{7,5},{8,12},{9,11},{10,... | collective-permute-start | bytes 1032200 | tf_op jit(solution)/shard_map/ppermute | solution.py:20
  55.9 10.5 %collective-permute-start.15 = (bf16[48,3584]{1,0:T(8,128)(2,1)S(1)}, bf16[48,3584]{1,0:T(8,128)(2,1)S(1)}, u32[]{:S(2)}, u32[]{:S(2)}) collective-permute-start(bf16[48,3584]{1,0:T(8,128)(2,1)S(1)} %get-tuple-element.32), channel_id=1, source_target_pairs={{0,4},{1,3},{2,6},{3,1},{4,0},{5,7},{6,2},{7,5},{8,12},{9,11},{10,... | collective-permute-start | bytes 1032200 | tf_op jit(solution)/shard_map/ppermute | solution.py:20
  56.4 1.4 %collective-permute-start.20 = (bf16[16,24,128]{2,1,0:T(8,128)(2,1)S(1)}, bf16[16,24,128]{2,1,0:T(8,128)(2,1)S(1)}, u32[]{:S(2)}, u32[]{:S(2)}) collective-permute-start(bf16[16,24,128]{2,1,0:T(8,128)(2,1)S(1)} %pad_maximum_fusion.2), channel_id=1, source_target_pairs={{0,1},{1,0},{2,3},{3,2},{4,5},{5,4},{6,7},{7,6},{8,9},{9,8},{10,11... | collective-permute-start | bytes 294920 | tf_op jit(solution)/shard_map/ppermute | solution.py:20
  57.8 24.5 %collective-permute-start.21 = (bf16[1,768,128]{2,1,0:T(8,128)(2,1)S(1)}, bf16[1,768,128]{2,1,0:T(8,128)(2,1)S(1)}, u32[]{:S(2)}, u32[]{:S(2)}) collective-permute-start(bf16[1,768,128]{2,1,0:T(8,128)(2,1)S(1)} %bitcast.29), channel_id=1, source_target_pairs={{0,16},{1,17},{2,18},{3,19},{4,20},{5,21},{6,22},{7,23},{8,24},{9,... | collective-permute-start | bytes 589832 | tf_op jit(solution)/shard_map/ppermute | solution.py:20
  61.8 7.3 %collective-permute-start.7 = (bf16[48,3584]{1,0:T(8,128)(2,1)S(1)}, bf16[48,3584]{1,0:T(8,128)(2,1)S(1)}, u32[]{:S(2)}, u32[]{:S(2)}) collective-permute-start(bf16[48,3584]{1,0:T(8,128)(2,1)S(1)} %add_convert_fusion.1), channel_id=1, source_target_pairs={{0,2},{1,5},{2,0},{3,7},{4,6},{5,1},{6,4},{7,3},{8,10},{9,13},{10,... | collective-permute-start | bytes 1032200 | tf_op jit(solution)/shard_map/ppermute | solution.py:20
  66.5 7.8 %collective-permute-start.16 = (bf16[48,3584]{1,0:T(8,128)(2,1)S(1)}, bf16[48,3584]{1,0:T(8,128)(2,1)S(1)}, u32[]{:S(2)}, u32[]{:S(2)}) collective-permute-start(bf16[48,3584]{1,0:T(8,128)(2,1)S(1)} %add_convert_fusion), channel_id=1, source_target_pairs={{0,2},{1,5},{2,0},{3,7},{4,6},{5,1},{6,4},{7,3},{8,10},{9,13},{10,... | collective-permute-start | bytes 1032200 | tf_op jit(solution)/shard_map/ppermute | solution.py:20
  69.2 13.9 %collective-permute-start.9 = (bf16[24,3584]{1,0:T(8,128)(2,1)S(1)}, bf16[24,3584]{1,0:T(8,128)(2,1)S(1)}, u32[]{:S(2)}, u32[]{:S(2)}) collective-permute-start(bf16[24,3584]{1,0:T(8,128)(2,1)S(1)} %get-tuple-element.40), channel_id=1, source_target_pairs={{0,8},{1,9},{2,10},{3,11},{4,12},{5,13},{6,14},{7,15},{8,0},{9,1},... | collective-permute-start | bytes 516104 | tf_op jit(solution)/shard_map/ppermute | solution.py:20
  74.4 15.8 %collective-permute-start.18 = (bf16[24,3584]{1,0:T(8,128)(2,1)S(1)}, bf16[24,3584]{1,0:T(8,128)(2,1)S(1)}, u32[]{:S(2)}, u32[]{:S(2)}) collective-permute-start(bf16[24,3584]{1,0:T(8,128)(2,1)S(1)} %get-tuple-element.39), channel_id=1, source_target_pairs={{0,16},{1,17},{2,18},{3,19},{4,20},{5,21},{6,22},{7,23},{8,24},{9,... | collective-permute-start | bytes 516104 | tf_op jit(solution)/shard_map/ppermute | solution.py:20
  81.0 9.2 %collective-permute-start.19 = (bf16[24,3584]{1,0:T(8,128)(2,1)S(1)}, bf16[24,3584]{1,0:T(8,128)(2,1)S(1)}, u32[]{:S(2)}, u32[]{:S(2)}) collective-permute-start(bf16[24,3584]{1,0:T(8,128)(2,1)S(1)} %get-tuple-element.38), channel_id=1, source_target_pairs={{0,24},{1,25},{2,26},{3,27},{4,28},{5,29},{6,30},{7,31},{8,16},{9,... | collective-permute-start | bytes 516104 | tf_op jit(solution)/shard_map/ppermute | solution.py:20
  (8 other events, 83.3 us)

commit v3 on v0

v3 whole, which is shorter than its diff:
```python
import functools

import jax
import jax.numpy as jnp
from jax import lax
from jax.experimental import pallas as pl
from jax.experimental.pallas import tpu as pltpu
from jax.sharding import PartitionSpec as P

SLICES = 8
CORE, FIRST, SECOND = 1, 2, 4
CHIPS = SLICES // 2
VMEM = pl.BlockSpec(memory_space=pltpu.VMEM)
SMEM = pl.BlockSpec(memory_space=pltpu.SMEM)
ANY = pl.BlockSpec(memory_space=pl.ANY)
MIB = 1024 * 1024


def swap(value, mask_of):
    count = lax.axis_size("ep")
    return lax.ppermute(value, "ep", [(i, i ^ mask_of(i)) for i in range(count)])


def after(value, others):
    return lax.optimization_barrier((value, others))[0]


def lane(i):
    return FIRST if i & CORE == 0 else SECOND


def cross(i):
    return SECOND if i & CORE == 0 else FIRST


def column_tile(width):
    return next(t for t in (1792, 512, 256, 128, width) if width % t == 0)


def route_kernel(experts, capacity, me_ref, expert_hbm, token_hbm, gate_hbm, tok_hbm, *refs):
    bufs, (hi_ref, lo_ref) = refs[:experts], refs[experts : experts + 2]
    expert_ref, token_ref, gate_ref, tok_ref, out_ref, sems, out_sems = refs[experts + 2 :]
    rows = expert_ref.shape[1]
    tok_count, width = tok_ref.shape
    places = experts * capacity
    tile = column_tile(width)
    tiles = width // tile
    small = [
        pltpu.make_async_copy(source, target, sems.at[i])
        for i, (source, target) in enumerate(
            ((expert_hbm, expert_ref), (token_hbm, token_ref), (gate_hbm, gate_ref))
        )
    ]
    large = [
        pltpu.make_async_copy(
            tok_hbm.at[:, pl.ds(k * tile, tile)], tok_ref.at[:, pl.ds(k * tile, tile)], sems.at[3 + k]
        )
        for k in range(tiles)
    ]
    for copy in small + large:
        copy.start()
    for copy in small:
        copy.wait()
    relative = expert_ref[...] ^ (me_ref[0] // SLICES)
    ranks = -(-experts // 8) * 8
    hits = (lax.broadcasted_iota(jnp.int32, (ranks, rows), 0) == relative).astype(jnp.float32)
    earlier = lax.broadcasted_iota(jnp.int32, (rows, rows), 0) < lax.broadcasted_iota(
        jnp.int32, (rows, rows), 1
    )
    before = jnp.dot(
        hits.astype(jnp.bfloat16),
        earlier.astype(jnp.float32).astype(jnp.bfloat16),
        preferred_element_type=jnp.float32,
    )
    slot = jnp.sum(hits * before, axis=0, keepdims=True).astype(jnp.int32)
    target = relative * capacity + slot
    place_hot = lax.broadcasted_iota(jnp.int32, (places, rows), 0) == target
    place_hot = place_hot.astype(jnp.float32).astype(jnp.bfloat16)
    token_hot = lax.broadcasted_iota(jnp.int32, (tok_count, rows), 0) == token_ref[...]
    token_hot = token_hot.astype(jnp.float32)
    contract = (((1,), (1,)), ((), ()))
    pick = lax.dot_general(
        place_hot, token_hot.astype(jnp.bfloat16), contract, preferred_element_type=jnp.float32
    ).astype(jnp.bfloat16)
    stores = []
    for k in range(tiles):
        cols = pl.ds(k * tile, tile)
        large[k].wait()
        picked = jnp.dot(pick, tok_ref[:, cols], preferred_element_type=jnp.float32)
        for s in range(experts):
            out_ref[s, :, cols] = picked[s * capacity : (s + 1) * capacity].astype(jnp.bfloat16)
    for s in range(experts):
        copy = pltpu.make_async_copy(out_ref.at[s], bufs[s], out_sems.at[s])
        copy.start()
        stores.append(copy)
    gate = gate_ref[...]
    gate_hi = gate.astype(jnp.bfloat16).astype(jnp.float32)
    for part, ref in ((gate_hi, hi_ref), (gate - gate_hi, lo_ref)):
        ref[...] = lax.dot_general(
            (token_hot * part).astype(jnp.bfloat16),
            place_hot,
            contract,
            preferred_element_type=jnp.float32,
        ).astype(jnp.bfloat16)
    for copy in stores:
        copy.wait()


def run_route(experts, capacity, me, route_expert, route_token, route_gate, tokens):
    tok_count, width = tokens.shape
    rows = route_token.shape[0]
    block = jax.ShapeDtypeStruct((capacity, width), jnp.bfloat16)
    mix = jax.ShapeDtypeStruct((tok_count, experts * capacity), jnp.bfloat16)
    return pl.pallas_call(
        functools.partial(route_kernel, experts, capacity),
        out_shape=[block] * experts + [mix] * 2,
        in_specs=[SMEM] + [ANY] * 4,
        out_specs=[ANY] * experts + [VMEM] * 2,
        scratch_shapes=[
            pltpu.VMEM((1, rows), jnp.int32),
            pltpu.VMEM((1, rows), jnp.int32),
            pltpu.VMEM((1, rows), jnp.float32),
            pltpu.VMEM((tok_count, width), jnp.bfloat16),
            pltpu.VMEM((experts, capacity, width), jnp.bfloat16),
            pltpu.SemaphoreType.DMA((3 + width // column_tile(width),)),
            pltpu.SemaphoreType.DMA((experts,)),
        ],
        compiler_params=pltpu.CompilerParams(vmem_limit_bytes=60 * MIB),
    )(
        me,
        route_expert.reshape(1, rows),
        route_token.reshape(1, rows),
        route_gate.reshape(1, rows),
        tokens,
    )


def expert_kernel(chunks, backs, me_ref, *refs):
    count = 2 * len(chunks)
    pieces, (win_a, win_b, wout_a, wout_b) = refs[:count], refs[count : count + 4]
    outs, hids = refs[count + 4 : count + 4 + 2 * len(backs)], refs[count + 4 + 2 * len(backs) : -2]
    rows_ref, hidden_ref = refs[-2:]
    units, width = wout_a.shape
    capacity = hids[0].shape[1]
    tile = column_tile(width)
    at = 0
    for piece in pieces:
        rows_ref[at : at + piece.shape[0]] = piece[...]
        at += piece.shape[0]
    me = me_ref[0]
    layer, chip, core = me // SLICES, (me % SLICES) // 2, me % 2
    lane_mask = (FIRST + core * (SECOND - FIRST)) // 2
    cross_mask = (SECOND - core * (SECOND - FIRST)) // 2
    masks = (0, lane_mask, cross_mask, lane_mask ^ cross_mask)
    blocks = [(s, k) for chunk in chunks for k in range(4) for s in chunk]
    for half, (win, hid) in enumerate(zip((win_a, win_b), hids)):
        total = jnp.dot(rows_ref[...], win[...], preferred_element_type=jnp.float32)
        gate, up = total[:, :units], total[:, units:]
        value = (gate / (1.0 + jnp.exp(-gate)) * up).astype(jnp.bfloat16)
        hidden_ref[:, units * half : units * (half + 1)] = value
        value = value.astype(jnp.float32)
        for i, (s, k) in enumerate(blocks):
            hid[(layer ^ s) * CHIPS + (chip ^ masks[k])] = value[
                i * capacity : (i + 1) * capacity
            ].astype(jnp.bfloat16)
    for at in range(0, width, tile):
        cols = slice(at, at + tile)
        out = jnp.dot(hidden_ref[:, :units], wout_a[:, cols], preferred_element_type=jnp.float32)
        out += jnp.dot(hidden_ref[:, units:], wout_b[:, cols], preferred_element_type=jnp.float32)
        for i, ref in enumerate(outs):
            parts = []
            for k in (0, 1) if i % 2 == 0 else (2, 3):
                for s in backs[i // 2]:
                    start = blocks.index((s, k)) * capacity
                    parts.append(out[start : start + capacity])
            ref[:, cols] = jnp.concatenate(parts, axis=0).astype(jnp.bfloat16)


def run_expert(chunks, backs, capacity, me, pieces, weights):
    width = pieces[0].shape[1]
    units = weights[2].shape[0]
    rows = sum(piece.shape[0] for piece in pieces)
    hid = jax.ShapeDtypeStruct((rows // capacity, capacity, units), jnp.bfloat16)
    outs = [
        jax.ShapeDtypeStruct((2 * len(back) * capacity, width), jnp.bfloat16)
        for back in backs
        for _ in (0, 1)
    ]
    return pl.pallas_call(
        functools.partial(expert_kernel, chunks, backs),
        out_shape=outs + [hid] * 2,
        in_specs=[SMEM] + [VMEM] * (len(pieces) + 4),
        out_specs=[VMEM] * (len(outs) + 2),
        scratch_shapes=[
            pltpu.VMEM((rows, width), jnp.bfloat16),
            pltpu.VMEM((rows, 2 * units), jnp.bfloat16),
        ],
        compiler_params=pltpu.CompilerParams(vmem_limit_bytes=16 * MIB),
        cost_estimate=pl.CostEstimate(flops=1, bytes_accessed=1, transcendentals=0),
    )(me, *pieces, *weights)


def weave_kernel(me_ref, mine_ref, other_ref, out_ref):
    core = me_ref[0] % 2
    out_ref[:, pl.ds(core, 1)] = mine_ref[...][:, None]
    out_ref[:, pl.ds(1 - core, 1)] = other_ref[...][:, None]


def keep_kernel(me_ref, swap_ref, mine_ref, far_ref, out_ref):
    flag = swap_ref[me_ref[0] % swap_ref.shape[0]]
    out_ref[...] = jnp.where(flag == 1, far_ref[...], mine_ref[...])


def mix_kernel(hi_ref, lo_ref, *refs):
    values = [r[...].astype(jnp.float32) for r in refs[:-1]]
    rows = jnp.concatenate(values, axis=0).astype(jnp.bfloat16)
    total = jnp.dot(hi_ref[...], rows, preferred_element_type=jnp.float32)
    total += jnp.dot(lo_ref[...], rows, preferred_element_type=jnp.float32)
    refs[-1][...] = total.astype(jnp.bfloat16)


def shards(tokens, route_token, route_expert, route_gate, w_in, w_out, swap_pairs):
    devices = lax.axis_size("ep")
    half_axis = devices // 2
    tok_count, width = tokens.shape
    units = w_out.shape[1]
    rows_dev = route_token.shape[0]
    experts = devices // SLICES
    capacity = min(rows_dev, 3 * rows_dev // (2 * experts))
    places = experts * capacity
    me = lax.axis_index("ep").astype(jnp.int32).reshape(1)
    small = pltpu.CompilerParams(vmem_limit_bytes=16 * MIB)

    weights = [
        w_in[0],
        swap(w_in[0], lambda i: CORE),
        w_out[0],
        swap(w_out[0], lambda i: CORE),
    ]
    *bufs, gate_hi, gate_lo = run_route(
        experts, capacity, me, route_expert, route_token, route_gate, tokens
    )

    chunks = [[0], [1, experts - 1]] + [[s] for s in range(2, experts - 1)]
    backs = [[s] for s in reversed(range(experts))]
    received = {0: bufs[0]}
    gathered = {}
    ready = list(bufs)
    for c, chunk in enumerate(chunks):
        for s in chunk:
            if s:
                received[s] = swap(ready[s], lambda i: SLICES * s)
        if c == 1:
            kept = [received[s] for s in chunk]
            kept = after(kept, gathered[0][0])
            ready, kept = lax.optimization_barrier((ready, kept))
            for s, value in zip(chunk, kept):
                received[s] = value
        if c > 1:
            kept = after([received[s] for s in chunk], gathered[c - 1][0])
            received.update(zip(chunk, kept))
        mine = jnp.concatenate([received[s] for s in chunk], axis=0)
        beside = swap(mine, lane)
        both = jnp.concatenate([mine, beside], axis=0)
        gathered[c] = [both, swap(both, cross)]

    *outs, hid_a, hid_b = run_expert(
        chunks, backs, capacity, me, sum([gathered[c] for c in range(len(chunks))], []), weights
    )

    finals = [None] * experts
    lasts, got, totals = [], [], []
    for b, back in enumerate(backs):
        near, away = outs[2 * b : 2 * b + 2]
        half = near.shape[0] // 2
        if b > 1:
            away = after(away, got[b - 2])
        came = swap(away, cross)
        if b > 1:
            came = after(came, totals[b - 2 : b - 1])
        got.append(came)
        relay = near[half:].astype(jnp.float32) + came[half:].astype(jnp.float32)
        last = swap(relay.astype(jnp.bfloat16), lane)
        lasts.append(last)
        part = []
        for i, s in enumerate(back):
            rows = slice(i * capacity, (i + 1) * capacity)
            total = sum(v[rows].astype(jnp.float32) for v in (near, came, last))
            total = total.astype(jnp.bfloat16)
            part.append(total)
            finals[s] = total if s == 0 else swap(total, lambda i: SLICES * s)
        totals.append(part)

    tile = column_tile(width)
    moving = lambda rows: pl.BlockSpec((rows, tile), lambda i: (0, i))
    fixed = pl.BlockSpec((tok_count, places), lambda i: (0, 0))
    mixed = pl.pallas_call(
        mix_kernel,
        out_shape=jax.ShapeDtypeStruct((tok_count, width), jnp.bfloat16),
        grid=(width // tile,),
        in_specs=[fixed] * 2 + [moving(capacity)] * experts,
        out_specs=moving(tok_count),
        compiler_params=small,
    )(gate_hi, gate_lo, *finals)

    other = swap(hid_b, lambda i: CORE)
    full = pl.pallas_call(
        weave_kernel,
        out_shape=jax.ShapeDtypeStruct((devices // 2, 2, capacity, units), jnp.bfloat16),
        in_specs=[SMEM, VMEM, VMEM],
        out_specs=VMEM,
        compiler_params=small,
    )(me, hid_a, other)
    far = after(swap(full, lambda i: half_axis), lasts[:2])
    saved = pl.pallas_call(
        keep_kernel,
        out_shape=jax.ShapeDtypeStruct(full.shape, full.dtype),
        in_specs=[SMEM, SMEM, VMEM, VMEM],
        out_specs=pl.BlockSpec(),
        compiler_params=small,
    )(me, swap_pairs, full, far)
    return (mixed, saved.reshape(1, devices * capacity, units))


def solution(mesh):
    return jax.shard_map(
        shards,
        mesh=mesh,
        in_specs=(
            P(("rep", "ep"), None),
            P(("rep", "ep")),
            P(("rep", "ep"), None),
            P(("rep", "ep")),
            P("ep", None, None),
            P("ep", None, None),
            P(),
        ),
        out_specs=(P(("rep", "ep"), None), P(("rep", "ep"), None, None)),
        check_vma=False,
    )
```

time: 295 us -> 82.4 us (0.28)
  blocking collectives: 130 us -> 0 us
  waiting for transfers between devices: 127 us -> 38.9 us
  starting transfers between devices: 6.37 us -> 31.7 us
  matrix products: 15.3 us -> 0 us
  Pallas kernels: 0 us -> 9.19 us
  other arithmetic: 7.77 us -> 0.47 us
  local copies, waits for them, and re-layouts: 6.48 us -> 1.04 us
    all_to_all x1 -> x0, blocking collectives: 130 us -> none  [shards(): lax.all_to_all(outgoing, 'ep', split_axis=0, concat_axis=0, tiled=True)]
    ppermute x1 -> x24, waiting for transfers between devices: 127 us -> 38.9 us  [swap(): lax.ppermute(value, 'ep', [(i, i ^ mask_of(i)) for i in range(count)])]
    ppermute x1 -> x24, starting transfers between devices: 2.65 us -> 31.7 us  [swap(): lax.ppermute(value, 'ep', [(i, i ^ mask_of(i)) for i in range(count)])]
    dot_general x6 -> x0, matrix products: 15.3 us -> none  [the longest x1 5.75 us: shards(): jnp.einsum('je,jcd->ecd', owner_table, returned, preferred_element_type=j...]
    pallas_call x0 -> x5, Pallas kernels: none -> 9.19 us  [the longest x1 3.13 us: run_route(): pl.pallas_call(functools.partial(route_kernel, experts, capacity), out_sh...]
    gather x2 -> x0, local copies, waits for them, and re-layouts: 5.87 us -> none  [the longest x1 3.29 us: shards(): outgoing = jnp.take(expert_buf, served_expert, axis=0)]
    select_n x5 -> x0, other arithmetic: 4.52 us -> none  [the longest x2 3.16 us: shards(): outgoing = jnp.take(expert_buf, served_expert, axis=0)]
    all_to_all x1 -> x0, starting transfers between devices: 3.72 us -> none  [shards(): lax.all_to_all(partial_value.reshape(devices, item_count, feature_width),...]
  transfers between devices with their start and end apart: 2 -> 24, of which waited for: 1 -> 12; matrix products, arithmetic and copies ran while one was open for 0% -> 2% of each run, Pallas kernels for 0% -> 2%
where the time goes in v3:
time: 82.4 us; the launch traced here: 82.2 us
  waiting for transfers between devices  38.9 us (47%)
  starting transfers between devices  31.7 us (38%)
  Pallas kernels  9.19 us (11%)
  local copies, waits for them, and re-layouts  1.04 us (1%)
  between operations  0.84 us (1%)
    ppermute x24, waiting for transfers between devices, swap(): lax.ppermute(value, 'ep', [(i, i ^ mask_of(i)) for i in range(count)])  38.9 us
    ppermute x24, starting transfers between devices, swap(): lax.ppermute(value, 'ep', [(i, i ^ mask_of(i)) for i in range(count)])  31.7 us
    pallas_call x1, Pallas kernels, run_route(): pl.pallas_call(functools.partial(route_kernel, experts, capacity), out_sh...  3.13 us
    pallas_call x1, Pallas kernels, run_expert(): pl.pallas_call(functools.partial(expert_kernel, chunks, backs), out_shape...  3.12 us
  transfers between devices with their start and end apart: 24, of which 12 were waited for; matrix products, arithmetic and copies ran while one was open for 2% of the time, Pallas kernels for 2%

profile of v3, /device:TPU:0, one launch (start us, length us, event | category | flops | bytes accessed | tf_op | source)
XLA Modules:
  0.0 82.2 jit_solution(12368138690197224743)
XLA Ops:
  0.6 3.1 %shard_map.86 = (bf16[24,3584]{1,0:T(8,128)(2,1)}, bf16[24,3584]{1,0:T(8,128)(2,1)}, bf16[24,3584]{1,0:T(8,128)(2,1)}, bf16[24,3584]{1,0:T(8,128)(2,1)}, bf16[12...) custom-call(s32[1]{0:T(128)} %bitcast.me_ref, s32[1,64]{1,0:T(1,128)} %bitcast.12, s32[1,64]{1,0:T(1,128)} %bitcast.13, ...), custom_call_target="tpu_custom_call" | custom-call | tf_op jit(solution)/shard_map/pallas_call | solution.py:114
  3.8 3.1 %collective-permute-start.2 = (bf16[24,3584]{1,0:T(8,128)(2,1)}, bf16[24,3584]{1,0:T(8,128)(2,1)S(1)}, u32[]{:S(2)}, u32[]{:S(2)}) collective-permute-start(bf16[24,3584]{1,0:T(8,128)(2,1)} %get-tuple-element.32), channel_id=1, source_target_pairs={{0,8},{1,9},{2,10},{3,11},{4,12},{5,13},{6,14},{7,15},{8,0},{9,1},... | collective-permute-start | bytes 516104 | tf_op jit(solution)/shard_map/ppermute | solution.py:21
  6.9 2.5 %collective-permute-start.3 = (bf16[24,3584]{1,0:T(8,128)(2,1)}, bf16[24,3584]{1,0:T(8,128)(2,1)S(1)}, u32[]{:S(2)}, u32[]{:S(2)}) collective-permute-start(bf16[24,3584]{1,0:T(8,128)(2,1)} %get-tuple-element.34), channel_id=1, source_target_pairs={{0,24},{1,25},{2,26},{3,27},{4,28},{5,29},{6,30},{7,31},{8,16},{9,... | collective-permute-start | bytes 516104 | tf_op jit(solution)/shard_map/ppermute | solution.py:21
  12.3 2.7 %collective-permute-done = bf16[24,3584]{1,0:T(8,128)(2,1)S(1)} collective-permute-done((bf16[24,3584]{1,0:T(8,128)(2,1)}, bf16[24,3584]{1,0:T(8,128)(2,1)S(1)}, u32[]{:S(2)}, u32[]{:S(2)}) %collective-permute-start) | collective-permute-done | bytes 172064 | tf_op jit(solution)/shard_map/ppermute | solution.py:21
  15.0 1.6 %collective-permute-start.1 = (bf16[48,3584]{1,0:T(8,128)(2,1)S(1)}, bf16[48,3584]{1,0:T(8,128)(2,1)S(1)}, u32[]{:S(2)}, u32[]{:S(2)}) collective-permute-start(bf16[48,3584]{1,0:T(8,128)(2,1)S(1)} %constant_dynamic-update-slice_fusion.refs_0_), channel_id=1, source_target_pairs={{0,4},{1,3},{2,6},{3,1},{4,0},{5,7},{6,2},{7,5},{8,12},{9,11},{10,... | collective-permute-start | bytes 1032200 | tf_op jit(solution)/shard_map/ppermute | solution.py:21
  17.4 1.8 %collective-permute-start.6 = (bf16[24,3584]{1,0:T(8,128)(2,1)}, bf16[24,3584]{1,0:T(8,128)(2,1)S(1)}, u32[]{:S(2)}, u32[]{:S(2)}) collective-permute-start(bf16[24,3584]{1,0:T(8,128)(2,1)} %get-tuple-element.39), channel_id=1, source_target_pairs={{0,16},{1,17},{2,18},{3,19},{4,20},{5,21},{6,22},{7,23},{8,24},{9,... | collective-permute-start | bytes 516104 | tf_op jit(solution)/shard_map/ppermute | solution.py:21
  20.8 5.7 %collective-permute-done.4 = bf16[48,3584]{1,0:T(8,128)(2,1)S(1)} collective-permute-done((bf16[48,3584]{1,0:T(8,128)(2,1)S(1)}, bf16[48,3584]{1,0:T(8,128)(2,1)S(1)}, u32[]{:S(2)}, u32[]{:S(2)}) %collective-permute-start.4) | collective-permute-done | bytes 344096 | tf_op jit(solution)/shard_map/ppermute | solution.py:21
  28.2 1.6 %collective-permute-start.5 = (bf16[96,3584]{1,0:T(8,128)(2,1)S(1)}, bf16[96,3584]{1,0:T(8,128)(2,1)S(1)}, u32[]{:S(2)}, u32[]{:S(2)}) collective-permute-start(bf16[96,3584]{1,0:T(8,128)(2,1)S(1)} %constant_dynamic-update-slice_fusion.2.refs_2_), channel_id=1, source_target_pairs={{0,4},{1,3},{2,6},{3,1},{4,0},{5,7},{6,2},{7,5},{8,12},{9,11},{10,... | collective-permute-start | bytes 2064392 | tf_op jit(solution)/shard_map/ppermute | solution.py:21
  29.8 4.2 %collective-permute-done.7 = bf16[24,3584]{1,0:T(8,128)(2,1)S(1)} collective-permute-done((bf16[24,3584]{1,0:T(8,128)(2,1)S(1)}, bf16[24,3584]{1,0:T(8,128)(2,1)S(1)}, u32[]{:S(2)}, u32[]{:S(2)}) %collective-permute-start.7) | collective-permute-done | bytes 172064 | tf_op jit(solution)/shard_map/ppermute | solution.py:21
  33.9 1.6 %collective-permute-start.8 = (bf16[48,3584]{1,0:T(8,128)(2,1)S(1)}, bf16[48,3584]{1,0:T(8,128)(2,1)S(1)}, u32[]{:S(2)}, u32[]{:S(2)}) collective-permute-start(bf16[48,3584]{1,0:T(8,128)(2,1)S(1)} %constant_dynamic-update-slice_fusion.5.refs_4_), channel_id=1, source_target_pairs={{0,4},{1,3},{2,6},{3,1},{4,0},{5,7},{6,2},{7,5},{8,12},{9,11},{10,... | collective-permute-start | bytes 1032200 | tf_op jit(solution)/shard_map/ppermute | solution.py:21
  35.5 7.3 %collective-permute-done.8.refs_5_ = bf16[48,3584]{1,0:T(8,128)(2,1)S(1)} collective-permute-done((bf16[48,3584]{1,0:T(8,128)(2,1)S(1)}, bf16[48,3584]{1,0:T(8,128)(2,1)S(1)}, u32[]{:S(2)}, u32[]{:S(2)}) %collective-permute-start.8) | collective-permute-done | bytes 344096 | tf_op jit(solution)/shard_map/ppermute | solution.py:21
  42.9 3.1 %shard_map.87 = (bf16[48,3584]{1,0:T(8,128)(2,1)S(1)}, bf16[48,3584]{1,0:T(8,128)(2,1)S(1)}, bf16[48,3584]{1,0:T(8,128)(2,1)S(1)}, bf16[48,3584]{1,0:T(8,128)(2,...) custom-call(s32[1]{0:T(128)} %bitcast.me_ref, ...), custom_call_target="tpu_custom_call" | custom-call | flops 1 | bytes 1 | tf_op jit(solution)/shard_map/pallas_call | solution.py:189
  46.0 1.6 %collective-permute-start.11 = (bf16[48,3584]{1,0:T(8,128)(2,1)S(1)}, bf16[48,3584]{1,0:T(8,128)(2,1)S(1)}, u32[]{:S(2)}, u32[]{:S(2)}) collective-permute-start(bf16[48,3584]{1,0:T(8,128)(2,1)S(1)} %get-tuple-element.43), channel_id=1, source_target_pairs={{0,4},{1,3},{2,6},{3,1},{4,0},{5,7},{6,2},{7,5},{8,12},{9,11},{10,... | collective-permute-start | bytes 1032200 | tf_op jit(solution)/shard_map/ppermute | solution.py:21
  50.2 3.2 %collective-permute-done.11 = bf16[48,3584]{1,0:T(8,128)(2,1)S(1)} collective-permute-done((bf16[48,3584]{1,0:T(8,128)(2,1)S(1)}, bf16[48,3584]{1,0:T(8,128)(2,1)S(1)}, u32[]{:S(2)}, u32[]{:S(2)}) %collective-permute-start.11) | collective-permute-done | bytes 344096 | tf_op jit(solution)/shard_map/ppermute | solution.py:21
  55.5 3.2 %collective-permute-done.15 = bf16[48,3584]{1,0:T(8,128)(2,1)S(1)} collective-permute-done((bf16[48,3584]{1,0:T(8,128)(2,1)S(1)}, bf16[48,3584]{1,0:T(8,128)(2,1)S(1)}, u32[]{:S(2)}, u32[]{:S(2)}) %collective-permute-start.15) | collective-permute-done | bytes 344096 | tf_op jit(solution)/shard_map/ppermute | solution.py:21
  58.8 2.4 %collective-permute-start.16 = (bf16[48,3584]{1,0:T(8,128)(2,1)S(1)}, bf16[48,3584]{1,0:T(8,128)(2,1)S(1)}, u32[]{:S(2)}, u32[]{:S(2)}) collective-permute-start(bf16[48,3584]{1,0:T(8,128)(2,1)S(1)} %get-tuple-element.50), channel_id=1, source_target_pairs={{0,4},{1,3},{2,6},{3,1},{4,0},{5,7},{6,2},{7,5},{8,12},{9,11},{10,... | collective-permute-start | bytes 1032200 | tf_op jit(solution)/shard_map/ppermute | solution.py:21
  61.3 2.3 %collective-permute-start.20 = (bf16[24,3584]{1,0:T(8,128)(2,1)S(1)}, bf16[24,3584]{1,0:T(8,128)(2,1)S(1)}, u32[]{:S(2)}, u32[]{:S(2)}) collective-permute-start(bf16[24,3584]{1,0:T(8,128)(2,1)S(1)} %add_convert_fusion.6), channel_id=1, source_target_pairs={{0,16},{1,17},{2,18},{3,19},{4,20},{5,21},{6,22},{7,23},{8,24},{9,... | collective-permute-start | bytes 516104 | tf_op jit(solution)/shard_map/ppermute | solution.py:21
  63.6 2.5 %collective-permute-done.17 = bf16[24,3584]{1,0:T(8,128)(2,1)S(1)} collective-permute-done((bf16[24,3584]{1,0:T(8,128)(2,1)S(1)}, bf16[24,3584]{1,0:T(8,128)(2,1)S(1)}, u32[]{:S(2)}, u32[]{:S(2)}) %collective-permute-start.17) | collective-permute-done | bytes 172064 | tf_op jit(solution)/shard_map/ppermute | solution.py:21
  66.2 2.0 %collective-permute-start.21 = (bf16[24,3584]{1,0:T(8,128)(2,1)S(1)}, bf16[24,3584]{1,0:T(8,128)(2,1)S(1)}, u32[]{:S(2)}, u32[]{:S(2)}) collective-permute-start(bf16[24,3584]{1,0:T(8,128)(2,1)S(1)} %add_convert_fusion.2), channel_id=1, source_target_pairs={{0,24},{1,25},{2,26},{3,27},{4,28},{5,29},{6,30},{7,31},{8,16},{9,... | collective-permute-start | bytes 516104 | tf_op jit(solution)/shard_map/ppermute | solution.py:21
  69.7 2.1 %collective-permute-start.14 = (bf16[24,3584]{1,0:T(8,128)(2,1)S(1)}, bf16[24,3584]{1,0:T(8,128)(2,1)S(1)}, u32[]{:S(2)}, u32[]{:S(2)}) collective-permute-start(bf16[24,3584]{1,0:T(8,128)(2,1)S(1)} %add_convert_fusion.5), channel_id=1, source_target_pairs={{0,2},{1,5},{2,0},{3,7},{4,6},{5,1},{6,4},{7,3},{8,10},{9,13},{10,... | collective-permute-start | bytes 516104 | tf_op jit(solution)/shard_map/ppermute | solution.py:21
  71.7 3.3 %collective-permute-done.18 = bf16[24,3584]{1,0:T(8,128)(2,1)S(1)} collective-permute-done((bf16[24,3584]{1,0:T(8,128)(2,1)S(1)}, bf16[24,3584]{1,0:T(8,128)(2,1)S(1)}, u32[]{:S(2)}, u32[]{:S(2)}) %collective-permute-start.18) | collective-permute-done | bytes 172064 | tf_op jit(solution)/shard_map/ppermute | solution.py:21
  75.2 1.7 %collective-permute-done.14 = bf16[24,3584]{1,0:T(8,128)(2,1)S(1)} collective-permute-done((bf16[24,3584]{1,0:T(8,128)(2,1)S(1)}, bf16[24,3584]{1,0:T(8,128)(2,1)S(1)}, u32[]{:S(2)}, u32[]{:S(2)}) %collective-permute-start.14) | collective-permute-done | bytes 172064 | tf_op jit(solution)/shard_map/ppermute | solution.py:21
  76.9 3.6 %collective-permute-done.19.refs_1_ = bf16[24,3584]{1,0:T(8,128)(2,1)S(1)} collective-permute-done((bf16[24,3584]{1,0:T(8,128)(2,1)S(1)}, bf16[24,3584]{1,0:T(8,128)(2,1)S(1)}, u32[]{:S(2)}, u32[]{:S(2)}) %collective-permute-start.19) | collective-permute-done | bytes 172064 | tf_op jit(solution)/shard_map/ppermute | solution.py:21
  80.5 1.6 %shard_map.88 = bf16[128,3584]{1,0:T(8,128)(2,1)} custom-call(bf16[128,96]{1,0:T(8,128)(2,1)S(1)} %copy-done.2, bf16[128,96]{1,0:T(8,128)(2,1)S(1)} %copy-done.3, bf16[24,3584]{1,0:T(8,128)(2,1)S(1)} %add_convert_fusion.4.refs_0_, bf16[24,3584]{1,0:T(8,128)(2,1)S(1)} %collective-permute-done.19.refs_1_, ...), custom_call_target="tpu_custom_call" | custom-call | tf_op jit(solution)/shard_map/pallas_call | solution.py:297
  (55 shorter events, 13.7 us)
Async XLA Ops:
  3.8 12.8 %collective-permute-start.2 = (bf16[24,3584]{1,0:T(8,128)(2,1)}, bf16[24,3584]{1,0:T(8,128)(2,1)S(1)}, u32[]{:S(2)}, u32[]{:S(2)}) collective-permute-start(bf16[24,3584]{1,0:T(8,128)(2,1)} %get-tuple-element.32), channel_id=1, source_target_pairs={{0,8},{1,9},{2,10},{3,11},{4,12},{5,13},{6,14},{7,15},{8,0},{9,1},... | collective-permute-start | bytes 516104 | tf_op jit(solution)/shard_map/ppermute | solution.py:21
  6.9 10.6 %collective-permute-start.3 = (bf16[24,3584]{1,0:T(8,128)(2,1)}, bf16[24,3584]{1,0:T(8,128)(2,1)S(1)}, u32[]{:S(2)}, u32[]{:S(2)}) collective-permute-start(bf16[24,3584]{1,0:T(8,128)(2,1)} %get-tuple-element.34), channel_id=1, source_target_pairs={{0,24},{1,25},{2,26},{3,27},{4,28},{5,29},{6,30},{7,31},{8,16},{9,... | collective-permute-start | bytes 516104 | tf_op jit(solution)/shard_map/ppermute | solution.py:21
  9.4 5.6 %collective-permute-start = (bf16[24,3584]{1,0:T(8,128)(2,1)}, bf16[24,3584]{1,0:T(8,128)(2,1)S(1)}, u32[]{:S(2)}, u32[]{:S(2)}) collective-permute-start(bf16[24,3584]{1,0:T(8,128)(2,1)} %get-tuple-element.31), channel_id=1, source_target_pairs={{0,2},{1,5},{2,0},{3,7},{4,6},{5,1},{6,4},{7,3},{8,10},{9,13},{10,... | collective-permute-start | bytes 516104 | tf_op jit(solution)/shard_map/ppermute | solution.py:21
  10.8 24.7 %collective-permute-start.10 = (bf16[128,3584]{1,0:T(8,128)(2,1)}, bf16[128,3584]{1,0:T(8,128)(2,1)S(1)}, u32[]{:S(2)}, u32[]{:S(2)}) collective-permute-start(bf16[128,3584]{1,0:T(8,128)(2,1)} %bitcast.9), channel_id=1, source_target_pairs={{0,1},{1,0},{2,3},{3,2},{4,5},{5,4},{6,7},{7,6},{8,9},{9,8},{10,11... | collective-permute-start | bytes 2752520 | tf_op jit(solution)/shard_map/ppermute | solution.py:21
  10.8 32.0 %collective-permute-start.9 = (bf16[3584,256]{1,0:T(8,128)(2,1)}, bf16[3584,256]{1,0:T(8,128)(2,1)S(1)}, u32[]{:S(2)}, u32[]{:S(2)}) collective-permute-start(bf16[3584,256]{1,0:T(8,128)(2,1)} %bitcast.7), channel_id=1, source_target_pairs={{0,1},{1,0},{2,3},{3,2},{4,5},{5,4},{6,7},{7,6},{8,9},{9,8},{10,11... | collective-permute-start | bytes 5505032 | tf_op jit(solution)/shard_map/ppermute | solution.py:21
  15.0 20.5 %collective-permute-start.1 = (bf16[48,3584]{1,0:T(8,128)(2,1)S(1)}, bf16[48,3584]{1,0:T(8,128)(2,1)S(1)}, u32[]{:S(2)}, u32[]{:S(2)}) collective-permute-start(bf16[48,3584]{1,0:T(8,128)(2,1)S(1)} %constant_dynamic-update-slice_fusion.refs_0_), channel_id=1, source_target_pairs={{0,4},{1,3},{2,6},{3,1},{4,0},{5,7},{6,2},{7,5},{8,12},{9,11},{10,... | collective-permute-start | bytes 1032200 | tf_op jit(solution)/shard_map/ppermute | solution.py:21
  17.4 9.1 %collective-permute-start.6 = (bf16[24,3584]{1,0:T(8,128)(2,1)}, bf16[24,3584]{1,0:T(8,128)(2,1)S(1)}, u32[]{:S(2)}, u32[]{:S(2)}) collective-permute-start(bf16[24,3584]{1,0:T(8,128)(2,1)} %get-tuple-element.39), channel_id=1, source_target_pairs={{0,16},{1,17},{2,18},{3,19},{4,20},{5,21},{6,22},{7,23},{8,24},{9,... | collective-permute-start | bytes 516104 | tf_op jit(solution)/shard_map/ppermute | solution.py:21
  19.2 7.3 %collective-permute-start.4 = (bf16[48,3584]{1,0:T(8,128)(2,1)S(1)}, bf16[48,3584]{1,0:T(8,128)(2,1)S(1)}, u32[]{:S(2)}, u32[]{:S(2)}) collective-permute-start(bf16[48,3584]{1,0:T(8,128)(2,1)S(1)} %pad_maximum_fusion), channel_id=1, source_target_pairs={{0,2},{1,5},{2,0},{3,7},{4,6},{5,1},{6,4},{7,3},{8,10},{9,13},{10,... | collective-permute-start | bytes 1032200 | tf_op jit(solution)/shard_map/ppermute | solution.py:21
  26.6 7.3 %collective-permute-start.7 = (bf16[24,3584]{1,0:T(8,128)(2,1)S(1)}, bf16[24,3584]{1,0:T(8,128)(2,1)S(1)}, u32[]{:S(2)}, u32[]{:S(2)}) collective-permute-start(bf16[24,3584]{1,0:T(8,128)(2,1)S(1)} %collective-permute-done.6), channel_id=1, source_target_pairs={{0,2},{1,5},{2,0},{3,7},{4,6},{5,1},{6,4},{7,3},{8,10},{9,13},{10,... | collective-permute-start | bytes 516104 | tf_op jit(solution)/shard_map/ppermute | solution.py:21
  28.2 14.7 %collective-permute-start.5 = (bf16[96,3584]{1,0:T(8,128)(2,1)S(1)}, bf16[96,3584]{1,0:T(8,128)(2,1)S(1)}, u32[]{:S(2)}, u32[]{:S(2)}) collective-permute-start(bf16[96,3584]{1,0:T(8,128)(2,1)S(1)} %constant_dynamic-update-slice_fusion.2.refs_2_), channel_id=1, source_target_pairs={{0,4},{1,3},{2,6},{3,1},{4,0},{5,7},{6,2},{7,5},{8,12},{9,11},{10,... | collective-permute-start | bytes 2064392 | tf_op jit(solution)/shard_map/ppermute | solution.py:21
  33.9 8.9 %collective-permute-start.8 = (bf16[48,3584]{1,0:T(8,128)(2,1)S(1)}, bf16[48,3584]{1,0:T(8,128)(2,1)S(1)}, u32[]{:S(2)}, u32[]{:S(2)}) collective-permute-start(bf16[48,3584]{1,0:T(8,128)(2,1)S(1)} %constant_dynamic-update-slice_fusion.5.refs_4_), channel_id=1, source_target_pairs={{0,4},{1,3},{2,6},{3,1},{4,0},{5,7},{6,2},{7,5},{8,12},{9,11},{10,... | collective-permute-start | bytes 1032200 | tf_op jit(solution)/shard_map/ppermute | solution.py:21
  46.0 7.3 %collective-permute-start.11 = (bf16[48,3584]{1,0:T(8,128)(2,1)S(1)}, bf16[48,3584]{1,0:T(8,128)(2,1)S(1)}, u32[]{:S(2)}, u32[]{:S(2)}) collective-permute-start(bf16[48,3584]{1,0:T(8,128)(2,1)S(1)} %get-tuple-element.43), channel_id=1, source_target_pairs={{0,4},{1,3},{2,6},{3,1},{4,0},{5,7},{6,2},{7,5},{8,12},{9,11},{10,... | collective-permute-start | bytes 1032200 | tf_op jit(solution)/shard_map/ppermute | solution.py:21
  47.6 1.3 %collective-permute-start.22 = (bf16[16,24,128]{2,1,0:T(8,128)(2,1)S(1)}, bf16[16,24,128]{2,1,0:T(8,128)(2,1)S(1)}, u32[]{:S(2)}, u32[]{:S(2)}) collective-permute-start(bf16[16,24,128]{2,1,0:T(8,128)(2,1)S(1)} %get-tuple-element.54), channel_id=1, source_target_pairs={{0,1},{1,0},{2,3},{3,2},{4,5},{5,4},{6,7},{7,6},{8,9},{9,8},{10,11... | collective-permute-start | bytes 294920 | tf_op jit(solution)/shard_map/ppermute | solution.py:21
  47.6 11.1 %collective-permute-start.15 = (bf16[48,3584]{1,0:T(8,128)(2,1)S(1)}, bf16[48,3584]{1,0:T(8,128)(2,1)S(1)}, u32[]{:S(2)}, u32[]{:S(2)}) collective-permute-start(bf16[48,3584]{1,0:T(8,128)(2,1)S(1)} %get-tuple-element.49), channel_id=1, source_target_pairs={{0,4},{1,3},{2,6},{3,1},{4,0},{5,7},{6,2},{7,5},{8,12},{9,11},{10,... | collective-permute-start | bytes 1032200 | tf_op jit(solution)/shard_map/ppermute | solution.py:21
  48.9 17.2 %collective-permute-start.23 = (bf16[16,2,24,128]{3,2,1,0:T(8,128)(2,1)S(1)}, bf16[16,2,24,128]{3,2,1,0:T(8,128)(2,1)S(1)}, u32[]{:S(2)}, u32[]{:S(2)}) collective-permute-start(bf16[16,2,24,128]{3,2,1,0:T(8,128)(2,1)S(1)} %shard_map.89.mine_ref), channel_id=1, source_target_pairs={{0,16},{1,17},{2,18},{3,19},{4,20},{5,21},{6,22},{7,23},{8,24},{9,... | collective-permute-start | bytes 589832 | tf_op jit(solution)/shard_map/ppermute | solution.py:21
  53.4 7.9 %collective-permute-start.13 = (bf16[24,3584]{1,0:T(8,128)(2,1)S(1)}, bf16[24,3584]{1,0:T(8,128)(2,1)S(1)}, u32[]{:S(2)}, u32[]{:S(2)}) collective-permute-start(bf16[24,3584]{1,0:T(8,128)(2,1)S(1)} %add_convert_fusion.7), channel_id=1, source_target_pairs={{0,2},{1,5},{2,0},{3,7},{4,6},{5,1},{6,4},{7,3},{8,10},{9,13},{10,... | collective-permute-start | bytes 516104 | tf_op jit(solution)/shard_map/ppermute | solution.py:21
  54.0 15.5 %collective-permute-start.12 = (bf16[48,3584]{1,0:T(8,128)(2,1)S(1)}, bf16[48,3584]{1,0:T(8,128)(2,1)S(1)}, u32[]{:S(2)}, u32[]{:S(2)}) collective-permute-start(bf16[48,3584]{1,0:T(8,128)(2,1)S(1)} %get-tuple-element.44), channel_id=1, source_target_pairs={{0,4},{1,3},{2,6},{3,1},{4,0},{5,7},{6,2},{7,5},{8,12},{9,11},{10,... | collective-permute-start | bytes 1032200 | tf_op jit(solution)/shard_map/ppermute | solution.py:21
  58.7 7.4 %collective-permute-start.17 = (bf16[24,3584]{1,0:T(8,128)(2,1)S(1)}, bf16[24,3584]{1,0:T(8,128)(2,1)S(1)}, u32[]{:S(2)}, u32[]{:S(2)}) collective-permute-start(bf16[24,3584]{1,0:T(8,128)(2,1)S(1)} %add_convert_fusion.3), channel_id=1, source_target_pairs={{0,2},{1,5},{2,0},{3,7},{4,6},{5,1},{6,4},{7,3},{8,10},{9,13},{10,... | collective-permute-start | bytes 516104 | tf_op jit(solution)/shard_map/ppermute | solution.py:21
  58.8 10.7 %collective-permute-start.16 = (bf16[48,3584]{1,0:T(8,128)(2,1)S(1)}, bf16[48,3584]{1,0:T(8,128)(2,1)S(1)}, u32[]{:S(2)}, u32[]{:S(2)}) collective-permute-start(bf16[48,3584]{1,0:T(8,128)(2,1)S(1)} %get-tuple-element.50), channel_id=1, source_target_pairs={{0,4},{1,3},{2,6},{3,1},{4,0},{5,7},{6,2},{7,5},{8,12},{9,11},{10,... | collective-permute-start | bytes 1032200 | tf_op jit(solution)/shard_map/ppermute | solution.py:21
  61.3 15.6 %collective-permute-start.20 = (bf16[24,3584]{1,0:T(8,128)(2,1)S(1)}, bf16[24,3584]{1,0:T(8,128)(2,1)S(1)}, u32[]{:S(2)}, u32[]{:S(2)}) collective-permute-start(bf16[24,3584]{1,0:T(8,128)(2,1)S(1)} %add_convert_fusion.6), channel_id=1, source_target_pairs={{0,16},{1,17},{2,18},{3,19},{4,20},{5,21},{6,22},{7,23},{8,24},{9,... | collective-permute-start | bytes 516104 | tf_op jit(solution)/shard_map/ppermute | solution.py:21
  66.2 10.7 %collective-permute-start.21 = (bf16[24,3584]{1,0:T(8,128)(2,1)S(1)}, bf16[24,3584]{1,0:T(8,128)(2,1)S(1)}, u32[]{:S(2)}, u32[]{:S(2)}) collective-permute-start(bf16[24,3584]{1,0:T(8,128)(2,1)S(1)} %add_convert_fusion.2), channel_id=1, source_target_pairs={{0,24},{1,25},{2,26},{3,27},{4,28},{5,29},{6,30},{7,31},{8,16},{9,... | collective-permute-start | bytes 516104 | tf_op jit(solution)/shard_map/ppermute | solution.py:21
  69.5 5.5 %collective-permute-start.18 = (bf16[24,3584]{1,0:T(8,128)(2,1)S(1)}, bf16[24,3584]{1,0:T(8,128)(2,1)S(1)}, u32[]{:S(2)}, u32[]{:S(2)}) collective-permute-start(bf16[24,3584]{1,0:T(8,128)(2,1)S(1)} %add_convert_fusion.1), channel_id=1, source_target_pairs={{0,2},{1,5},{2,0},{3,7},{4,6},{5,1},{6,4},{7,3},{8,10},{9,13},{10,... | collective-permute-start | bytes 516104 | tf_op jit(solution)/shard_map/ppermute | solution.py:21
  69.7 7.2 %collective-permute-start.14 = (bf16[24,3584]{1,0:T(8,128)(2,1)S(1)}, bf16[24,3584]{1,0:T(8,128)(2,1)S(1)}, u32[]{:S(2)}, u32[]{:S(2)}) collective-permute-start(bf16[24,3584]{1,0:T(8,128)(2,1)S(1)} %add_convert_fusion.5), channel_id=1, source_target_pairs={{0,2},{1,5},{2,0},{3,7},{4,6},{5,1},{6,4},{7,3},{8,10},{9,13},{10,... | collective-permute-start | bytes 516104 | tf_op jit(solution)/shard_map/ppermute | solution.py:21
  75.1 5.5 %collective-permute-start.19 = (bf16[24,3584]{1,0:T(8,128)(2,1)S(1)}, bf16[24,3584]{1,0:T(8,128)(2,1)S(1)}, u32[]{:S(2)}, u32[]{:S(2)}) collective-permute-start(bf16[24,3584]{1,0:T(8,128)(2,1)S(1)} %add_convert_fusion), channel_id=1, source_target_pairs={{0,8},{1,9},{2,10},{3,11},{4,12},{5,13},{6,14},{7,15},{8,0},{9,1},... | collective-permute-start | bytes 516104 | tf_op jit(solution)/shard_map/ppermute | solution.py:21
  (5 other events, 138.8 us)

commit v4 on v3

--- a/solution.py
+++ b/solution.py
@@ -39,7 +39,7 @@
 
 def route_kernel(experts, capacity, me_ref, expert_hbm, token_hbm, gate_hbm, tok_hbm, *refs):
     bufs, (hi_ref, lo_ref) = refs[:experts], refs[experts : experts + 2]
-    expert_ref, token_ref, gate_ref, tok_ref, out_ref, sems, out_sems = refs[experts + 2 :]
+    expert_ref, token_ref, gate_ref, tok_ref, sems = refs[experts + 2 :]
     rows = expert_ref.shape[1]
     tok_count, width = tok_ref.shape
     places = experts * capacity
@@ -82,17 +82,12 @@
     pick = lax.dot_general(
         place_hot, token_hot.astype(jnp.bfloat16), contract, preferred_element_type=jnp.float32
     ).astype(jnp.bfloat16)
-    stores = []
     for k in range(tiles):
         cols = pl.ds(k * tile, tile)
         large[k].wait()
         picked = jnp.dot(pick, tok_ref[:, cols], preferred_element_type=jnp.float32)
         for s in range(experts):
-            out_ref[s, :, cols] = picked[s * capacity : (s + 1) * capacity].astype(jnp.bfloat16)
-    for s in range(experts):
-        copy = pltpu.make_async_copy(out_ref.at[s], bufs[s], out_sems.at[s])
-        copy.start()
-        stores.append(copy)
+            bufs[s][:, cols] = picked[s * capacity : (s + 1) * capacity].astype(jnp.bfloat16)
     gate = gate_ref[...]
     gate_hi = gate.astype(jnp.bfloat16).astype(jnp.float32)
     for part, ref in ((gate_hi, hi_ref), (gate - gate_hi, lo_ref)):
@@ -102,8 +97,6 @@
             contract,
             preferred_element_type=jnp.float32,
         ).astype(jnp.bfloat16)
-    for copy in stores:
-        copy.wait()
 
 
 def run_route(experts, capacity, me, route_expert, route_token, route_gate, tokens):
@@ -115,15 +108,13 @@
         functools.partial(route_kernel, experts, capacity),
         out_shape=[block] * experts + [mix] * 2,
         in_specs=[SMEM] + [ANY] * 4,
-        out_specs=[ANY] * experts + [VMEM] * 2,
+        out_specs=[VMEM] * (experts + 2),
         scratch_shapes=[
             pltpu.VMEM((1, rows), jnp.int32),
             pltpu.VMEM((1, rows), jnp.int32),
             pltpu.VMEM((1, rows), jnp.float32),
             pltpu.VMEM((tok_count, width), jnp.bfloat16),
-            pltpu.VMEM((experts, capacity, width), jnp.bfloat16),
             pltpu.SemaphoreType.DMA((3 + width // column_tile(width),)),
-            pltpu.SemaphoreType.DMA((experts,)),
         ],
         compiler_params=pltpu.CompilerParams(vmem_limit_bytes=60 * MIB),
     )(
@@ -135,10 +126,11 @@
     )
 
 
-def expert_kernel(chunks, backs, me_ref, *refs):
+def expert_kernel(chunks, backs, ahead, final, me_ref, *refs):
     count = 2 * len(chunks)
     pieces, (win_a, win_b, wout_a, wout_b) = refs[:count], refs[count : count + 4]
-    outs, hids = refs[count + 4 : count + 4 + 2 * len(backs)], refs[count + 4 + 2 * len(backs) : -2]
+    held, refs = refs[count + 4 : count + 4 + 2 * len(ahead)], refs[count + 4 + 2 * len(ahead) :]
+    outs, hids = refs[: 2 * len(backs)], refs[2 * len(backs) : -2]
     rows_ref, hidden_ref = refs[-2:]
     units, width = wout_a.shape
     capacity = hids[0].shape[1]
@@ -153,6 +145,14 @@
     cross_mask = (SECOND - core * (SECOND - FIRST)) // 2
     masks = (0, lane_mask, cross_mask, lane_mask ^ cross_mask)
     blocks = [(s, k) for chunk in chunks for k in range(4) for s in chunk]
+
+    def spot(s, k):
+        return (layer ^ s) * CHIPS + (chip ^ masks[k])
+
+    for e, earlier in enumerate(ahead):
+        for half in (0, 1):
+            for i, (s, k) in enumerate(earlier):
+                hids[half][spot(s, k)] = held[2 * e + half][i]
     for half, (win, hid) in enumerate(zip((win_a, win_b), hids)):
         total = jnp.dot(rows_ref[...], win[...], preferred_element_type=jnp.float32)
         gate, up = total[:, :units], total[:, units:]
@@ -160,7 +160,7 @@
         hidden_ref[:, units * half : units * (half + 1)] = value
         value = value.astype(jnp.float32)
         for i, (s, k) in enumerate(blocks):
-            hid[(layer ^ s) * CHIPS + (chip ^ masks[k])] = value[
+            hid[spot(s, k) if final else i] = value[
                 i * capacity : (i + 1) * capacity
             ].astype(jnp.bfloat16)
     for at in range(0, width, tile):
@@ -176,20 +176,21 @@
             ref[:, cols] = jnp.concatenate(parts, axis=0).astype(jnp.bfloat16)
 
 
-def run_expert(chunks, backs, capacity, me, pieces, weights):
+def run_expert(chunks, backs, ahead, held, capacity, final, me, pieces, weights):
     width = pieces[0].shape[1]
     units = weights[2].shape[0]
     rows = sum(piece.shape[0] for piece in pieces)
-    hid = jax.ShapeDtypeStruct((rows // capacity, capacity, units), jnp.bfloat16)
+    places = rows // capacity + (sum(len(earlier) for earlier in ahead) if final else 0)
+    hid = jax.ShapeDtypeStruct((places, capacity, units), jnp.bfloat16)
     outs = [
         jax.ShapeDtypeStruct((2 * len(back) * capacity, width), jnp.bfloat16)
         for back in backs
         for _ in (0, 1)
     ]
     return pl.pallas_call(
-        functools.partial(expert_kernel, chunks, backs),
+        functools.partial(expert_kernel, chunks, backs, ahead, final),
         out_shape=outs + [hid] * 2,
-        in_specs=[SMEM] + [VMEM] * (len(pieces) + 4),
+        in_specs=[SMEM] + [VMEM] * (len(pieces) + 4 + len(held)),
         out_specs=[VMEM] * (len(outs) + 2),
         scratch_shapes=[
             pltpu.VMEM((rows, width), jnp.bfloat16),
@@ -197,7 +198,7 @@
         ],
         compiler_params=pltpu.CompilerParams(vmem_limit_bytes=16 * MIB),
         cost_estimate=pl.CostEstimate(flops=1, bytes_accessed=1, transcendentals=0),
-    )(me, *pieces, *weights)
+    )(me, *pieces, *weights, *held)
 
 
 def weave_kernel(me_ref, mine_ref, other_ref, out_ref):
@@ -217,6 +218,33 @@
     total = jnp.dot(hi_ref[...], rows, preferred_element_type=jnp.float32)
     total += jnp.dot(lo_ref[...], rows, preferred_element_type=jnp.float32)
     refs[-1][...] = total.astype(jnp.bfloat16)
+
+
+GATHER = [[0], [1, 3], [2]]
+BACKS = [[3], [2], [1], [0]]
+GROUPS = [[0, 1], [2]]
+PLAN = (
+    ("Z", 3, 3), ("L", 0, 0), ("Z", 1, 3), ("W", 1, 1), ("z", 1, 0), ("l", 0, 0), ("z", 3, 3),
+    ("X", 0, 0), ("W", 0, 3), ("Z", 2, 3), ("L", 1, 3), ("l", 1, 2), ("X", 1, 2), ("w", 0, 1),
+    ("z", 2, 3), ("L", 2, 0), ("w", 1, 2), ("x", 0, 1), ("l", 2, 3), ("X", 2, 1), ("x", 1, 0),
+    ("K", 0, 0), ("x", 2, 0), ("K", 1, 0), ("C", 1, 0), ("C", 0, 0), ("H", 0, 1), ("h", 0, 0),
+    ("C", 2, 0), ("F", 0, 1), ("c", 1, 2), ("c", 0, 0), ("C", 3, 1), ("A", 0, 2), ("a", 0, 3),
+    ("A", 1, 0), ("c", 2, 0), ("a", 1, 1), ("B", 2, 0), ("c", 3, 2), ("A", 2, 0), ("a", 2, 2),
+    ("A", 3, 0), ("f", 0, 2), ("b", 2, 1), ("B", 3, 0), ("B", 1, 0), ("b", 3, 2), ("a", 3, 1),
+    ("b", 1, 1),
+)
+
+
+def plain_plan(experts):
+    steps = [("W", 0), ("W", 1)] + [("Z", s) for s in range(1, experts)] + [("w", 0), ("w", 1)]
+    steps += [("z", s) for s in range(1, experts)]
+    for s in range(experts):
+        steps += [("L", s), ("l", s), ("X", s), ("x", s)]
+    steps += [("K", 0), ("H", 0), ("h", 0), ("F", 0), ("f", 0)]
+    for s in range(experts):
+        steps += [("C", s), ("c", s), ("A", s), ("a", s)]
+    steps += [("B", s) for s in range(1, experts)] + [("b", s) for s in range(1, experts)]
+    return [(kind, at, 0) for kind, at in steps]
 
 
 def shards(tokens, route_token, route_expert, route_gate, w_in, w_out, swap_pairs):
@@ -230,67 +258,106 @@
     places = experts * capacity
     me = lax.axis_index("ep").astype(jnp.int32).reshape(1)
     small = pltpu.CompilerParams(vmem_limit_bytes=16 * MIB)
-
-    weights = [
-        w_in[0],
-        swap(w_in[0], lambda i: CORE),
-        w_out[0],
-        swap(w_out[0], lambda i: CORE),
-    ]
+    tuned = experts == 1 + max(max(chunk) for chunk in GATHER)
+    singles = [[s] for s in range(experts)]
+    chunks, backs, groups = (GATHER, BACKS, GROUPS) if tuned else (singles, singles, [list(range(experts))])
+    plan = PLAN if tuned else plain_plan(experts)
+
     *bufs, gate_hi, gate_lo = run_route(
         experts, capacity, me, route_expert, route_token, route_gate, tokens
     )
-
-    chunks = [[0], [1, experts - 1]] + [[s] for s in range(2, experts - 1)]
-    backs = [[s] for s in reversed(range(experts))]
-    received = {0: bufs[0]}
-    gathered = {}
-    ready = list(bufs)
-    for c, chunk in enumerate(chunks):
-        for s in chunk:
-            if s:
-                received[s] = swap(ready[s], lambda i: SLICES * s)
-        if c == 1:
-            kept = [received[s] for s in chunk]
-            kept = after(kept, gathered[0][0])
-            ready, kept = lax.optimization_barrier((ready, kept))
-            for s, value in zip(chunk, kept):
-                received[s] = value
-        if c > 1:
-            kept = after([received[s] for s in chunk], gathered[c - 1][0])
-            received.update(zip(chunk, kept))
-        mine = jnp.concatenate([received[s] for s in chunk], axis=0)
-        beside = swap(mine, lane)
-        both = jnp.concatenate([mine, beside], axis=0)
-        gathered[c] = [both, swap(both, cross)]
-
-    *outs, hid_a, hid_b = run_expert(
-        chunks, backs, capacity, me, sum([gathered[c] for c in range(len(chunks))], []), weights
-    )
-
-    finals = [None] * experts
-    lasts, got, totals = [], [], []
-    for b, back in enumerate(backs):
-        near, away = outs[2 * b : 2 * b + 2]
-        half = near.shape[0] // 2
-        if b > 1:
-            away = after(away, got[b - 2])
-        came = swap(away, cross)
-        if b > 1:
-            came = after(came, totals[b - 2 : b - 1])
-        got.append(came)
-        relay = near[half:].astype(jnp.float32) + came[half:].astype(jnp.float32)
-        last = swap(relay.astype(jnp.bfloat16), lane)
-        lasts.append(last)
-        part = []
-        for i, s in enumerate(back):
-            rows = slice(i * capacity, (i + 1) * capacity)
-            total = sum(v[rows].astype(jnp.float32) for v in (near, came, last))
-            total = total.astype(jnp.bfloat16)
-            part.append(total)
-            finals[s] = total if s == 0 else swap(total, lambda i: SLICES * s)
-        totals.append(part)
-
+    both_weights = [w_in[0], w_out[0]]
+    flying, came, both = {}, {("z", 0): bufs[0]}, {}
+    near, away, sums, held, ahead = {}, {}, {}, [], []
+    token = me
+
+    def send(key, value, mask_of, mark):
+        nonlocal token
+        if mark == 3:
+            token, value = lax.optimization_barrier((token, value))
+        elif mark == 2:
+            token = after(token, value)
+        elif mark == 1:
+            value = after(value, token)
+        flying[key] = swap(value, mask_of)
+
+    for kind, s, mark in plan:
+        if kind == "W":
+            send(("w", s), both_weights[s], lambda i: CORE, mark)
+        elif kind == "Z":
+            send(("z", s), bufs[s], lambda i: SLICES * s, mark)
+        elif kind == "L":
+            both[s] = [came["z", e] for e in chunks[s]]
+            mine = jnp.concatenate(both[s], axis=0) if len(both[s]) > 1 else both[s][0]
+            send(("l", s), mine, lane, mark)
+        elif kind == "X":
+            both[s] = jnp.concatenate(both[s] + [came["l", s]], axis=0)
+            send(("x", s), both[s], cross, mark)
+        elif kind == "K":
+            group = groups[s]
+            pieces = sum([[both[c], came["x", c]] for c in group], [])
+            weights = [w_in[0], came["w", 0], w_out[0], came["w", 1]]
+            inside = [e for c in group for e in chunks[c]]
+            mine = [i for i, back in enumerate(backs) if back[0] in inside]
+            final = s == len(groups) - 1
+            *outs, hid_a, hid_b = run_expert(
+                [chunks[c] for c in group],
+                [backs[i] for i in mine],
+                ahead if final else [],
+                held if final else [],
+                capacity,
+                final,
+                me,
+                pieces,
+                weights,
+            )
+            held = held + [hid_a, hid_b]
+            ahead = ahead + [[(e, k) for c in group for k in range(4) for e in chunks[c]]]
+            for i, index in enumerate(mine):
+                near[index], away[index] = outs[2 * i : 2 * i + 2]
+        elif kind == "C":
+            send(("c", s), away[s], cross, mark)
+        elif kind == "A":
+            half = near[s].shape[0] // 2
+            relay = near[s][half:].astype(jnp.float32) + came["c", s][half:].astype(jnp.float32)
+            send(("a", s), relay.astype(jnp.bfloat16), lane, mark)
+        elif kind == "B":
+            send(("b", s), sums[s], lambda i: SLICES * s, mark)
+        elif kind == "H":
+            send(("h", 0), hid_b, lambda i: CORE, mark)
+        elif kind == "F":
+            full = pl.pallas_call(
+                weave_kernel,
+                out_shape=jax.ShapeDtypeStruct((devices // 2, 2, capacity, units), jnp.bfloat16),
+                in_specs=[SMEM, VMEM, VMEM],
+                out_specs=VMEM,
+                compiler_params=small,
+            )(me, hid_a, came["h", 0])
+            send(("f", 0), full, lambda i: half_axis, mark)
+        else:
+            value = flying[kind, s]
+            if mark == 3:
+                token, value = lax.optimization_barrier((token, value))
+            elif mark == 2:
+                token = after(token, value)
+            elif mark == 1:
+                value = after(value, token)
+            came[kind, s] = value
+            if kind == "a":
+                parts = (near[s], came["c", s], came["a", s])
+                for i, e in enumerate(backs[s]):
+                    rows = slice(i * capacity, (i + 1) * capacity)
+                    total = sum(part[rows].astype(jnp.float32) for part in parts)
+                    sums[e] = total.astype(jnp.bfloat16)
+
+    saved = pl.pallas_call(
+        keep_kernel,
+        out_shape=jax.ShapeDtypeStruct(full.shape, full.dtype),
+        in_specs=[SMEM, SMEM, VMEM, VMEM],
+        out_specs=pl.BlockSpec(),
+        compiler_params=small,
+    )(me, swap_pairs, full, came["f", 0])
+    finals = after([sums[0]] + [came["b", s] for s in range(1, experts)], token)
     tile = column_tile(width)
     moving = lambda rows: pl.BlockSpec((rows, tile), lambda i: (0, i))
     fixed = pl.BlockSpec((tok_count, places), lambda i: (0, 0))
@@ -302,23 +369,6 @@
         out_specs=moving(tok_count),
         compiler_params=small,
     )(gate_hi, gate_lo, *finals)
-
-    other = swap(hid_b, lambda i: CORE)
-    full = pl.pallas_call(
-        weave_kernel,
-        out_shape=jax.ShapeDtypeStruct((devices // 2, 2, capacity, units), jnp.bfloat16),
-        in_specs=[SMEM, VMEM, VMEM],
-        out_specs=VMEM,
-        compiler_params=small,
-    )(me, hid_a, other)
-    far = after(swap(full, lambda i: half_axis), lasts[:2])
-    saved = pl.pallas_call(
-        keep_kernel,
-        out_shape=jax.ShapeDtypeStruct(full.shape, full.dtype),
-        in_specs=[SMEM, SMEM, VMEM, VMEM],
-        out_specs=pl.BlockSpec(),
-        compiler_params=small,
-    )(me, swap_pairs, full, far)
     return (mixed, saved.reshape(1, devices * capacity, units))
 
 

time: 82.4 us -> 78.1 us (0.948)
  starting transfers between devices: 31.7 us -> 24 us
  waiting for transfers between devices: 38.9 us -> 42.4 us
    ppermute x24, starting transfers between devices: 31.7 us -> 24 us  [swap(): lax.ppermute(value, 'ep', [(i, i ^ mask_of(i)) for i in range(count)])]
    ppermute x24, waiting for transfers between devices: 38.9 us -> 42.4 us  [swap(): lax.ppermute(value, 'ep', [(i, i ^ mask_of(i)) for i in range(count)])]
    pallas_call x1 -> x2, Pallas kernels: 3.12 us -> 3.65 us  [run_expert(): pl.pallas_call(functools.partial(expert_kernel, chunks, backs, ahead, fin...]
  transfers between devices with their start and end apart: 24 -> 24, of which waited for: 12 -> 15; matrix products, arithmetic and copies ran while one was open for 2% -> 2% of each run, Pallas kernels for 2% -> 6%
where the time goes in v4:
time: 78.1 us; the launch traced here: 77.9 us
  waiting for transfers between devices  42.4 us (54%)
  starting transfers between devices  24 us (31%)
  Pallas kernels  9.2 us (12%)
  local copies, waits for them, and re-layouts  1.05 us (1%)
  between operations  0.85 us (1%)
    ppermute x24, waiting for transfers between devices, swap(): lax.ppermute(value, 'ep', [(i, i ^ mask_of(i)) for i in range(count)])  42.4 us
    ppermute x24, starting transfers between devices, swap(): lax.ppermute(value, 'ep', [(i, i ^ mask_of(i)) for i in range(count)])  24 us
    pallas_call x2, Pallas kernels, run_expert(): pl.pallas_call(functools.partial(expert_kernel, chunks, backs, ahead, fin...  3.65 us
    pallas_call x1, Pallas kernels, run_route(): pl.pallas_call(functools.partial(route_kernel, experts, capacity), out_sh...  2.59 us
    pallas_call x1, Pallas kernels, shards(): pl.pallas_call(mix_kernel, out_shape=jax.ShapeDtypeStruct((tok_count, wid...  1.65 us
  transfers between devices with their start and end apart: 24, of which 15 were waited for; matrix products, arithmetic and copies ran while one was open for 2% of the time, Pallas kernels for 6%

profile of v4, /device:TPU:0, one launch (start us, length us, event | category | flops | bytes accessed | tf_op | source)
XLA Modules:
  0.0 77.9 jit_solution(8725295250003664808)
XLA Ops:
  0.6 2.6 %shard_map.86 = (bf16[24,3584]{1,0:T(8,128)(2,1)}, bf16[24,3584]{1,0:T(8,128)(2,1)}, bf16[24,3584]{1,0:T(8,128)(2,1)}, bf16[24,3584]{1,0:T(8,128)(2,1)}, bf16[12...) custom-call(s32[1]{0:T(128)} %bitcast.me_ref, s32[1,64]{1,0:T(1,128)} %bitcast.14, s32[1,64]{1,0:T(1,128)} %bitcast.15, ...), custom_call_target="tpu_custom_call" | custom-call | tf_op jit(solution)/shard_map/pallas_call | solution.py:107
  3.3 3.0 %collective-permute-start = (bf16[24,3584]{1,0:T(8,128)(2,1)}, bf16[24,3584]{1,0:T(8,128)(2,1)S(1)}, u32[]{:S(2)}, u32[]{:S(2)}) collective-permute-start(bf16[24,3584]{1,0:T(8,128)(2,1)} %get-tuple-element.64), channel_id=1, source_target_pairs={{0,2},{1,5},{2,0},{3,7},{4,6},{5,1},{6,4},{7,3},{8,10},{9,13},{10,... | collective-permute-start | bytes 516104 | tf_op jit(solution)/shard_map/ppermute | solution.py:21
  6.3 3.6 %collective-permute-start.2 = (bf16[24,3584]{1,0:T(8,128)(2,1)}, bf16[24,3584]{1,0:T(8,128)(2,1)S(1)}, u32[]{:S(2)}, u32[]{:S(2)}) collective-permute-start(bf16[24,3584]{1,0:T(8,128)(2,1)} %get-tuple-element.69), channel_id=1, source_target_pairs={{0,24},{1,25},{2,26},{3,27},{4,28},{5,29},{6,30},{7,31},{8,16},{9,... | collective-permute-start | bytes 516104 | tf_op jit(solution)/shard_map/ppermute | solution.py:21
  10.8 1.6 %collective-permute-start.1 = (bf16[48,3584]{1,0:T(8,128)(2,1)S(1)}, bf16[48,3584]{1,0:T(8,128)(2,1)S(1)}, u32[]{:S(2)}, u32[]{:S(2)}) collective-permute-start(bf16[48,3584]{1,0:T(8,128)(2,1)S(1)} %constant_dynamic-update-slice_fusion.refs_0_), channel_id=1, source_target_pairs={{0,4},{1,3},{2,6},{3,1},{4,0},{5,7},{6,2},{7,5},{8,12},{9,11},{10,... | collective-permute-start | bytes 1032200 | tf_op jit(solution)/shard_map/ppermute | solution.py:21
  12.4 3.1 %collective-permute-done.2 = bf16[24,3584]{1,0:T(8,128)(2,1)S(1)} collective-permute-done((bf16[24,3584]{1,0:T(8,128)(2,1)}, bf16[24,3584]{1,0:T(8,128)(2,1)S(1)}, u32[]{:S(2)}, u32[]{:S(2)}) %collective-permute-start.2) | collective-permute-done | bytes 172064 | tf_op jit(solution)/shard_map/ppermute | solution.py:21
  15.6 2.4 %collective-permute-done.3 = bf16[24,3584]{1,0:T(8,128)(2,1)S(1)} collective-permute-done((bf16[24,3584]{1,0:T(8,128)(2,1)}, bf16[24,3584]{1,0:T(8,128)(2,1)S(1)}, u32[]{:S(2)}, u32[]{:S(2)}) %collective-permute-start.3) | collective-permute-done | bytes 172064 | tf_op jit(solution)/shard_map/ppermute | solution.py:21
  18.0 1.6 %collective-permute-start.4 = (bf16[48,3584]{1,0:T(8,128)(2,1)S(1)}, bf16[48,3584]{1,0:T(8,128)(2,1)S(1)}, u32[]{:S(2)}, u32[]{:S(2)}) collective-permute-start(bf16[48,3584]{1,0:T(8,128)(2,1)S(1)} %pad_maximum_fusion), channel_id=1, source_target_pairs={{0,2},{1,5},{2,0},{3,7},{4,6},{5,1},{6,4},{7,3},{8,10},{9,13},{10,... | collective-permute-start | bytes 1032200 | tf_op jit(solution)/shard_map/ppermute | solution.py:21
  20.3 5.0 %collective-permute-done.4 = bf16[48,3584]{1,0:T(8,128)(2,1)S(1)} collective-permute-done((bf16[48,3584]{1,0:T(8,128)(2,1)S(1)}, bf16[48,3584]{1,0:T(8,128)(2,1)S(1)}, u32[]{:S(2)}, u32[]{:S(2)}) %collective-permute-start.4) | collective-permute-done | bytes 344096 | tf_op jit(solution)/shard_map/ppermute | solution.py:21
  25.9 5.1 %collective-permute-done.5 = bf16[24,3584]{1,0:T(8,128)(2,1)S(1)} collective-permute-done((bf16[24,3584]{1,0:T(8,128)(2,1)S(1)}, bf16[24,3584]{1,0:T(8,128)(2,1)S(1)}, u32[]{:S(2)}, u32[]{:S(2)}) %collective-permute-start.5) | collective-permute-done | bytes 172064 | tf_op jit(solution)/shard_map/ppermute | solution.py:21
  31.6 4.8 %collective-permute-done.9 = bf16[24,3584]{1,0:T(8,128)(2,1)S(1)} collective-permute-done((bf16[24,3584]{1,0:T(8,128)(2,1)S(1)}, bf16[24,3584]{1,0:T(8,128)(2,1)S(1)}, u32[]{:S(2)}, u32[]{:S(2)}) %collective-permute-start.9) | collective-permute-done | bytes 172064 | tf_op jit(solution)/shard_map/ppermute | solution.py:21
  38.2 2.4 %shard_map.87 = (bf16[48,3584]{1,0:T(8,128)(2,1)S(1)}, bf16[48,3584]{1,0:T(8,128)(2,1)S(1)}, bf16[48,3584]{1,0:T(8,128)(2,1)S(1)}, bf16[48,3584]{1,0:T(8,128)(2,...) custom-call(s32[1]{0:T(128)} %bitcast.me_ref, ...), custom_call_target="tpu_custom_call" | custom-call | flops 1 | bytes 1 | tf_op jit(solution)/shard_map/pallas_call | solution.py:190
  41.2 2.6 %collective-permute-done.10.refs_1_ = bf16[48,3584]{1,0:T(8,128)(2,1)S(1)} collective-permute-done((bf16[48,3584]{1,0:T(8,128)(2,1)S(1)}, bf16[48,3584]{1,0:T(8,128)(2,1)S(1)}, u32[]{:S(2)}, u32[]{:S(2)}) %collective-permute-start.10) | collective-permute-done | bytes 344096 | tf_op jit(solution)/shard_map/ppermute | solution.py:21
  45.7 1.5 %collective-permute-start.16 = (bf16[48,3584]{1,0:T(8,128)(2,1)S(1)}, bf16[48,3584]{1,0:T(8,128)(2,1)S(1)}, u32[]{:S(2)}, u32[]{:S(2)}) collective-permute-start(bf16[48,3584]{1,0:T(8,128)(2,1)S(1)} %get-tuple-element.104), channel_id=1, source_target_pairs={{0,4},{1,3},{2,6},{3,1},{4,0},{5,7},{6,2},{7,5},{8,12},{9,11},{10,... | collective-permute-start | bytes 1032200 | tf_op jit(solution)/shard_map/ppermute | solution.py:21
  48.0 4.4 %collective-permute-done.11 = bf16[48,3584]{1,0:T(8,128)(2,1)S(1)} collective-permute-done((bf16[48,3584]{1,0:T(8,128)(2,1)S(1)}, bf16[48,3584]{1,0:T(8,128)(2,1)S(1)}, u32[]{:S(2)}, u32[]{:S(2)}) %collective-permute-start.11) | collective-permute-done | bytes 344096 | tf_op jit(solution)/shard_map/ppermute | solution.py:21
  52.4 1.4 %collective-permute-start.15 = (bf16[24,3584]{1,0:T(8,128)(2,1)S(1)}, bf16[24,3584]{1,0:T(8,128)(2,1)S(1)}, u32[]{:S(2)}, u32[]{:S(2)}) collective-permute-start(bf16[24,3584]{1,0:T(8,128)(2,1)S(1)} %add_convert_fusion.6), channel_id=1, source_target_pairs={{0,2},{1,5},{2,0},{3,7},{4,6},{5,1},{6,4},{7,3},{8,10},{9,13},{10,... | collective-permute-start | bytes 516104 | tf_op jit(solution)/shard_map/ppermute | solution.py:21
  54.2 3.4 %collective-permute-done.16 = bf16[48,3584]{1,0:T(8,128)(2,1)S(1)} collective-permute-done((bf16[48,3584]{1,0:T(8,128)(2,1)S(1)}, bf16[48,3584]{1,0:T(8,128)(2,1)S(1)}, u32[]{:S(2)}, u32[]{:S(2)}) %collective-permute-start.16) | collective-permute-done | bytes 344096 | tf_op jit(solution)/shard_map/ppermute | solution.py:21
  57.6 1.5 %collective-permute-start.17 = (bf16[24,3584]{1,0:T(8,128)(2,1)S(1)}, bf16[24,3584]{1,0:T(8,128)(2,1)S(1)}, u32[]{:S(2)}, u32[]{:S(2)}) collective-permute-start(bf16[24,3584]{1,0:T(8,128)(2,1)S(1)} %add_convert_fusion.5), channel_id=1, source_target_pairs={{0,2},{1,5},{2,0},{3,7},{4,6},{5,1},{6,4},{7,3},{8,10},{9,13},{10,... | collective-permute-start | bytes 516104 | tf_op jit(solution)/shard_map/ppermute | solution.py:21
  59.9 1.6 %collective-permute-start.20 = (bf16[24,3584]{1,0:T(8,128)(2,1)S(1)}, bf16[24,3584]{1,0:T(8,128)(2,1)S(1)}, u32[]{:S(2)}, u32[]{:S(2)}) collective-permute-start(bf16[24,3584]{1,0:T(8,128)(2,1)S(1)} %add_convert_fusion.4), channel_id=1, source_target_pairs={{0,24},{1,25},{2,26},{3,27},{4,28},{5,29},{6,30},{7,31},{8,16},{9,... | collective-permute-start | bytes 516104 | tf_op jit(solution)/shard_map/ppermute | solution.py:21
  61.6 1.5 %collective-permute-done.17 = bf16[24,3584]{1,0:T(8,128)(2,1)S(1)} collective-permute-done((bf16[24,3584]{1,0:T(8,128)(2,1)S(1)}, bf16[24,3584]{1,0:T(8,128)(2,1)S(1)}, u32[]{:S(2)}, u32[]{:S(2)}) %collective-permute-start.17) | collective-permute-done | bytes 172064 | tf_op jit(solution)/shard_map/ppermute | solution.py:21
  63.2 1.4 %collective-permute-start.21 = (bf16[24,3584]{1,0:T(8,128)(2,1)S(1)}, bf16[24,3584]{1,0:T(8,128)(2,1)S(1)}, u32[]{:S(2)}, u32[]{:S(2)}) collective-permute-start(bf16[24,3584]{1,0:T(8,128)(2,1)S(1)} %add_convert_fusion.2), channel_id=1, source_target_pairs={{0,8},{1,9},{2,10},{3,11},{4,12},{5,13},{6,14},{7,15},{8,0},{9,1},... | collective-permute-start | bytes 516104 | tf_op jit(solution)/shard_map/ppermute | solution.py:21
  65.6 1.5 %collective-permute-start.13 = (bf16[24,3584]{1,0:T(8,128)(2,1)S(1)}, bf16[24,3584]{1,0:T(8,128)(2,1)S(1)}, u32[]{:S(2)}, u32[]{:S(2)}) collective-permute-start(bf16[24,3584]{1,0:T(8,128)(2,1)S(1)} %add_convert_fusion.7), channel_id=1, source_target_pairs={{0,2},{1,5},{2,0},{3,7},{4,6},{5,1},{6,4},{7,3},{8,10},{9,13},{10,... | collective-permute-start | bytes 516104 | tf_op jit(solution)/shard_map/ppermute | solution.py:21
  68.7 3.6 %collective-permute-done.21.refs_1_ = bf16[24,3584]{1,0:T(8,128)(2,1)S(1)} collective-permute-done((bf16[24,3584]{1,0:T(8,128)(2,1)S(1)}, bf16[24,3584]{1,0:T(8,128)(2,1)S(1)}, u32[]{:S(2)}, u32[]{:S(2)}) %collective-permute-start.21) | collective-permute-done | bytes 172064 | tf_op jit(solution)/shard_map/ppermute | solution.py:21
  72.3 3.9 %collective-permute-done.23.refs_2_ = bf16[24,3584]{1,0:T(8,128)(2,1)S(1)} collective-permute-done((bf16[24,3584]{1,0:T(8,128)(2,1)S(1)}, bf16[24,3584]{1,0:T(8,128)(2,1)S(1)}, u32[]{:S(2)}, u32[]{:S(2)}) %collective-permute-start.23) | collective-permute-done | bytes 172064 | tf_op jit(solution)/shard_map/ppermute | solution.py:21
  76.3 1.7 %shard_map.90 = bf16[128,3584]{1,0:T(8,128)(2,1)} custom-call(bf16[128,96]{1,0:T(8,128)(2,1)S(1)} %copy-done.2, bf16[128,96]{1,0:T(8,128)(2,1)S(1)} %copy-done.3, bf16[24,3584]{1,0:T(8,128)(2,1)S(1)} %add_convert_fusion.3.refs_0_, bf16[24,3584]{1,0:T(8,128)(2,1)S(1)} %collective-permute-done.21.refs_1_, ...), custom_call_target="tpu_custom_call" | custom-call | tf_op jit(solution)/shard_map/pallas_call | solution.py:364
  (58 shorter events, 11.6 us)
Async XLA Ops:
  3.3 7.6 %collective-permute-start = (bf16[24,3584]{1,0:T(8,128)(2,1)}, bf16[24,3584]{1,0:T(8,128)(2,1)S(1)}, u32[]{:S(2)}, u32[]{:S(2)}) collective-permute-start(bf16[24,3584]{1,0:T(8,128)(2,1)} %get-tuple-element.64), channel_id=1, source_target_pairs={{0,2},{1,5},{2,0},{3,7},{4,6},{5,1},{6,4},{7,3},{8,10},{9,13},{10,... | collective-permute-start | bytes 516104 | tf_op jit(solution)/shard_map/ppermute | solution.py:21
  6.3 9.3 %collective-permute-start.2 = (bf16[24,3584]{1,0:T(8,128)(2,1)}, bf16[24,3584]{1,0:T(8,128)(2,1)S(1)}, u32[]{:S(2)}, u32[]{:S(2)}) collective-permute-start(bf16[24,3584]{1,0:T(8,128)(2,1)} %get-tuple-element.69), channel_id=1, source_target_pairs={{0,24},{1,25},{2,26},{3,27},{4,28},{5,29},{6,30},{7,31},{8,16},{9,... | collective-permute-start | bytes 516104 | tf_op jit(solution)/shard_map/ppermute | solution.py:21
  9.9 8.1 %collective-permute-start.3 = (bf16[24,3584]{1,0:T(8,128)(2,1)}, bf16[24,3584]{1,0:T(8,128)(2,1)S(1)}, u32[]{:S(2)}, u32[]{:S(2)}) collective-permute-start(bf16[24,3584]{1,0:T(8,128)(2,1)} %get-tuple-element.74), channel_id=1, source_target_pairs={{0,8},{1,9},{2,10},{3,11},{4,12},{5,13},{6,14},{7,15},{8,0},{9,1},... | collective-permute-start | bytes 516104 | tf_op jit(solution)/shard_map/ppermute | solution.py:21
  9.9 21.7 %collective-permute-start.6 = (bf16[128,3584]{1,0:T(8,128)(2,1)}, bf16[128,3584]{1,0:T(8,128)(2,1)S(1)}, u32[]{:S(2)}, u32[]{:S(2)}) collective-permute-start(bf16[128,3584]{1,0:T(8,128)(2,1)} %bitcast.10), channel_id=1, source_target_pairs={{0,1},{1,0},{2,3},{3,2},{4,5},{5,4},{6,7},{7,6},{8,9},{9,8},{10,11... | collective-permute-start | bytes 2752520 | tf_op jit(solution)/shard_map/ppermute | solution.py:21
  10.8 26.2 %collective-permute-start.1 = (bf16[48,3584]{1,0:T(8,128)(2,1)S(1)}, bf16[48,3584]{1,0:T(8,128)(2,1)S(1)}, u32[]{:S(2)}, u32[]{:S(2)}) collective-permute-start(bf16[48,3584]{1,0:T(8,128)(2,1)S(1)} %constant_dynamic-update-slice_fusion.refs_0_), channel_id=1, source_target_pairs={{0,4},{1,3},{2,6},{3,1},{4,0},{5,7},{6,2},{7,5},{8,12},{9,11},{10,... | collective-permute-start | bytes 1032200 | tf_op jit(solution)/shard_map/ppermute | solution.py:21
  18.0 7.3 %collective-permute-start.4 = (bf16[48,3584]{1,0:T(8,128)(2,1)S(1)}, bf16[48,3584]{1,0:T(8,128)(2,1)S(1)}, u32[]{:S(2)}, u32[]{:S(2)}) collective-permute-start(bf16[48,3584]{1,0:T(8,128)(2,1)S(1)} %pad_maximum_fusion), channel_id=1, source_target_pairs={{0,2},{1,5},{2,0},{3,7},{4,6},{5,1},{6,4},{7,3},{8,10},{9,13},{10,... | collective-permute-start | bytes 1032200 | tf_op jit(solution)/shard_map/ppermute | solution.py:21
  19.6 17.5 %collective-permute-start.8 = (bf16[3584,256]{1,0:T(8,128)(2,1)S(1)}, bf16[3584,256]{1,0:T(8,128)(2,1)S(1)}, u32[]{:S(2)}, u32[]{:S(2)}) collective-permute-start(bf16[3584,256]{1,0:T(8,128)(2,1)S(1)} %bitcast.7), channel_id=1, source_target_pairs={{0,1},{1,0},{2,3},{3,2},{4,5},{5,4},{6,7},{7,6},{8,9},{9,8},{10,11... | collective-permute-start | bytes 5505032 | tf_op jit(solution)/shard_map/ppermute | solution.py:21
  19.6 11.4 %collective-permute-start.5 = (bf16[24,3584]{1,0:T(8,128)(2,1)S(1)}, bf16[24,3584]{1,0:T(8,128)(2,1)S(1)}, u32[]{:S(2)}, u32[]{:S(2)}) collective-permute-start(bf16[24,3584]{1,0:T(8,128)(2,1)S(1)} %copy-done.5), channel_id=1, source_target_pairs={{0,16},{1,17},{2,18},{3,19},{4,20},{5,21},{6,22},{7,23},{8,24},{9,... | collective-permute-start | bytes 516104 | tf_op jit(solution)/shard_map/ppermute | solution.py:21
  25.4 12.8 %collective-permute-start.7 = (bf16[96,3584]{1,0:T(8,128)(2,1)S(1)}, bf16[96,3584]{1,0:T(8,128)(2,1)S(1)}, u32[]{:S(2)}, u32[]{:S(2)}) collective-permute-start(bf16[96,3584]{1,0:T(8,128)(2,1)S(1)} %constant_dynamic-update-slice_fusion.2.refs_2_), channel_id=1, source_target_pairs={{0,4},{1,3},{2,6},{3,1},{4,0},{5,7},{6,2},{7,5},{8,12},{9,11},{10,... | collective-permute-start | bytes 2064392 | tf_op jit(solution)/shard_map/ppermute | solution.py:21
  31.1 5.4 %collective-permute-start.9 = (bf16[24,3584]{1,0:T(8,128)(2,1)S(1)}, bf16[24,3584]{1,0:T(8,128)(2,1)S(1)}, u32[]{:S(2)}, u32[]{:S(2)}) collective-permute-start(bf16[24,3584]{1,0:T(8,128)(2,1)S(1)} %collective-permute-done.5), channel_id=1, source_target_pairs={{0,2},{1,5},{2,0},{3,7},{4,6},{5,1},{6,4},{7,3},{8,10},{9,13},{10,... | collective-permute-start | bytes 516104 | tf_op jit(solution)/shard_map/ppermute | solution.py:21
  36.5 7.3 %collective-permute-start.10 = (bf16[48,3584]{1,0:T(8,128)(2,1)S(1)}, bf16[48,3584]{1,0:T(8,128)(2,1)S(1)}, u32[]{:S(2)}, u32[]{:S(2)}) collective-permute-start(bf16[48,3584]{1,0:T(8,128)(2,1)S(1)} %constant_dynamic-update-slice_fusion.5.refs_0_), channel_id=1, source_target_pairs={{0,4},{1,3},{2,6},{3,1},{4,0},{5,7},{6,2},{7,5},{8,12},{9,11},{10,... | collective-permute-start | bytes 1032200 | tf_op jit(solution)/shard_map/ppermute | solution.py:21
  40.6 7.3 %collective-permute-start.14 = (bf16[48,3584]{1,0:T(8,128)(2,1)S(1)}, bf16[48,3584]{1,0:T(8,128)(2,1)S(1)}, u32[]{:S(2)}, u32[]{:S(2)}) collective-permute-start(bf16[48,3584]{1,0:T(8,128)(2,1)S(1)} %get-tuple-element.99), channel_id=1, source_target_pairs={{0,4},{1,3},{2,6},{3,1},{4,0},{5,7},{6,2},{7,5},{8,12},{9,11},{10,... | collective-permute-start | bytes 1032200 | tf_op jit(solution)/shard_map/ppermute | solution.py:21
  45.0 2.2 %collective-permute-start.18 = (bf16[16,24,128]{2,1,0:T(8,128)(2,1)S(1)}, bf16[16,24,128]{2,1,0:T(8,128)(2,1)S(1)}, u32[]{:S(2)}, u32[]{:S(2)}) collective-permute-start(bf16[16,24,128]{2,1,0:T(8,128)(2,1)S(1)} %get-tuple-element.108), channel_id=1, source_target_pairs={{0,1},{1,0},{2,3},{3,2},{4,5},{5,4},{6,7},{7,6},{8,9},{9,8},{10,11... | collective-permute-start | bytes 294920 | tf_op jit(solution)/shard_map/ppermute | solution.py:21
  45.1 7.3 %collective-permute-start.11 = (bf16[48,3584]{1,0:T(8,128)(2,1)S(1)}, bf16[48,3584]{1,0:T(8,128)(2,1)S(1)}, u32[]{:S(2)}, u32[]{:S(2)}) collective-permute-start(bf16[48,3584]{1,0:T(8,128)(2,1)S(1)} %get-tuple-element.95), channel_id=1, source_target_pairs={{0,4},{1,3},{2,6},{3,1},{4,0},{5,7},{6,2},{7,5},{8,12},{9,11},{10,... | collective-permute-start | bytes 1032200 | tf_op jit(solution)/shard_map/ppermute | solution.py:21
  45.7 11.9 %collective-permute-start.16 = (bf16[48,3584]{1,0:T(8,128)(2,1)S(1)}, bf16[48,3584]{1,0:T(8,128)(2,1)S(1)}, u32[]{:S(2)}, u32[]{:S(2)}) collective-permute-start(bf16[48,3584]{1,0:T(8,128)(2,1)S(1)} %get-tuple-element.104), channel_id=1, source_target_pairs={{0,4},{1,3},{2,6},{3,1},{4,0},{5,7},{6,2},{7,5},{8,12},{9,11},{10,... | collective-permute-start | bytes 1032200 | tf_op jit(solution)/shard_map/ppermute | solution.py:21
  47.3 19.8 %collective-permute-start.19 = (bf16[16,2,24,128]{3,2,1,0:T(8,128)(2,1)S(1)}, bf16[16,2,24,128]{3,2,1,0:T(8,128)(2,1)S(1)}, u32[]{:S(2)}, u32[]{:S(2)}) collective-permute-start(bf16[16,2,24,128]{3,2,1,0:T(8,128)(2,1)S(1)} %shard_map.89.mine_ref), channel_id=1, source_target_pairs={{0,16},{1,17},{2,18},{3,19},{4,20},{5,21},{6,22},{7,23},{8,24},{9,... | collective-permute-start | bytes 589832 | tf_op jit(solution)/shard_map/ppermute | solution.py:21
  52.4 7.4 %collective-permute-start.15 = (bf16[24,3584]{1,0:T(8,128)(2,1)S(1)}, bf16[24,3584]{1,0:T(8,128)(2,1)S(1)}, u32[]{:S(2)}, u32[]{:S(2)}) collective-permute-start(bf16[24,3584]{1,0:T(8,128)(2,1)S(1)} %add_convert_fusion.6), channel_id=1, source_target_pairs={{0,2},{1,5},{2,0},{3,7},{4,6},{5,1},{6,4},{7,3},{8,10},{9,13},{10,... | collective-permute-start | bytes 516104 | tf_op jit(solution)/shard_map/ppermute | solution.py:21
  53.9 11.6 %collective-permute-start.12 = (bf16[48,3584]{1,0:T(8,128)(2,1)S(1)}, bf16[48,3584]{1,0:T(8,128)(2,1)S(1)}, u32[]{:S(2)}, u32[]{:S(2)}) collective-permute-start(bf16[48,3584]{1,0:T(8,128)(2,1)S(1)} %get-tuple-element.97), channel_id=1, source_target_pairs={{0,4},{1,3},{2,6},{3,1},{4,0},{5,7},{6,2},{7,5},{8,12},{9,11},{10,... | collective-permute-start | bytes 1032200 | tf_op jit(solution)/shard_map/ppermute | solution.py:21
  57.6 5.5 %collective-permute-start.17 = (bf16[24,3584]{1,0:T(8,128)(2,1)S(1)}, bf16[24,3584]{1,0:T(8,128)(2,1)S(1)}, u32[]{:S(2)}, u32[]{:S(2)}) collective-permute-start(bf16[24,3584]{1,0:T(8,128)(2,1)S(1)} %add_convert_fusion.5), channel_id=1, source_target_pairs={{0,2},{1,5},{2,0},{3,7},{4,6},{5,1},{6,4},{7,3},{8,10},{9,13},{10,... | collective-permute-start | bytes 516104 | tf_op jit(solution)/shard_map/ppermute | solution.py:21
  59.2 5.7 %collective-permute-start.22 = (bf16[24,3584]{1,0:T(8,128)(2,1)S(1)}, bf16[24,3584]{1,0:T(8,128)(2,1)S(1)}, u32[]{:S(2)}, u32[]{:S(2)}) collective-permute-start(bf16[24,3584]{1,0:T(8,128)(2,1)S(1)} %add_convert_fusion.1), channel_id=1, source_target_pairs={{0,2},{1,5},{2,0},{3,7},{4,6},{5,1},{6,4},{7,3},{8,10},{9,13},{10,... | collective-permute-start | bytes 516104 | tf_op jit(solution)/shard_map/ppermute | solution.py:21
  59.9 8.8 %collective-permute-start.20 = (bf16[24,3584]{1,0:T(8,128)(2,1)S(1)}, bf16[24,3584]{1,0:T(8,128)(2,1)S(1)}, u32[]{:S(2)}, u32[]{:S(2)}) collective-permute-start(bf16[24,3584]{1,0:T(8,128)(2,1)S(1)} %add_convert_fusion.4), channel_id=1, source_target_pairs={{0,24},{1,25},{2,26},{3,27},{4,28},{5,29},{6,30},{7,31},{8,16},{9,... | collective-permute-start | bytes 516104 | tf_op jit(solution)/shard_map/ppermute | solution.py:21
  63.2 9.1 %collective-permute-start.21 = (bf16[24,3584]{1,0:T(8,128)(2,1)S(1)}, bf16[24,3584]{1,0:T(8,128)(2,1)S(1)}, u32[]{:S(2)}, u32[]{:S(2)}) collective-permute-start(bf16[24,3584]{1,0:T(8,128)(2,1)S(1)} %add_convert_fusion.2), channel_id=1, source_target_pairs={{0,8},{1,9},{2,10},{3,11},{4,12},{5,13},{6,14},{7,15},{8,0},{9,1},... | collective-permute-start | bytes 516104 | tf_op jit(solution)/shard_map/ppermute | solution.py:21
  65.0 11.2 %collective-permute-start.23 = (bf16[24,3584]{1,0:T(8,128)(2,1)S(1)}, bf16[24,3584]{1,0:T(8,128)(2,1)S(1)}, u32[]{:S(2)}, u32[]{:S(2)}) collective-permute-start(bf16[24,3584]{1,0:T(8,128)(2,1)S(1)} %add_convert_fusion), channel_id=1, source_target_pairs={{0,16},{1,17},{2,18},{3,19},{4,20},{5,21},{6,22},{7,23},{8,24},{9,... | collective-permute-start | bytes 516104 | tf_op jit(solution)/shard_map/ppermute | solution.py:21
  65.6 10.6 %collective-permute-start.13 = (bf16[24,3584]{1,0:T(8,128)(2,1)S(1)}, bf16[24,3584]{1,0:T(8,128)(2,1)S(1)}, u32[]{:S(2)}, u32[]{:S(2)}) collective-permute-start(bf16[24,3584]{1,0:T(8,128)(2,1)S(1)} %add_convert_fusion.7), channel_id=1, source_target_pairs={{0,2},{1,5},{2,0},{3,7},{4,6},{5,1},{6,4},{7,3},{8,10},{9,13},{10,... | collective-permute-start | bytes 516104 | tf_op jit(solution)/shard_map/ppermute | solution.py:21
  (6 other events, 123.5 us)

commit v5 on v4

--- a/solution.py
+++ b/solution.py
@@ -213,25 +213,36 @@
 
 
 def mix_kernel(hi_ref, lo_ref, *refs):
-    values = [r[...].astype(jnp.float32) for r in refs[:-1]]
-    rows = jnp.concatenate(values, axis=0).astype(jnp.bfloat16)
-    total = jnp.dot(hi_ref[...], rows, preferred_element_type=jnp.float32)
-    total += jnp.dot(lo_ref[...], rows, preferred_element_type=jnp.float32)
-    refs[-1][...] = total.astype(jnp.bfloat16)
+    values, out, (stage_ref, sems) = refs[:-3], refs[-3], refs[-2:]
+    width = stage_ref.shape[1]
+    tile = column_tile(width)
+    copies = []
+    for k in range(width // tile):
+        cols = pl.ds(k * tile, tile)
+        rows = jnp.concatenate([r[:, cols].astype(jnp.float32) for r in values], axis=0)
+        rows = rows.astype(jnp.bfloat16)
+        total = jnp.dot(hi_ref[...], rows, preferred_element_type=jnp.float32)
+        total += jnp.dot(lo_ref[...], rows, preferred_element_type=jnp.float32)
+        stage_ref[:, cols] = total.astype(jnp.bfloat16)
+        copy = pltpu.make_async_copy(stage_ref.at[:, cols], out.at[:, cols], sems.at[k])
+        copy.start()
+        copies.append(copy)
+    for copy in copies:
+        copy.wait()
 
 
 GATHER = [[0], [1, 3], [2]]
 BACKS = [[3], [2], [1], [0]]
 GROUPS = [[0, 1], [2]]
 PLAN = (
-    ("Z", 3, 3), ("L", 0, 0), ("Z", 1, 3), ("W", 1, 1), ("z", 1, 0), ("l", 0, 0), ("z", 3, 3),
-    ("X", 0, 0), ("W", 0, 3), ("Z", 2, 3), ("L", 1, 3), ("l", 1, 2), ("X", 1, 2), ("w", 0, 1),
-    ("z", 2, 3), ("L", 2, 0), ("w", 1, 2), ("x", 0, 1), ("l", 2, 3), ("X", 2, 1), ("x", 1, 0),
-    ("K", 0, 0), ("x", 2, 0), ("K", 1, 0), ("C", 1, 0), ("C", 0, 0), ("H", 0, 1), ("h", 0, 0),
-    ("C", 2, 0), ("F", 0, 1), ("c", 1, 2), ("c", 0, 0), ("C", 3, 1), ("A", 0, 2), ("a", 0, 3),
-    ("A", 1, 0), ("c", 2, 0), ("a", 1, 1), ("B", 2, 0), ("c", 3, 2), ("A", 2, 0), ("a", 2, 2),
-    ("A", 3, 0), ("f", 0, 2), ("b", 2, 1), ("B", 3, 0), ("B", 1, 0), ("b", 3, 2), ("a", 3, 1),
-    ("b", 1, 1),
+    ("Z", 3, 3), ("L", 0, 0), ("Z", 1, 0), ("W", 1, 1), ("z", 1, 0), ("l", 0, 0), ("z", 3, 3),
+    ("X", 0, 0), ("W", 0, 2), ("Z", 2, 3), ("L", 1, 3), ("l", 1, 2), ("X", 1, 2), ("w", 0, 1),
+    ("z", 2, 3), ("L", 2, 0), ("w", 1, 0), ("x", 0, 1), ("l", 2, 3), ("X", 2, 1), ("x", 1, 0),
+    ("K", 0, 0), ("x", 2, 0), ("K", 1, 0), ("C", 2, 0), ("C", 0, 0), ("C", 1, 0), ("H", 0, 1),
+    ("h", 0, 0), ("F", 0, 1), ("c", 0, 2), ("A", 0, 2), ("c", 1, 1), ("A", 1, 2), ("a", 0, 1),
+    ("B", 3, 2), ("c", 2, 1), ("A", 2, 0), ("a", 1, 0), ("B", 2, 0), ("f", 0, 1), ("C", 3, 1),
+    ("a", 2, 0), ("B", 1, 0), ("c", 3, 0), ("A", 3, 0), ("a", 3, 0), ("b", 3, 0), ("b", 2, 1),
+    ("b", 1, 0),
 )
 
 
@@ -358,15 +369,15 @@
         compiler_params=small,
     )(me, swap_pairs, full, came["f", 0])
     finals = after([sums[0]] + [came["b", s] for s in range(1, experts)], token)
-    tile = column_tile(width)
-    moving = lambda rows: pl.BlockSpec((rows, tile), lambda i: (0, i))
-    fixed = pl.BlockSpec((tok_count, places), lambda i: (0, 0))
     mixed = pl.pallas_call(
         mix_kernel,
         out_shape=jax.ShapeDtypeStruct((tok_count, width), jnp.bfloat16),
-        grid=(width // tile,),
-        in_specs=[fixed] * 2 + [moving(capacity)] * experts,
-        out_specs=moving(tok_count),
+        in_specs=[VMEM] * (2 + experts),
+        out_specs=ANY,
+        scratch_shapes=[
+            pltpu.VMEM((tok_count, width), jnp.bfloat16),
+            pltpu.SemaphoreType.DMA((width // column_tile(width),)),
+        ],
         compiler_params=small,
     )(gate_hi, gate_lo, *finals)
     return (mixed, saved.reshape(1, devices * capacity, units))

time: 78.1 us -> 76 us (0.973)
  waiting for transfers between devices: 42.4 us -> 38.7 us
  starting transfers between devices: 24 us -> 26 us
    ppermute x24, waiting for transfers between devices: 42.4 us -> 38.7 us  [swap(): lax.ppermute(value, 'ep', [(i, i ^ mask_of(i)) for i in range(count)])]
    ppermute x24, starting transfers between devices: 24 us -> 26 us  [swap(): lax.ppermute(value, 'ep', [(i, i ^ mask_of(i)) for i in range(count)])]
  transfers between devices with their start and end apart: 24 -> 24, of which waited for: 15 -> 13; matrix products, arithmetic and copies ran while one was open for 2% -> 2% of each run, Pallas kernels for 6% -> 7%
where the time goes in v5:
time: 76 us; the launch traced here: 75.8 us
  waiting for transfers between devices  38.7 us (51%)
  starting transfers between devices  26 us (34%)
  Pallas kernels  8.8 us (12%)
  local copies, waits for them, and re-layouts  1.04 us (1%)
  between operations  0.84 us (1%)
    ppermute x24, waiting for transfers between devices, swap(): lax.ppermute(value, 'ep', [(i, i ^ mask_of(i)) for i in range(count)])  38.7 us
    ppermute x24, starting transfers between devices, swap(): lax.ppermute(value, 'ep', [(i, i ^ mask_of(i)) for i in range(count)])  26 us
    pallas_call x2, Pallas kernels, run_expert(): pl.pallas_call(functools.partial(expert_kernel, chunks, backs, ahead, fin...  3.63 us
    pallas_call x1, Pallas kernels, run_route(): pl.pallas_call(functools.partial(route_kernel, experts, capacity), out_sh...  2.45 us
  transfers between devices with their start and end apart: 24, of which 13 were waited for; matrix products, arithmetic and copies ran while one was open for 2% of the time, Pallas kernels for 7%

profile of v5, /device:TPU:0, one launch (start us, length us, event | category | flops | bytes accessed | tf_op | source)
XLA Modules:
  0.0 75.8 jit_solution(6486803472434908387)
XLA Ops:
  0.6 2.4 %shard_map.86 = (bf16[24,3584]{1,0:T(8,128)(2,1)}, bf16[24,3584]{1,0:T(8,128)(2,1)}, bf16[24,3584]{1,0:T(8,128)(2,1)}, bf16[24,3584]{1,0:T(8,128)(2,1)}, bf16[12...) custom-call(s32[1]{0:T(128)} %bitcast.me_ref, s32[1,64]{1,0:T(1,128)} %bitcast.14, s32[1,64]{1,0:T(1,128)} %bitcast.15, ...), custom_call_target="tpu_custom_call" | custom-call | tf_op jit(solution)/shard_map/pallas_call | solution.py:107
  3.1 3.0 %collective-permute-start = (bf16[24,3584]{1,0:T(8,128)(2,1)}, bf16[24,3584]{1,0:T(8,128)(2,1)S(1)}, u32[]{:S(2)}, u32[]{:S(2)}) collective-permute-start(bf16[24,3584]{1,0:T(8,128)(2,1)} %get-tuple-element.57), channel_id=1, source_target_pairs={{0,2},{1,5},{2,0},{3,7},{4,6},{5,1},{6,4},{7,3},{8,10},{9,13},{10,... | collective-permute-start | bytes 516104 | tf_op jit(solution)/shard_map/ppermute | solution.py:21
  6.1 3.6 %collective-permute-start.2 = (bf16[24,3584]{1,0:T(8,128)(2,1)}, bf16[24,3584]{1,0:T(8,128)(2,1)S(1)}, u32[]{:S(2)}, u32[]{:S(2)}) collective-permute-start(bf16[24,3584]{1,0:T(8,128)(2,1)} %get-tuple-element.60), channel_id=1, source_target_pairs={{0,24},{1,25},{2,26},{3,27},{4,28},{5,29},{6,30},{7,31},{8,16},{9,... | collective-permute-start | bytes 516104 | tf_op jit(solution)/shard_map/ppermute | solution.py:21
  11.2 1.6 %collective-permute-start.1 = (bf16[48,3584]{1,0:T(8,128)(2,1)S(1)}, bf16[48,3584]{1,0:T(8,128)(2,1)S(1)}, u32[]{:S(2)}, u32[]{:S(2)}) collective-permute-start(bf16[48,3584]{1,0:T(8,128)(2,1)S(1)} %constant_dynamic-update-slice_fusion.refs_0_), channel_id=1, source_target_pairs={{0,4},{1,3},{2,6},{3,1},{4,0},{5,7},{6,2},{7,5},{8,12},{9,11},{10,... | collective-permute-start | bytes 1032200 | tf_op jit(solution)/shard_map/ppermute | solution.py:21
  12.8 2.6 %collective-permute-done.2 = bf16[24,3584]{1,0:T(8,128)(2,1)S(1)} collective-permute-done((bf16[24,3584]{1,0:T(8,128)(2,1)}, bf16[24,3584]{1,0:T(8,128)(2,1)S(1)}, u32[]{:S(2)}, u32[]{:S(2)}) %collective-permute-start.2) | collective-permute-done | bytes 172064 | tf_op jit(solution)/shard_map/ppermute | solution.py:21
  15.4 2.4 %collective-permute-done.3 = bf16[24,3584]{1,0:T(8,128)(2,1)S(1)} collective-permute-done((bf16[24,3584]{1,0:T(8,128)(2,1)}, bf16[24,3584]{1,0:T(8,128)(2,1)S(1)}, u32[]{:S(2)}, u32[]{:S(2)}) %collective-permute-start.3) | collective-permute-done | bytes 172064 | tf_op jit(solution)/shard_map/ppermute | solution.py:21
  17.9 1.6 %collective-permute-start.4 = (bf16[48,3584]{1,0:T(8,128)(2,1)S(1)}, bf16[48,3584]{1,0:T(8,128)(2,1)S(1)}, u32[]{:S(2)}, u32[]{:S(2)}) collective-permute-start(bf16[48,3584]{1,0:T(8,128)(2,1)S(1)} %pad_maximum_fusion), channel_id=1, source_target_pairs={{0,2},{1,5},{2,0},{3,7},{4,6},{5,1},{6,4},{7,3},{8,10},{9,13},{10,... | collective-permute-start | bytes 1032200 | tf_op jit(solution)/shard_map/ppermute | solution.py:21
  20.1 5.1 %collective-permute-done.4 = bf16[48,3584]{1,0:T(8,128)(2,1)S(1)} collective-permute-done((bf16[48,3584]{1,0:T(8,128)(2,1)S(1)}, bf16[48,3584]{1,0:T(8,128)(2,1)S(1)}, u32[]{:S(2)}, u32[]{:S(2)}) %collective-permute-start.4) | collective-permute-done | bytes 344096 | tf_op jit(solution)/shard_map/ppermute | solution.py:21
  25.8 3.1 %collective-permute-done.5 = bf16[24,3584]{1,0:T(8,128)(2,1)S(1)} collective-permute-done((bf16[24,3584]{1,0:T(8,128)(2,1)}, bf16[24,3584]{1,0:T(8,128)(2,1)S(1)}, u32[]{:S(2)}, u32[]{:S(2)}) %collective-permute-start.5) | collective-permute-done | bytes 172064 | tf_op jit(solution)/shard_map/ppermute | solution.py:21
  28.9 1.7 %collective-permute-start.9 = (bf16[24,3584]{1,0:T(8,128)(2,1)S(1)}, bf16[24,3584]{1,0:T(8,128)(2,1)S(1)}, u32[]{:S(2)}, u32[]{:S(2)}) collective-permute-start(bf16[24,3584]{1,0:T(8,128)(2,1)S(1)} %collective-permute-done.5), channel_id=1, source_target_pairs={{0,2},{1,5},{2,0},{3,7},{4,6},{5,1},{6,4},{7,3},{8,10},{9,13},{10,... | collective-permute-start | bytes 516104 | tf_op jit(solution)/shard_map/ppermute | solution.py:21
  30.6 5.4 %collective-permute-done.9 = bf16[24,3584]{1,0:T(8,128)(2,1)S(1)} collective-permute-done((bf16[24,3584]{1,0:T(8,128)(2,1)S(1)}, bf16[24,3584]{1,0:T(8,128)(2,1)S(1)}, u32[]{:S(2)}, u32[]{:S(2)}) %collective-permute-start.9) | collective-permute-done | bytes 172064 | tf_op jit(solution)/shard_map/ppermute | solution.py:21
  36.4 1.6 %collective-permute-done.6.refs_3_ = bf16[96,3584]{1,0:T(8,128)(2,1)S(1)} collective-permute-done((bf16[96,3584]{1,0:T(8,128)(2,1)S(1)}, bf16[96,3584]{1,0:T(8,128)(2,1)S(1)}, u32[]{:S(2)}, u32[]{:S(2)}) %collective-permute-start.6) | collective-permute-done | bytes 688160 | tf_op jit(solution)/shard_map/ppermute | solution.py:21
  38.1 2.4 %shard_map.87 = (bf16[48,3584]{1,0:T(8,128)(2,1)S(1)}, bf16[48,3584]{1,0:T(8,128)(2,1)S(1)}, bf16[48,3584]{1,0:T(8,128)(2,1)S(1)}, bf16[48,3584]{1,0:T(8,128)(2,...) custom-call(s32[1]{0:T(128)} %bitcast.me_ref, ...), custom_call_target="tpu_custom_call" | custom-call | flops 1 | bytes 1 | tf_op jit(solution)/shard_map/pallas_call | solution.py:190
  41.1 2.3 %collective-permute-done.11.refs_1_ = bf16[48,3584]{1,0:T(8,128)(2,1)S(1)} collective-permute-done((bf16[48,3584]{1,0:T(8,128)(2,1)S(1)}, bf16[48,3584]{1,0:T(8,128)(2,1)S(1)}, u32[]{:S(2)}, u32[]{:S(2)}) %collective-permute-start.11) | collective-permute-done | bytes 344096 | tf_op jit(solution)/shard_map/ppermute | solution.py:21
  45.0 1.7 %collective-permute-start.16 = (bf16[48,3584]{1,0:T(8,128)(2,1)S(1)}, bf16[48,3584]{1,0:T(8,128)(2,1)S(1)}, u32[]{:S(2)}, u32[]{:S(2)}) collective-permute-start(bf16[48,3584]{1,0:T(8,128)(2,1)S(1)} %get-tuple-element.96), channel_id=1, source_target_pairs={{0,4},{1,3},{2,6},{3,1},{4,0},{5,7},{6,2},{7,5},{8,12},{9,11},{10,... | collective-permute-start | bytes 1032200 | tf_op jit(solution)/shard_map/ppermute | solution.py:21
  47.8 1.6 %collective-permute-start.13 = (bf16[24,3584]{1,0:T(8,128)(2,1)S(1)}, bf16[24,3584]{1,0:T(8,128)(2,1)S(1)}, u32[]{:S(2)}, u32[]{:S(2)}) collective-permute-start(bf16[24,3584]{1,0:T(8,128)(2,1)S(1)} %add_convert_fusion.7), channel_id=1, source_target_pairs={{0,2},{1,5},{2,0},{3,7},{4,6},{5,1},{6,4},{7,3},{8,10},{9,13},{10,... | collective-permute-start | bytes 516104 | tf_op jit(solution)/shard_map/ppermute | solution.py:21
  49.4 4.4 %collective-permute-done.12 = bf16[48,3584]{1,0:T(8,128)(2,1)S(1)} collective-permute-done((bf16[48,3584]{1,0:T(8,128)(2,1)S(1)}, bf16[48,3584]{1,0:T(8,128)(2,1)S(1)}, u32[]{:S(2)}, u32[]{:S(2)}) %collective-permute-start.12) | collective-permute-done | bytes 344096 | tf_op jit(solution)/shard_map/ppermute | solution.py:21
  53.9 1.8 %collective-permute-start.19 = (bf16[24,3584]{1,0:T(8,128)(2,1)S(1)}, bf16[24,3584]{1,0:T(8,128)(2,1)S(1)}, u32[]{:S(2)}, u32[]{:S(2)}) collective-permute-start(bf16[24,3584]{1,0:T(8,128)(2,1)S(1)} %add_convert_fusion.6), channel_id=1, source_target_pairs={{0,2},{1,5},{2,0},{3,7},{4,6},{5,1},{6,4},{7,3},{8,10},{9,13},{10,... | collective-permute-start | bytes 516104 | tf_op jit(solution)/shard_map/ppermute | solution.py:21
  55.8 1.4 %collective-permute-start.21 = (bf16[24,3584]{1,0:T(8,128)(2,1)S(1)}, bf16[24,3584]{1,0:T(8,128)(2,1)S(1)}, u32[]{:S(2)}, u32[]{:S(2)}) collective-permute-start(bf16[24,3584]{1,0:T(8,128)(2,1)S(1)} %add_convert_fusion.5), channel_id=1, source_target_pairs={{0,24},{1,25},{2,26},{3,27},{4,28},{5,29},{6,30},{7,31},{8,16},{9,... | collective-permute-start | bytes 516104 | tf_op jit(solution)/shard_map/ppermute | solution.py:21
  59.4 1.8 %collective-permute-start.17 = (bf16[24,3584]{1,0:T(8,128)(2,1)S(1)}, bf16[24,3584]{1,0:T(8,128)(2,1)S(1)}, u32[]{:S(2)}, u32[]{:S(2)}) collective-permute-start(bf16[24,3584]{1,0:T(8,128)(2,1)S(1)} %add_convert_fusion.2), channel_id=1, source_target_pairs={{0,2},{1,5},{2,0},{3,7},{4,6},{5,1},{6,4},{7,3},{8,10},{9,13},{10,... | collective-permute-start | bytes 516104 | tf_op jit(solution)/shard_map/ppermute | solution.py:21
  62.7 2.7 %collective-permute-done.14 = bf16[48,3584]{1,0:T(8,128)(2,1)S(1)} collective-permute-done((bf16[48,3584]{1,0:T(8,128)(2,1)S(1)}, bf16[48,3584]{1,0:T(8,128)(2,1)S(1)}, u32[]{:S(2)}, u32[]{:S(2)}) %collective-permute-start.14) | collective-permute-done | bytes 344096 | tf_op jit(solution)/shard_map/ppermute | solution.py:21
  65.4 1.8 %collective-permute-start.15 = (bf16[24,3584]{1,0:T(8,128)(2,1)S(1)}, bf16[24,3584]{1,0:T(8,128)(2,1)S(1)}, u32[]{:S(2)}, u32[]{:S(2)}) collective-permute-start(bf16[24,3584]{1,0:T(8,128)(2,1)S(1)} %add_convert_fusion.4), channel_id=1, source_target_pairs={{0,2},{1,5},{2,0},{3,7},{4,6},{5,1},{6,4},{7,3},{8,10},{9,13},{10,... | collective-permute-start | bytes 516104 | tf_op jit(solution)/shard_map/ppermute | solution.py:21
  67.7 5.0 %collective-permute-done.20.refs_2_ = bf16[24,3584]{1,0:T(8,128)(2,1)S(1)} collective-permute-done((bf16[24,3584]{1,0:T(8,128)(2,1)S(1)}, bf16[24,3584]{1,0:T(8,128)(2,1)S(1)}, u32[]{:S(2)}, u32[]{:S(2)}) %collective-permute-start.20) | collective-permute-done | bytes 172064 | tf_op jit(solution)/shard_map/ppermute | solution.py:21
  72.7 1.7 %collective-permute-done.18.refs_1_ = bf16[24,3584]{1,0:T(8,128)(2,1)S(1)} collective-permute-done((bf16[24,3584]{1,0:T(8,128)(2,1)S(1)}, bf16[24,3584]{1,0:T(8,128)(2,1)S(1)}, u32[]{:S(2)}, u32[]{:S(2)}) %collective-permute-start.18) | collective-permute-done | bytes 172064 | tf_op jit(solution)/shard_map/ppermute | solution.py:21
  (56 shorter events, 12.2 us)
Async XLA Ops:
  3.1 8.1 %collective-permute-start = (bf16[24,3584]{1,0:T(8,128)(2,1)}, bf16[24,3584]{1,0:T(8,128)(2,1)S(1)}, u32[]{:S(2)}, u32[]{:S(2)}) collective-permute-start(bf16[24,3584]{1,0:T(8,128)(2,1)} %get-tuple-element.57), channel_id=1, source_target_pairs={{0,2},{1,5},{2,0},{3,7},{4,6},{5,1},{6,4},{7,3},{8,10},{9,13},{10,... | collective-permute-start | bytes 516104 | tf_op jit(solution)/shard_map/ppermute | solution.py:21
  6.1 9.3 %collective-permute-start.2 = (bf16[24,3584]{1,0:T(8,128)(2,1)}, bf16[24,3584]{1,0:T(8,128)(2,1)S(1)}, u32[]{:S(2)}, u32[]{:S(2)}) collective-permute-start(bf16[24,3584]{1,0:T(8,128)(2,1)} %get-tuple-element.60), channel_id=1, source_target_pairs={{0,24},{1,25},{2,26},{3,27},{4,28},{5,29},{6,30},{7,31},{8,16},{9,... | collective-permute-start | bytes 516104 | tf_op jit(solution)/shard_map/ppermute | solution.py:21
  9.7 8.1 %collective-permute-start.3 = (bf16[24,3584]{1,0:T(8,128)(2,1)}, bf16[24,3584]{1,0:T(8,128)(2,1)S(1)}, u32[]{:S(2)}, u32[]{:S(2)}) collective-permute-start(bf16[24,3584]{1,0:T(8,128)(2,1)} %get-tuple-element.65), channel_id=1, source_target_pairs={{0,8},{1,9},{2,10},{3,11},{4,12},{5,13},{6,14},{7,15},{8,0},{9,1},... | collective-permute-start | bytes 516104 | tf_op jit(solution)/shard_map/ppermute | solution.py:21
  9.7 26.7 %collective-permute-start.7 = (bf16[3584,256]{1,0:T(8,128)(2,1)}, bf16[3584,256]{1,0:T(8,128)(2,1)S(1)}, u32[]{:S(2)}, u32[]{:S(2)}) collective-permute-start(bf16[3584,256]{1,0:T(8,128)(2,1)} %bitcast.7), channel_id=1, source_target_pairs={{0,1},{1,0},{2,3},{3,2},{4,5},{5,4},{6,7},{7,6},{8,9},{9,8},{10,11... | collective-permute-start | bytes 5505032 | tf_op jit(solution)/shard_map/ppermute | solution.py:21
  9.7 26.7 %collective-permute-start.8 = (bf16[128,3584]{1,0:T(8,128)(2,1)}, bf16[128,3584]{1,0:T(8,128)(2,1)S(1)}, u32[]{:S(2)}, u32[]{:S(2)}) collective-permute-start(bf16[128,3584]{1,0:T(8,128)(2,1)} %bitcast.10), channel_id=1, source_target_pairs={{0,1},{1,0},{2,3},{3,2},{4,5},{5,4},{6,7},{7,6},{8,9},{9,8},{10,11... | collective-permute-start | bytes 2752520 | tf_op jit(solution)/shard_map/ppermute | solution.py:21
  11.2 25.2 %collective-permute-start.1 = (bf16[48,3584]{1,0:T(8,128)(2,1)S(1)}, bf16[48,3584]{1,0:T(8,128)(2,1)S(1)}, u32[]{:S(2)}, u32[]{:S(2)}) collective-permute-start(bf16[48,3584]{1,0:T(8,128)(2,1)S(1)} %constant_dynamic-update-slice_fusion.refs_0_), channel_id=1, source_target_pairs={{0,4},{1,3},{2,6},{3,1},{4,0},{5,7},{6,2},{7,5},{8,12},{9,11},{10,... | collective-permute-start | bytes 1032200 | tf_op jit(solution)/shard_map/ppermute | solution.py:21
  17.9 7.3 %collective-permute-start.4 = (bf16[48,3584]{1,0:T(8,128)(2,1)S(1)}, bf16[48,3584]{1,0:T(8,128)(2,1)S(1)}, u32[]{:S(2)}, u32[]{:S(2)}) collective-permute-start(bf16[48,3584]{1,0:T(8,128)(2,1)S(1)} %pad_maximum_fusion), channel_id=1, source_target_pairs={{0,2},{1,5},{2,0},{3,7},{4,6},{5,1},{6,4},{7,3},{8,10},{9,13},{10,... | collective-permute-start | bytes 1032200 | tf_op jit(solution)/shard_map/ppermute | solution.py:21
  19.4 9.5 %collective-permute-start.5 = (bf16[24,3584]{1,0:T(8,128)(2,1)}, bf16[24,3584]{1,0:T(8,128)(2,1)S(1)}, u32[]{:S(2)}, u32[]{:S(2)}) collective-permute-start(bf16[24,3584]{1,0:T(8,128)(2,1)} %get-tuple-element.71), channel_id=1, source_target_pairs={{0,16},{1,17},{2,18},{3,19},{4,20},{5,21},{6,22},{7,23},{8,24},{9,... | collective-permute-start | bytes 516104 | tf_op jit(solution)/shard_map/ppermute | solution.py:21
  25.2 12.8 %collective-permute-start.6 = (bf16[96,3584]{1,0:T(8,128)(2,1)S(1)}, bf16[96,3584]{1,0:T(8,128)(2,1)S(1)}, u32[]{:S(2)}, u32[]{:S(2)}) collective-permute-start(bf16[96,3584]{1,0:T(8,128)(2,1)S(1)} %constant_dynamic-update-slice_fusion.2.refs_2_), channel_id=1, source_target_pairs={{0,4},{1,3},{2,6},{3,1},{4,0},{5,7},{6,2},{7,5},{8,12},{9,11},{10,... | collective-permute-start | bytes 2064392 | tf_op jit(solution)/shard_map/ppermute | solution.py:21
  28.9 7.1 %collective-permute-start.9 = (bf16[24,3584]{1,0:T(8,128)(2,1)S(1)}, bf16[24,3584]{1,0:T(8,128)(2,1)S(1)}, u32[]{:S(2)}, u32[]{:S(2)}) collective-permute-start(bf16[24,3584]{1,0:T(8,128)(2,1)S(1)} %collective-permute-done.5), channel_id=1, source_target_pairs={{0,2},{1,5},{2,0},{3,7},{4,6},{5,1},{6,4},{7,3},{8,10},{9,13},{10,... | collective-permute-start | bytes 516104 | tf_op jit(solution)/shard_map/ppermute | solution.py:21
  36.1 7.3 %collective-permute-start.11 = (bf16[48,3584]{1,0:T(8,128)(2,1)S(1)}, bf16[48,3584]{1,0:T(8,128)(2,1)S(1)}, u32[]{:S(2)}, u32[]{:S(2)}) collective-permute-start(bf16[48,3584]{1,0:T(8,128)(2,1)S(1)} %constant_dynamic-update-slice_fusion.5.refs_0_), channel_id=1, source_target_pairs={{0,4},{1,3},{2,6},{3,1},{4,0},{5,7},{6,2},{7,5},{8,12},{9,11},{10,... | collective-permute-start | bytes 1032200 | tf_op jit(solution)/shard_map/ppermute | solution.py:21
  40.5 7.3 %collective-permute-start.10 = (bf16[48,3584]{1,0:T(8,128)(2,1)S(1)}, bf16[48,3584]{1,0:T(8,128)(2,1)S(1)}, u32[]{:S(2)}, u32[]{:S(2)}) collective-permute-start(bf16[48,3584]{1,0:T(8,128)(2,1)S(1)} %get-tuple-element.80), channel_id=1, source_target_pairs={{0,4},{1,3},{2,6},{3,1},{4,0},{5,7},{6,2},{7,5},{8,12},{9,11},{10,... | collective-permute-start | bytes 1032200 | tf_op jit(solution)/shard_map/ppermute | solution.py:21
  44.6 2.2 %collective-permute-start.22 = (bf16[16,24,128]{2,1,0:T(8,128)(2,1)S(1)}, bf16[16,24,128]{2,1,0:T(8,128)(2,1)S(1)}, u32[]{:S(2)}, u32[]{:S(2)}) collective-permute-start(bf16[16,24,128]{2,1,0:T(8,128)(2,1)S(1)} %get-tuple-element.105), channel_id=1, source_target_pairs={{0,1},{1,0},{2,3},{3,2},{4,5},{5,4},{6,7},{7,6},{8,9},{9,8},{10,11... | collective-permute-start | bytes 294920 | tf_op jit(solution)/shard_map/ppermute | solution.py:21
  44.7 9.2 %collective-permute-start.12 = (bf16[48,3584]{1,0:T(8,128)(2,1)S(1)}, bf16[48,3584]{1,0:T(8,128)(2,1)S(1)}, u32[]{:S(2)}, u32[]{:S(2)}) collective-permute-start(bf16[48,3584]{1,0:T(8,128)(2,1)S(1)} %get-tuple-element.89), channel_id=1, source_target_pairs={{0,4},{1,3},{2,6},{3,1},{4,0},{5,7},{6,2},{7,5},{8,12},{9,11},{10,... | collective-permute-start | bytes 1032200 | tf_op jit(solution)/shard_map/ppermute | solution.py:21
  45.0 14.3 %collective-permute-start.16 = (bf16[48,3584]{1,0:T(8,128)(2,1)S(1)}, bf16[48,3584]{1,0:T(8,128)(2,1)S(1)}, u32[]{:S(2)}, u32[]{:S(2)}) collective-permute-start(bf16[48,3584]{1,0:T(8,128)(2,1)S(1)} %get-tuple-element.96), channel_id=1, source_target_pairs={{0,4},{1,3},{2,6},{3,1},{4,0},{5,7},{6,2},{7,5},{8,12},{9,11},{10,... | collective-permute-start | bytes 1032200 | tf_op jit(solution)/shard_map/ppermute | solution.py:21
  46.8 14.6 %collective-permute-start.23 = (bf16[16,2,24,128]{3,2,1,0:T(8,128)(2,1)S(1)}, bf16[16,2,24,128]{3,2,1,0:T(8,128)(2,1)S(1)}, u32[]{:S(2)}, u32[]{:S(2)}) collective-permute-start(bf16[16,2,24,128]{3,2,1,0:T(8,128)(2,1)S(1)} %shard_map.90.mine_ref), channel_id=1, source_target_pairs={{0,16},{1,17},{2,18},{3,19},{4,20},{5,21},{6,22},{7,23},{8,24},{9,... | collective-permute-start | bytes 589832 | tf_op jit(solution)/shard_map/ppermute | solution.py:21
  47.8 7.9 %collective-permute-start.13 = (bf16[24,3584]{1,0:T(8,128)(2,1)S(1)}, bf16[24,3584]{1,0:T(8,128)(2,1)S(1)}, u32[]{:S(2)}, u32[]{:S(2)}) collective-permute-start(bf16[24,3584]{1,0:T(8,128)(2,1)S(1)} %add_convert_fusion.7), channel_id=1, source_target_pairs={{0,2},{1,5},{2,0},{3,7},{4,6},{5,1},{6,4},{7,3},{8,10},{9,13},{10,... | collective-permute-start | bytes 516104 | tf_op jit(solution)/shard_map/ppermute | solution.py:21
  53.9 7.3 %collective-permute-start.19 = (bf16[24,3584]{1,0:T(8,128)(2,1)S(1)}, bf16[24,3584]{1,0:T(8,128)(2,1)S(1)}, u32[]{:S(2)}, u32[]{:S(2)}) collective-permute-start(bf16[24,3584]{1,0:T(8,128)(2,1)S(1)} %add_convert_fusion.6), channel_id=1, source_target_pairs={{0,2},{1,5},{2,0},{3,7},{4,6},{5,1},{6,4},{7,3},{8,10},{9,13},{10,... | collective-permute-start | bytes 516104 | tf_op jit(solution)/shard_map/ppermute | solution.py:21
  55.8 17.0 %collective-permute-start.21 = (bf16[24,3584]{1,0:T(8,128)(2,1)S(1)}, bf16[24,3584]{1,0:T(8,128)(2,1)S(1)}, u32[]{:S(2)}, u32[]{:S(2)}) collective-permute-start(bf16[24,3584]{1,0:T(8,128)(2,1)S(1)} %add_convert_fusion.5), channel_id=1, source_target_pairs={{0,24},{1,25},{2,26},{3,27},{4,28},{5,29},{6,30},{7,31},{8,16},{9,... | collective-permute-start | bytes 516104 | tf_op jit(solution)/shard_map/ppermute | solution.py:21
  57.2 8.1 %collective-permute-start.14 = (bf16[48,3584]{1,0:T(8,128)(2,1)S(1)}, bf16[48,3584]{1,0:T(8,128)(2,1)S(1)}, u32[]{:S(2)}, u32[]{:S(2)}) collective-permute-start(bf16[48,3584]{1,0:T(8,128)(2,1)S(1)} %get-tuple-element.94), channel_id=1, source_target_pairs={{0,4},{1,3},{2,6},{3,1},{4,0},{5,7},{6,2},{7,5},{8,12},{9,11},{10,... | collective-permute-start | bytes 1032200 | tf_op jit(solution)/shard_map/ppermute | solution.py:21
  59.4 7.8 %collective-permute-start.17 = (bf16[24,3584]{1,0:T(8,128)(2,1)S(1)}, bf16[24,3584]{1,0:T(8,128)(2,1)S(1)}, u32[]{:S(2)}, u32[]{:S(2)}) collective-permute-start(bf16[24,3584]{1,0:T(8,128)(2,1)S(1)} %add_convert_fusion.2), channel_id=1, source_target_pairs={{0,2},{1,5},{2,0},{3,7},{4,6},{5,1},{6,4},{7,3},{8,10},{9,13},{10,... | collective-permute-start | bytes 516104 | tf_op jit(solution)/shard_map/ppermute | solution.py:21
  61.3 11.3 %collective-permute-start.20 = (bf16[24,3584]{1,0:T(8,128)(2,1)S(1)}, bf16[24,3584]{1,0:T(8,128)(2,1)S(1)}, u32[]{:S(2)}, u32[]{:S(2)}) collective-permute-start(bf16[24,3584]{1,0:T(8,128)(2,1)S(1)} %add_convert_fusion), channel_id=1, source_target_pairs={{0,16},{1,17},{2,18},{3,19},{4,20},{5,21},{6,22},{7,23},{8,24},{9,... | collective-permute-start | bytes 516104 | tf_op jit(solution)/shard_map/ppermute | solution.py:21
  65.4 7.2 %collective-permute-start.15 = (bf16[24,3584]{1,0:T(8,128)(2,1)S(1)}, bf16[24,3584]{1,0:T(8,128)(2,1)S(1)}, u32[]{:S(2)}, u32[]{:S(2)}) collective-permute-start(bf16[24,3584]{1,0:T(8,128)(2,1)S(1)} %add_convert_fusion.4), channel_id=1, source_target_pairs={{0,2},{1,5},{2,0},{3,7},{4,6},{5,1},{6,4},{7,3},{8,10},{9,13},{10,... | collective-permute-start | bytes 516104 | tf_op jit(solution)/shard_map/ppermute | solution.py:21
  67.3 7.1 %collective-permute-start.18 = (bf16[24,3584]{1,0:T(8,128)(2,1)S(1)}, bf16[24,3584]{1,0:T(8,128)(2,1)S(1)}, u32[]{:S(2)}, u32[]{:S(2)}) collective-permute-start(bf16[24,3584]{1,0:T(8,128)(2,1)S(1)} %add_convert_fusion.1), channel_id=1, source_target_pairs={{0,8},{1,9},{2,10},{3,11},{4,12},{5,13},{6,14},{7,15},{8,0},{9,1},... | collective-permute-start | bytes 516104 | tf_op jit(solution)/shard_map/ppermute | solution.py:21
  (5 other events, 116.7 us)

commit v6 on v5

--- a/solution.py
+++ b/solution.py
@@ -235,14 +235,14 @@
 BACKS = [[3], [2], [1], [0]]
 GROUPS = [[0, 1], [2]]
 PLAN = (
-    ("Z", 3, 3), ("L", 0, 0), ("Z", 1, 0), ("W", 1, 1), ("z", 1, 0), ("l", 0, 0), ("z", 3, 3),
-    ("X", 0, 0), ("W", 0, 2), ("Z", 2, 3), ("L", 1, 3), ("l", 1, 2), ("X", 1, 2), ("w", 0, 1),
+    ("Z", 3, 3), ("L", 0, 0), ("Z", 1, 0), ("W", 1, 1), ("l", 0, 0), ("X", 0, 0), ("z", 3, 3),
+    ("Z", 2, 3), ("z", 1, 1), ("W", 0, 2), ("L", 1, 3), ("l", 1, 2), ("X", 1, 2), ("w", 0, 1),
     ("z", 2, 3), ("L", 2, 0), ("w", 1, 0), ("x", 0, 1), ("l", 2, 3), ("X", 2, 1), ("x", 1, 0),
     ("K", 0, 0), ("x", 2, 0), ("K", 1, 0), ("C", 2, 0), ("C", 0, 0), ("C", 1, 0), ("H", 0, 1),
     ("h", 0, 0), ("F", 0, 1), ("c", 0, 2), ("A", 0, 2), ("c", 1, 1), ("A", 1, 2), ("a", 0, 1),
-    ("B", 3, 2), ("c", 2, 1), ("A", 2, 0), ("a", 1, 0), ("B", 2, 0), ("f", 0, 1), ("C", 3, 1),
-    ("a", 2, 0), ("B", 1, 0), ("c", 3, 0), ("A", 3, 0), ("a", 3, 0), ("b", 3, 0), ("b", 2, 1),
-    ("b", 1, 0),
+    ("B", 3, 2), ("C", 3, 1), ("c", 2, 1), ("A", 2, 0), ("a", 1, 0), ("B", 2, 0), ("f", 0, 1),
+    ("a", 2, 0), ("B", 1, 0), ("c", 3, 0), ("A", 3, 0), ("b", 3, 3), ("b", 2, 3), ("b", 1, 3),
+    ("a", 3, 1),
 )
 
 

time: 76 us -> 75.3 us (level)
  waiting for transfers between devices: 38.7 us -> 37 us
  starting transfers between devices: 26 us -> 27 us
    ppermute x24, waiting for transfers between devices: 38.7 us -> 37 us  [swap(): lax.ppermute(value, 'ep', [(i, i ^ mask_of(i)) for i in range(count)])]
    ppermute x24, starting transfers between devices: 26 us -> 27 us  [swap(): lax.ppermute(value, 'ep', [(i, i ^ mask_of(i)) for i in range(count)])]
where the time goes in v6:
time: 75.3 us; the launch traced here: 75.2 us
  waiting for transfers between devices  37 us (49%)
  starting transfers between devices  27 us (36%)
  Pallas kernels  8.81 us (12%)
  local copies, waits for them, and re-layouts  1.04 us (1%)
  between operations  0.83 us (1%)
    ppermute x24, waiting for transfers between devices, swap(): lax.ppermute(value, 'ep', [(i, i ^ mask_of(i)) for i in range(count)])  37 us
    ppermute x24, starting transfers between devices, swap(): lax.ppermute(value, 'ep', [(i, i ^ mask_of(i)) for i in range(count)])  27 us
    pallas_call x2, Pallas kernels, run_expert(): pl.pallas_call(functools.partial(expert_kernel, chunks, backs, ahead, fin...  3.64 us
    pallas_call x1, Pallas kernels, run_route(): pl.pallas_call(functools.partial(route_kernel, experts, capacity), out_sh...  2.45 us
  transfers between devices with their start and end apart: 24, of which 13 were waited for; matrix products, arithmetic and copies ran while one was open for 2% of the time, Pallas kernels for 7%

profile of v6, /device:TPU:0, one launch (start us, length us, event | category | flops | bytes accessed | tf_op | source)
XLA Modules:
  0.0 75.2 jit_solution(14372094093309168373)
XLA Ops:
  0.6 2.4 %shard_map.86 = (bf16[24,3584]{1,0:T(8,128)(2,1)}, bf16[24,3584]{1,0:T(8,128)(2,1)}, bf16[24,3584]{1,0:T(8,128)(2,1)}, bf16[24,3584]{1,0:T(8,128)(2,1)}, bf16[12...) custom-call(s32[1]{0:T(128)} %bitcast.me_ref, s32[1,64]{1,0:T(1,128)} %bitcast.14, s32[1,64]{1,0:T(1,128)} %bitcast.15, ...), custom_call_target="tpu_custom_call" | custom-call | tf_op jit(solution)/shard_map/pallas_call | solution.py:107
  3.1 3.0 %collective-permute-start = (bf16[24,3584]{1,0:T(8,128)(2,1)}, bf16[24,3584]{1,0:T(8,128)(2,1)S(1)}, u32[]{:S(2)}, u32[]{:S(2)}) collective-permute-start(bf16[24,3584]{1,0:T(8,128)(2,1)} %get-tuple-element.64), channel_id=1, source_target_pairs={{0,2},{1,5},{2,0},{3,7},{4,6},{5,1},{6,4},{7,3},{8,10},{9,13},{10,... | collective-permute-start | bytes 516104 | tf_op jit(solution)/shard_map/ppermute | solution.py:21
  6.1 3.6 %collective-permute-start.2 = (bf16[24,3584]{1,0:T(8,128)(2,1)}, bf16[24,3584]{1,0:T(8,128)(2,1)S(1)}, u32[]{:S(2)}, u32[]{:S(2)}) collective-permute-start(bf16[24,3584]{1,0:T(8,128)(2,1)} %get-tuple-element.67), channel_id=1, source_target_pairs={{0,24},{1,25},{2,26},{3,27},{4,28},{5,29},{6,30},{7,31},{8,16},{9,... | collective-permute-start | bytes 516104 | tf_op jit(solution)/shard_map/ppermute | solution.py:21
  11.2 1.6 %collective-permute-start.1 = (bf16[48,3584]{1,0:T(8,128)(2,1)S(1)}, bf16[48,3584]{1,0:T(8,128)(2,1)S(1)}, u32[]{:S(2)}, u32[]{:S(2)}) collective-permute-start(bf16[48,3584]{1,0:T(8,128)(2,1)S(1)} %constant_dynamic-update-slice_fusion.refs_0_), channel_id=1, source_target_pairs={{0,4},{1,3},{2,6},{3,1},{4,0},{5,7},{6,2},{7,5},{8,12},{9,11},{10,... | collective-permute-start | bytes 1032200 | tf_op jit(solution)/shard_map/ppermute | solution.py:21
  12.8 2.6 %collective-permute-done.2 = bf16[24,3584]{1,0:T(8,128)(2,1)S(1)} collective-permute-done((bf16[24,3584]{1,0:T(8,128)(2,1)}, bf16[24,3584]{1,0:T(8,128)(2,1)S(1)}, u32[]{:S(2)}, u32[]{:S(2)}) %collective-permute-start.2) | collective-permute-done | bytes 172064 | tf_op jit(solution)/shard_map/ppermute | solution.py:21
  15.4 2.4 %collective-permute-done.3 = bf16[24,3584]{1,0:T(8,128)(2,1)S(1)} collective-permute-done((bf16[24,3584]{1,0:T(8,128)(2,1)}, bf16[24,3584]{1,0:T(8,128)(2,1)S(1)}, u32[]{:S(2)}, u32[]{:S(2)}) %collective-permute-start.3) | collective-permute-done | bytes 172064 | tf_op jit(solution)/shard_map/ppermute | solution.py:21
  17.9 1.6 %collective-permute-start.4 = (bf16[48,3584]{1,0:T(8,128)(2,1)S(1)}, bf16[48,3584]{1,0:T(8,128)(2,1)S(1)}, u32[]{:S(2)}, u32[]{:S(2)}) collective-permute-start(bf16[48,3584]{1,0:T(8,128)(2,1)S(1)} %pad_maximum_fusion), channel_id=1, source_target_pairs={{0,2},{1,5},{2,0},{3,7},{4,6},{5,1},{6,4},{7,3},{8,10},{9,13},{10,... | collective-permute-start | bytes 1032200 | tf_op jit(solution)/shard_map/ppermute | solution.py:21
  20.1 5.1 %collective-permute-done.4 = bf16[48,3584]{1,0:T(8,128)(2,1)S(1)} collective-permute-done((bf16[48,3584]{1,0:T(8,128)(2,1)S(1)}, bf16[48,3584]{1,0:T(8,128)(2,1)S(1)}, u32[]{:S(2)}, u32[]{:S(2)}) %collective-permute-start.4) | collective-permute-done | bytes 344096 | tf_op jit(solution)/shard_map/ppermute | solution.py:21
  25.8 3.1 %collective-permute-done.5 = bf16[24,3584]{1,0:T(8,128)(2,1)S(1)} collective-permute-done((bf16[24,3584]{1,0:T(8,128)(2,1)}, bf16[24,3584]{1,0:T(8,128)(2,1)S(1)}, u32[]{:S(2)}, u32[]{:S(2)}) %collective-permute-start.5) | collective-permute-done | bytes 172064 | tf_op jit(solution)/shard_map/ppermute | solution.py:21
  28.9 1.7 %collective-permute-start.9 = (bf16[24,3584]{1,0:T(8,128)(2,1)S(1)}, bf16[24,3584]{1,0:T(8,128)(2,1)S(1)}, u32[]{:S(2)}, u32[]{:S(2)}) collective-permute-start(bf16[24,3584]{1,0:T(8,128)(2,1)S(1)} %collective-permute-done.5), channel_id=1, source_target_pairs={{0,2},{1,5},{2,0},{3,7},{4,6},{5,1},{6,4},{7,3},{8,10},{9,13},{10,... | collective-permute-start | bytes 516104 | tf_op jit(solution)/shard_map/ppermute | solution.py:21
  30.7 5.4 %collective-permute-done.9 = bf16[24,3584]{1,0:T(8,128)(2,1)S(1)} collective-permute-done((bf16[24,3584]{1,0:T(8,128)(2,1)S(1)}, bf16[24,3584]{1,0:T(8,128)(2,1)S(1)}, u32[]{:S(2)}, u32[]{:S(2)}) %collective-permute-start.9) | collective-permute-done | bytes 172064 | tf_op jit(solution)/shard_map/ppermute | solution.py:21
  36.4 1.6 %collective-permute-done.6.refs_3_ = bf16[96,3584]{1,0:T(8,128)(2,1)S(1)} collective-permute-done((bf16[96,3584]{1,0:T(8,128)(2,1)S(1)}, bf16[96,3584]{1,0:T(8,128)(2,1)S(1)}, u32[]{:S(2)}, u32[]{:S(2)}) %collective-permute-start.6) | collective-permute-done | bytes 688160 | tf_op jit(solution)/shard_map/ppermute | solution.py:21
  38.1 2.4 %shard_map.87 = (bf16[48,3584]{1,0:T(8,128)(2,1)S(1)}, bf16[48,3584]{1,0:T(8,128)(2,1)S(1)}, bf16[48,3584]{1,0:T(8,128)(2,1)S(1)}, bf16[48,3584]{1,0:T(8,128)(2,...) custom-call(s32[1]{0:T(128)} %bitcast.me_ref, ...), custom_call_target="tpu_custom_call" | custom-call | flops 1 | bytes 1 | tf_op jit(solution)/shard_map/pallas_call | solution.py:190
  41.1 2.3 %collective-permute-done.11.refs_1_ = bf16[48,3584]{1,0:T(8,128)(2,1)S(1)} collective-permute-done((bf16[48,3584]{1,0:T(8,128)(2,1)S(1)}, bf16[48,3584]{1,0:T(8,128)(2,1)S(1)}, u32[]{:S(2)}, u32[]{:S(2)}) %collective-permute-start.11) | collective-permute-done | bytes 344096 | tf_op jit(solution)/shard_map/ppermute | solution.py:21
  45.1 1.7 %collective-permute-start.19 = (bf16[48,3584]{1,0:T(8,128)(2,1)S(1)}, bf16[48,3584]{1,0:T(8,128)(2,1)S(1)}, u32[]{:S(2)}, u32[]{:S(2)}) collective-permute-start(bf16[48,3584]{1,0:T(8,128)(2,1)S(1)} %get-tuple-element.106), channel_id=1, source_target_pairs={{0,4},{1,3},{2,6},{3,1},{4,0},{5,7},{6,2},{7,5},{8,12},{9,11},{10,... | collective-permute-start | bytes 1032200 | tf_op jit(solution)/shard_map/ppermute | solution.py:21
  47.9 1.6 %collective-permute-start.13 = (bf16[24,3584]{1,0:T(8,128)(2,1)S(1)}, bf16[24,3584]{1,0:T(8,128)(2,1)S(1)}, u32[]{:S(2)}, u32[]{:S(2)}) collective-permute-start(bf16[24,3584]{1,0:T(8,128)(2,1)S(1)} %add_convert_fusion.7), channel_id=1, source_target_pairs={{0,2},{1,5},{2,0},{3,7},{4,6},{5,1},{6,4},{7,3},{8,10},{9,13},{10,... | collective-permute-start | bytes 516104 | tf_op jit(solution)/shard_map/ppermute | solution.py:21
  49.4 4.4 %collective-permute-done.12 = bf16[48,3584]{1,0:T(8,128)(2,1)S(1)} collective-permute-done((bf16[48,3584]{1,0:T(8,128)(2,1)S(1)}, bf16[48,3584]{1,0:T(8,128)(2,1)S(1)}, u32[]{:S(2)}, u32[]{:S(2)}) %collective-permute-start.12) | collective-permute-done | bytes 344096 | tf_op jit(solution)/shard_map/ppermute | solution.py:21
  53.9 1.8 %collective-permute-start.17 = (bf16[24,3584]{1,0:T(8,128)(2,1)S(1)}, bf16[24,3584]{1,0:T(8,128)(2,1)S(1)}, u32[]{:S(2)}, u32[]{:S(2)}) collective-permute-start(bf16[24,3584]{1,0:T(8,128)(2,1)S(1)} %add_convert_fusion.6), channel_id=1, source_target_pairs={{0,2},{1,5},{2,0},{3,7},{4,6},{5,1},{6,4},{7,3},{8,10},{9,13},{10,... | collective-permute-start | bytes 516104 | tf_op jit(solution)/shard_map/ppermute | solution.py:21
  55.8 1.4 %collective-permute-start.16 = (bf16[24,3584]{1,0:T(8,128)(2,1)S(1)}, bf16[24,3584]{1,0:T(8,128)(2,1)S(1)}, u32[]{:S(2)}, u32[]{:S(2)}) collective-permute-start(bf16[24,3584]{1,0:T(8,128)(2,1)S(1)} %add_convert_fusion.5), channel_id=1, source_target_pairs={{0,24},{1,25},{2,26},{3,27},{4,28},{5,29},{6,30},{7,31},{8,16},{9,... | collective-permute-start | bytes 516104 | tf_op jit(solution)/shard_map/ppermute | solution.py:21
  57.9 1.5 %collective-permute-done.19 = bf16[48,3584]{1,0:T(8,128)(2,1)S(1)} collective-permute-done((bf16[48,3584]{1,0:T(8,128)(2,1)S(1)}, bf16[48,3584]{1,0:T(8,128)(2,1)S(1)}, u32[]{:S(2)}, u32[]{:S(2)}) %collective-permute-start.19) | collective-permute-done | bytes 344096 | tf_op jit(solution)/shard_map/ppermute | solution.py:21
  59.4 1.8 %collective-permute-start.20 = (bf16[24,3584]{1,0:T(8,128)(2,1)S(1)}, bf16[24,3584]{1,0:T(8,128)(2,1)S(1)}, u32[]{:S(2)}, u32[]{:S(2)}) collective-permute-start(bf16[24,3584]{1,0:T(8,128)(2,1)S(1)} %add_convert_fusion.2), channel_id=1, source_target_pairs={{0,2},{1,5},{2,0},{3,7},{4,6},{5,1},{6,4},{7,3},{8,10},{9,13},{10,... | collective-permute-start | bytes 516104 | tf_op jit(solution)/shard_map/ppermute | solution.py:21
  61.4 3.5 %collective-permute-done.20 = bf16[24,3584]{1,0:T(8,128)(2,1)S(1)} collective-permute-done((bf16[24,3584]{1,0:T(8,128)(2,1)S(1)}, bf16[24,3584]{1,0:T(8,128)(2,1)S(1)}, u32[]{:S(2)}, u32[]{:S(2)}) %collective-permute-start.20) | collective-permute-done | bytes 172064 | tf_op jit(solution)/shard_map/ppermute | solution.py:21
  66.2 2.1 %collective-permute-start.15 = (bf16[24,3584]{1,0:T(8,128)(2,1)S(1)}, bf16[24,3584]{1,0:T(8,128)(2,1)S(1)}, u32[]{:S(2)}, u32[]{:S(2)}) collective-permute-start(bf16[24,3584]{1,0:T(8,128)(2,1)S(1)} %add_convert_fusion.4), channel_id=1, source_target_pairs={{0,2},{1,5},{2,0},{3,7},{4,6},{5,1},{6,4},{7,3},{8,10},{9,13},{10,... | collective-permute-start | bytes 516104 | tf_op jit(solution)/shard_map/ppermute | solution.py:21
  69.6 3.1 %collective-permute-done.18.refs_2_ = bf16[24,3584]{1,0:T(8,128)(2,1)S(1)} collective-permute-done((bf16[24,3584]{1,0:T(8,128)(2,1)S(1)}, bf16[24,3584]{1,0:T(8,128)(2,1)S(1)}, u32[]{:S(2)}, u32[]{:S(2)}) %collective-permute-start.18) | collective-permute-done | bytes 172064 | tf_op jit(solution)/shard_map/ppermute | solution.py:21
  (56 shorter events, 12.5 us)
Async XLA Ops:
  3.1 8.1 %collective-permute-start = (bf16[24,3584]{1,0:T(8,128)(2,1)}, bf16[24,3584]{1,0:T(8,128)(2,1)S(1)}, u32[]{:S(2)}, u32[]{:S(2)}) collective-permute-start(bf16[24,3584]{1,0:T(8,128)(2,1)} %get-tuple-element.64), channel_id=1, source_target_pairs={{0,2},{1,5},{2,0},{3,7},{4,6},{5,1},{6,4},{7,3},{8,10},{9,13},{10,... | collective-permute-start | bytes 516104 | tf_op jit(solution)/shard_map/ppermute | solution.py:21
  6.1 9.3 %collective-permute-start.2 = (bf16[24,3584]{1,0:T(8,128)(2,1)}, bf16[24,3584]{1,0:T(8,128)(2,1)S(1)}, u32[]{:S(2)}, u32[]{:S(2)}) collective-permute-start(bf16[24,3584]{1,0:T(8,128)(2,1)} %get-tuple-element.67), channel_id=1, source_target_pairs={{0,24},{1,25},{2,26},{3,27},{4,28},{5,29},{6,30},{7,31},{8,16},{9,... | collective-permute-start | bytes 516104 | tf_op jit(solution)/shard_map/ppermute | solution.py:21
  9.7 8.1 %collective-permute-start.3 = (bf16[24,3584]{1,0:T(8,128)(2,1)}, bf16[24,3584]{1,0:T(8,128)(2,1)S(1)}, u32[]{:S(2)}, u32[]{:S(2)}) collective-permute-start(bf16[24,3584]{1,0:T(8,128)(2,1)} %get-tuple-element.72), channel_id=1, source_target_pairs={{0,8},{1,9},{2,10},{3,11},{4,12},{5,13},{6,14},{7,15},{8,0},{9,1},... | collective-permute-start | bytes 516104 | tf_op jit(solution)/shard_map/ppermute | solution.py:21
  9.7 26.7 %collective-permute-start.7 = (bf16[3584,256]{1,0:T(8,128)(2,1)}, bf16[3584,256]{1,0:T(8,128)(2,1)S(1)}, u32[]{:S(2)}, u32[]{:S(2)}) collective-permute-start(bf16[3584,256]{1,0:T(8,128)(2,1)} %bitcast.7), channel_id=1, source_target_pairs={{0,1},{1,0},{2,3},{3,2},{4,5},{5,4},{6,7},{7,6},{8,9},{9,8},{10,11... | collective-permute-start | bytes 5505032 | tf_op jit(solution)/shard_map/ppermute | solution.py:21
  9.7 26.7 %collective-permute-start.8 = (bf16[128,3584]{1,0:T(8,128)(2,1)}, bf16[128,3584]{1,0:T(8,128)(2,1)S(1)}, u32[]{:S(2)}, u32[]{:S(2)}) collective-permute-start(bf16[128,3584]{1,0:T(8,128)(2,1)} %bitcast.10), channel_id=1, source_target_pairs={{0,1},{1,0},{2,3},{3,2},{4,5},{5,4},{6,7},{7,6},{8,9},{9,8},{10,11... | collective-permute-start | bytes 2752520 | tf_op jit(solution)/shard_map/ppermute | solution.py:21
  11.2 25.2 %collective-permute-start.1 = (bf16[48,3584]{1,0:T(8,128)(2,1)S(1)}, bf16[48,3584]{1,0:T(8,128)(2,1)S(1)}, u32[]{:S(2)}, u32[]{:S(2)}) collective-permute-start(bf16[48,3584]{1,0:T(8,128)(2,1)S(1)} %constant_dynamic-update-slice_fusion.refs_0_), channel_id=1, source_target_pairs={{0,4},{1,3},{2,6},{3,1},{4,0},{5,7},{6,2},{7,5},{8,12},{9,11},{10,... | collective-permute-start | bytes 1032200 | tf_op jit(solution)/shard_map/ppermute | solution.py:21
  17.9 7.3 %collective-permute-start.4 = (bf16[48,3584]{1,0:T(8,128)(2,1)S(1)}, bf16[48,3584]{1,0:T(8,128)(2,1)S(1)}, u32[]{:S(2)}, u32[]{:S(2)}) collective-permute-start(bf16[48,3584]{1,0:T(8,128)(2,1)S(1)} %pad_maximum_fusion), channel_id=1, source_target_pairs={{0,2},{1,5},{2,0},{3,7},{4,6},{5,1},{6,4},{7,3},{8,10},{9,13},{10,... | collective-permute-start | bytes 1032200 | tf_op jit(solution)/shard_map/ppermute | solution.py:21
  19.4 9.5 %collective-permute-start.5 = (bf16[24,3584]{1,0:T(8,128)(2,1)}, bf16[24,3584]{1,0:T(8,128)(2,1)S(1)}, u32[]{:S(2)}, u32[]{:S(2)}) collective-permute-start(bf16[24,3584]{1,0:T(8,128)(2,1)} %get-tuple-element.79), channel_id=1, source_target_pairs={{0,16},{1,17},{2,18},{3,19},{4,20},{5,21},{6,22},{7,23},{8,24},{9,... | collective-permute-start | bytes 516104 | tf_op jit(solution)/shard_map/ppermute | solution.py:21
  25.2 12.8 %collective-permute-start.6 = (bf16[96,3584]{1,0:T(8,128)(2,1)S(1)}, bf16[96,3584]{1,0:T(8,128)(2,1)S(1)}, u32[]{:S(2)}, u32[]{:S(2)}) collective-permute-start(bf16[96,3584]{1,0:T(8,128)(2,1)S(1)} %constant_dynamic-update-slice_fusion.2.refs_2_), channel_id=1, source_target_pairs={{0,4},{1,3},{2,6},{3,1},{4,0},{5,7},{6,2},{7,5},{8,12},{9,11},{10,... | collective-permute-start | bytes 2064392 | tf_op jit(solution)/shard_map/ppermute | solution.py:21
  28.9 7.1 %collective-permute-start.9 = (bf16[24,3584]{1,0:T(8,128)(2,1)S(1)}, bf16[24,3584]{1,0:T(8,128)(2,1)S(1)}, u32[]{:S(2)}, u32[]{:S(2)}) collective-permute-start(bf16[24,3584]{1,0:T(8,128)(2,1)S(1)} %collective-permute-done.5), channel_id=1, source_target_pairs={{0,2},{1,5},{2,0},{3,7},{4,6},{5,1},{6,4},{7,3},{8,10},{9,13},{10,... | collective-permute-start | bytes 516104 | tf_op jit(solution)/shard_map/ppermute | solution.py:21
  36.1 7.3 %collective-permute-start.11 = (bf16[48,3584]{1,0:T(8,128)(2,1)S(1)}, bf16[48,3584]{1,0:T(8,128)(2,1)S(1)}, u32[]{:S(2)}, u32[]{:S(2)}) collective-permute-start(bf16[48,3584]{1,0:T(8,128)(2,1)S(1)} %constant_dynamic-update-slice_fusion.5.refs_0_), channel_id=1, source_target_pairs={{0,4},{1,3},{2,6},{3,1},{4,0},{5,7},{6,2},{7,5},{8,12},{9,11},{10,... | collective-permute-start | bytes 1032200 | tf_op jit(solution)/shard_map/ppermute | solution.py:21
  40.5 7.3 %collective-permute-start.10 = (bf16[48,3584]{1,0:T(8,128)(2,1)S(1)}, bf16[48,3584]{1,0:T(8,128)(2,1)S(1)}, u32[]{:S(2)}, u32[]{:S(2)}) collective-permute-start(bf16[48,3584]{1,0:T(8,128)(2,1)S(1)} %get-tuple-element.88), channel_id=1, source_target_pairs={{0,4},{1,3},{2,6},{3,1},{4,0},{5,7},{6,2},{7,5},{8,12},{9,11},{10,... | collective-permute-start | bytes 1032200 | tf_op jit(solution)/shard_map/ppermute | solution.py:21
  44.6 2.2 %collective-permute-start.22 = (bf16[16,24,128]{2,1,0:T(8,128)(2,1)S(1)}, bf16[16,24,128]{2,1,0:T(8,128)(2,1)S(1)}, u32[]{:S(2)}, u32[]{:S(2)}) collective-permute-start(bf16[16,24,128]{2,1,0:T(8,128)(2,1)S(1)} %get-tuple-element.119), channel_id=1, source_target_pairs={{0,1},{1,0},{2,3},{3,2},{4,5},{5,4},{6,7},{7,6},{8,9},{9,8},{10,11... | collective-permute-start | bytes 294920 | tf_op jit(solution)/shard_map/ppermute | solution.py:21
  44.7 9.2 %collective-permute-start.12 = (bf16[48,3584]{1,0:T(8,128)(2,1)S(1)}, bf16[48,3584]{1,0:T(8,128)(2,1)S(1)}, u32[]{:S(2)}, u32[]{:S(2)}) collective-permute-start(bf16[48,3584]{1,0:T(8,128)(2,1)S(1)} %get-tuple-element.97), channel_id=1, source_target_pairs={{0,4},{1,3},{2,6},{3,1},{4,0},{5,7},{6,2},{7,5},{8,12},{9,11},{10,... | collective-permute-start | bytes 1032200 | tf_op jit(solution)/shard_map/ppermute | solution.py:21
  45.1 14.3 %collective-permute-start.19 = (bf16[48,3584]{1,0:T(8,128)(2,1)S(1)}, bf16[48,3584]{1,0:T(8,128)(2,1)S(1)}, u32[]{:S(2)}, u32[]{:S(2)}) collective-permute-start(bf16[48,3584]{1,0:T(8,128)(2,1)S(1)} %get-tuple-element.106), channel_id=1, source_target_pairs={{0,4},{1,3},{2,6},{3,1},{4,0},{5,7},{6,2},{7,5},{8,12},{9,11},{10,... | collective-permute-start | bytes 1032200 | tf_op jit(solution)/shard_map/ppermute | solution.py:21
  46.8 21.4 %collective-permute-start.23 = (bf16[16,2,24,128]{3,2,1,0:T(8,128)(2,1)S(1)}, bf16[16,2,24,128]{3,2,1,0:T(8,128)(2,1)S(1)}, u32[]{:S(2)}, u32[]{:S(2)}) collective-permute-start(bf16[16,2,24,128]{3,2,1,0:T(8,128)(2,1)S(1)} %shard_map.90.mine_ref), channel_id=1, source_target_pairs={{0,16},{1,17},{2,18},{3,19},{4,20},{5,21},{6,22},{7,23},{8,24},{9,... | collective-permute-start | bytes 589832 | tf_op jit(solution)/shard_map/ppermute | solution.py:21
  47.9 7.8 %collective-permute-start.13 = (bf16[24,3584]{1,0:T(8,128)(2,1)S(1)}, bf16[24,3584]{1,0:T(8,128)(2,1)S(1)}, u32[]{:S(2)}, u32[]{:S(2)}) collective-permute-start(bf16[24,3584]{1,0:T(8,128)(2,1)S(1)} %add_convert_fusion.7), channel_id=1, source_target_pairs={{0,2},{1,5},{2,0},{3,7},{4,6},{5,1},{6,4},{7,3},{8,10},{9,13},{10,... | collective-permute-start | bytes 516104 | tf_op jit(solution)/shard_map/ppermute | solution.py:21
  53.9 7.3 %collective-permute-start.17 = (bf16[24,3584]{1,0:T(8,128)(2,1)S(1)}, bf16[24,3584]{1,0:T(8,128)(2,1)S(1)}, u32[]{:S(2)}, u32[]{:S(2)}) collective-permute-start(bf16[24,3584]{1,0:T(8,128)(2,1)S(1)} %add_convert_fusion.6), channel_id=1, source_target_pairs={{0,2},{1,5},{2,0},{3,7},{4,6},{5,1},{6,4},{7,3},{8,10},{9,13},{10,... | collective-permute-start | bytes 516104 | tf_op jit(solution)/shard_map/ppermute | solution.py:21
  55.8 13.8 %collective-permute-start.16 = (bf16[24,3584]{1,0:T(8,128)(2,1)S(1)}, bf16[24,3584]{1,0:T(8,128)(2,1)S(1)}, u32[]{:S(2)}, u32[]{:S(2)}) collective-permute-start(bf16[24,3584]{1,0:T(8,128)(2,1)S(1)} %add_convert_fusion.5), channel_id=1, source_target_pairs={{0,24},{1,25},{2,26},{3,27},{4,28},{5,29},{6,30},{7,31},{8,16},{9,... | collective-permute-start | bytes 516104 | tf_op jit(solution)/shard_map/ppermute | solution.py:21
  57.2 8.9 %collective-permute-start.14 = (bf16[48,3584]{1,0:T(8,128)(2,1)S(1)}, bf16[48,3584]{1,0:T(8,128)(2,1)S(1)}, u32[]{:S(2)}, u32[]{:S(2)}) collective-permute-start(bf16[48,3584]{1,0:T(8,128)(2,1)S(1)} %get-tuple-element.102), channel_id=1, source_target_pairs={{0,4},{1,3},{2,6},{3,1},{4,0},{5,7},{6,2},{7,5},{8,12},{9,11},{10,... | collective-permute-start | bytes 1032200 | tf_op jit(solution)/shard_map/ppermute | solution.py:21
  59.4 5.5 %collective-permute-start.20 = (bf16[24,3584]{1,0:T(8,128)(2,1)S(1)}, bf16[24,3584]{1,0:T(8,128)(2,1)S(1)}, u32[]{:S(2)}, u32[]{:S(2)}) collective-permute-start(bf16[24,3584]{1,0:T(8,128)(2,1)S(1)} %add_convert_fusion.2), channel_id=1, source_target_pairs={{0,2},{1,5},{2,0},{3,7},{4,6},{5,1},{6,4},{7,3},{8,10},{9,13},{10,... | collective-permute-start | bytes 516104 | tf_op jit(solution)/shard_map/ppermute | solution.py:21
  61.3 11.3 %collective-permute-start.18 = (bf16[24,3584]{1,0:T(8,128)(2,1)S(1)}, bf16[24,3584]{1,0:T(8,128)(2,1)S(1)}, u32[]{:S(2)}, u32[]{:S(2)}) collective-permute-start(bf16[24,3584]{1,0:T(8,128)(2,1)S(1)} %add_convert_fusion.3), channel_id=1, source_target_pairs={{0,16},{1,17},{2,18},{3,19},{4,20},{5,21},{6,22},{7,23},{8,24},{9,... | collective-permute-start | bytes 516104 | tf_op jit(solution)/shard_map/ppermute | solution.py:21
  65.0 8.7 %collective-permute-start.21 = (bf16[24,3584]{1,0:T(8,128)(2,1)S(1)}, bf16[24,3584]{1,0:T(8,128)(2,1)S(1)}, u32[]{:S(2)}, u32[]{:S(2)}) collective-permute-start(bf16[24,3584]{1,0:T(8,128)(2,1)S(1)} %add_convert_fusion.1), channel_id=1, source_target_pairs={{0,8},{1,9},{2,10},{3,11},{4,12},{5,13},{6,14},{7,15},{8,0},{9,1},... | collective-permute-start | bytes 516104 | tf_op jit(solution)/shard_map/ppermute | solution.py:21
  66.2 7.5 %collective-permute-start.15 = (bf16[24,3584]{1,0:T(8,128)(2,1)S(1)}, bf16[24,3584]{1,0:T(8,128)(2,1)S(1)}, u32[]{:S(2)}, u32[]{:S(2)}) collective-permute-start(bf16[24,3584]{1,0:T(8,128)(2,1)S(1)} %add_convert_fusion.4), channel_id=1, source_target_pairs={{0,2},{1,5},{2,0},{3,7},{4,6},{5,1},{6,4},{7,3},{8,10},{9,13},{10,... | collective-permute-start | bytes 516104 | tf_op jit(solution)/shard_map/ppermute | solution.py:21
  (5 other events, 119.1 us)

commit v7 on v6

--- a/solution.py
+++ b/solution.py
@@ -82,12 +82,6 @@
     pick = lax.dot_general(
         place_hot, token_hot.astype(jnp.bfloat16), contract, preferred_element_type=jnp.float32
     ).astype(jnp.bfloat16)
-    for k in range(tiles):
-        cols = pl.ds(k * tile, tile)
-        large[k].wait()
-        picked = jnp.dot(pick, tok_ref[:, cols], preferred_element_type=jnp.float32)
-        for s in range(experts):
-            bufs[s][:, cols] = picked[s * capacity : (s + 1) * capacity].astype(jnp.bfloat16)
     gate = gate_ref[...]
     gate_hi = gate.astype(jnp.bfloat16).astype(jnp.float32)
     for part, ref in ((gate_hi, hi_ref), (gate - gate_hi, lo_ref)):
@@ -97,6 +91,12 @@
             contract,
             preferred_element_type=jnp.float32,
         ).astype(jnp.bfloat16)
+    for k in range(tiles):
+        cols = pl.ds(k * tile, tile)
+        large[k].wait()
+        picked = jnp.dot(pick, tok_ref[:, cols], preferred_element_type=jnp.float32)
+        for s in range(experts):
+            bufs[s][:, cols] = picked[s * capacity : (s + 1) * capacity].astype(jnp.bfloat16)
 
 
 def run_route(experts, capacity, me, route_expert, route_token, route_gate, tokens):

time: 75.3 us -> 75.3 us (level)
  no operation moved by 1% of the time
where the time goes in v7:
time: 75.3 us; the launch traced here: 75.2 us
  waiting for transfers between devices  37 us (49%)
  starting transfers between devices  27.1 us (36%)
  Pallas kernels  8.81 us (12%)
  local copies, waits for them, and re-layouts  1.04 us (1%)
  between operations  0.83 us (1%)
    ppermute x24, waiting for transfers between devices, swap(): lax.ppermute(value, 'ep', [(i, i ^ mask_of(i)) for i in range(count)])  37 us
    ppermute x24, starting transfers between devices, swap(): lax.ppermute(value, 'ep', [(i, i ^ mask_of(i)) for i in range(count)])  27.1 us
    pallas_call x2, Pallas kernels, run_expert(): pl.pallas_call(functools.partial(expert_kernel, chunks, backs, ahead, fin...  3.63 us
    pallas_call x1, Pallas kernels, run_route(): pl.pallas_call(functools.partial(route_kernel, experts, capacity), out_sh...  2.45 us
  transfers between devices with their start and end apart: 24, of which 13 were waited for; matrix products, arithmetic and copies ran while one was open for 2% of the time, Pallas kernels for 7%

profile of v7, /device:TPU:0, one launch (start us, length us, event | category | flops | bytes accessed | tf_op | source)
XLA Modules:
  0.0 75.2 jit_solution(4631230751369930120)
XLA Ops:
  0.6 2.5 %shard_map.86 = (bf16[24,3584]{1,0:T(8,128)(2,1)}, bf16[24,3584]{1,0:T(8,128)(2,1)}, bf16[24,3584]{1,0:T(8,128)(2,1)}, bf16[24,3584]{1,0:T(8,128)(2,1)}, bf16[12...) custom-call(s32[1]{0:T(128)} %bitcast.me_ref, s32[1,64]{1,0:T(1,128)} %bitcast.14, s32[1,64]{1,0:T(1,128)} %bitcast.15, ...), custom_call_target="tpu_custom_call" | custom-call | tf_op jit(solution)/shard_map/pallas_call | solution.py:107
  3.1 3.0 %collective-permute-start = (bf16[24,3584]{1,0:T(8,128)(2,1)}, bf16[24,3584]{1,0:T(8,128)(2,1)S(1)}, u32[]{:S(2)}, u32[]{:S(2)}) collective-permute-start(bf16[24,3584]{1,0:T(8,128)(2,1)} %get-tuple-element.64), channel_id=1, source_target_pairs={{0,2},{1,5},{2,0},{3,7},{4,6},{5,1},{6,4},{7,3},{8,10},{9,13},{10,... | collective-permute-start | bytes 516104 | tf_op jit(solution)/shard_map/ppermute | solution.py:21
  6.1 3.6 %collective-permute-start.2 = (bf16[24,3584]{1,0:T(8,128)(2,1)}, bf16[24,3584]{1,0:T(8,128)(2,1)S(1)}, u32[]{:S(2)}, u32[]{:S(2)}) collective-permute-start(bf16[24,3584]{1,0:T(8,128)(2,1)} %get-tuple-element.67), channel_id=1, source_target_pairs={{0,24},{1,25},{2,26},{3,27},{4,28},{5,29},{6,30},{7,31},{8,16},{9,... | collective-permute-start | bytes 516104 | tf_op jit(solution)/shard_map/ppermute | solution.py:21
  11.2 1.6 %collective-permute-start.1 = (bf16[48,3584]{1,0:T(8,128)(2,1)S(1)}, bf16[48,3584]{1,0:T(8,128)(2,1)S(1)}, u32[]{:S(2)}, u32[]{:S(2)}) collective-permute-start(bf16[48,3584]{1,0:T(8,128)(2,1)S(1)} %constant_dynamic-update-slice_fusion.refs_0_), channel_id=1, source_target_pairs={{0,4},{1,3},{2,6},{3,1},{4,0},{5,7},{6,2},{7,5},{8,12},{9,11},{10,... | collective-permute-start | bytes 1032200 | tf_op jit(solution)/shard_map/ppermute | solution.py:21
  12.8 2.6 %collective-permute-done.2 = bf16[24,3584]{1,0:T(8,128)(2,1)S(1)} collective-permute-done((bf16[24,3584]{1,0:T(8,128)(2,1)}, bf16[24,3584]{1,0:T(8,128)(2,1)S(1)}, u32[]{:S(2)}, u32[]{:S(2)}) %collective-permute-start.2) | collective-permute-done | bytes 172064 | tf_op jit(solution)/shard_map/ppermute | solution.py:21
  15.4 2.4 %collective-permute-done.3 = bf16[24,3584]{1,0:T(8,128)(2,1)S(1)} collective-permute-done((bf16[24,3584]{1,0:T(8,128)(2,1)}, bf16[24,3584]{1,0:T(8,128)(2,1)S(1)}, u32[]{:S(2)}, u32[]{:S(2)}) %collective-permute-start.3) | collective-permute-done | bytes 172064 | tf_op jit(solution)/shard_map/ppermute | solution.py:21
  17.9 1.6 %collective-permute-start.4 = (bf16[48,3584]{1,0:T(8,128)(2,1)S(1)}, bf16[48,3584]{1,0:T(8,128)(2,1)S(1)}, u32[]{:S(2)}, u32[]{:S(2)}) collective-permute-start(bf16[48,3584]{1,0:T(8,128)(2,1)S(1)} %pad_maximum_fusion), channel_id=1, source_target_pairs={{0,2},{1,5},{2,0},{3,7},{4,6},{5,1},{6,4},{7,3},{8,10},{9,13},{10,... | collective-permute-start | bytes 1032200 | tf_op jit(solution)/shard_map/ppermute | solution.py:21
  20.1 5.1 %collective-permute-done.4 = bf16[48,3584]{1,0:T(8,128)(2,1)S(1)} collective-permute-done((bf16[48,3584]{1,0:T(8,128)(2,1)S(1)}, bf16[48,3584]{1,0:T(8,128)(2,1)S(1)}, u32[]{:S(2)}, u32[]{:S(2)}) %collective-permute-start.4) | collective-permute-done | bytes 344096 | tf_op jit(solution)/shard_map/ppermute | solution.py:21
  25.8 3.1 %collective-permute-done.5 = bf16[24,3584]{1,0:T(8,128)(2,1)S(1)} collective-permute-done((bf16[24,3584]{1,0:T(8,128)(2,1)}, bf16[24,3584]{1,0:T(8,128)(2,1)S(1)}, u32[]{:S(2)}, u32[]{:S(2)}) %collective-permute-start.5) | collective-permute-done | bytes 172064 | tf_op jit(solution)/shard_map/ppermute | solution.py:21
  28.9 1.7 %collective-permute-start.9 = (bf16[24,3584]{1,0:T(8,128)(2,1)S(1)}, bf16[24,3584]{1,0:T(8,128)(2,1)S(1)}, u32[]{:S(2)}, u32[]{:S(2)}) collective-permute-start(bf16[24,3584]{1,0:T(8,128)(2,1)S(1)} %collective-permute-done.5), channel_id=1, source_target_pairs={{0,2},{1,5},{2,0},{3,7},{4,6},{5,1},{6,4},{7,3},{8,10},{9,13},{10,... | collective-permute-start | bytes 516104 | tf_op jit(solution)/shard_map/ppermute | solution.py:21
  30.7 5.4 %collective-permute-done.9 = bf16[24,3584]{1,0:T(8,128)(2,1)S(1)} collective-permute-done((bf16[24,3584]{1,0:T(8,128)(2,1)S(1)}, bf16[24,3584]{1,0:T(8,128)(2,1)S(1)}, u32[]{:S(2)}, u32[]{:S(2)}) %collective-permute-start.9) | collective-permute-done | bytes 172064 | tf_op jit(solution)/shard_map/ppermute | solution.py:21
  36.4 1.6 %collective-permute-done.6.refs_3_ = bf16[96,3584]{1,0:T(8,128)(2,1)S(1)} collective-permute-done((bf16[96,3584]{1,0:T(8,128)(2,1)S(1)}, bf16[96,3584]{1,0:T(8,128)(2,1)S(1)}, u32[]{:S(2)}, u32[]{:S(2)}) %collective-permute-start.6) | collective-permute-done | bytes 688160 | tf_op jit(solution)/shard_map/ppermute | solution.py:21
  38.1 2.4 %shard_map.87 = (bf16[48,3584]{1,0:T(8,128)(2,1)S(1)}, bf16[48,3584]{1,0:T(8,128)(2,1)S(1)}, bf16[48,3584]{1,0:T(8,128)(2,1)S(1)}, bf16[48,3584]{1,0:T(8,128)(2,...) custom-call(s32[1]{0:T(128)} %bitcast.me_ref, ...), custom_call_target="tpu_custom_call" | custom-call | flops 1 | bytes 1 | tf_op jit(solution)/shard_map/pallas_call | solution.py:190
  41.1 2.3 %collective-permute-done.11.refs_1_ = bf16[48,3584]{1,0:T(8,128)(2,1)S(1)} collective-permute-done((bf16[48,3584]{1,0:T(8,128)(2,1)S(1)}, bf16[48,3584]{1,0:T(8,128)(2,1)S(1)}, u32[]{:S(2)}, u32[]{:S(2)}) %collective-permute-start.11) | collective-permute-done | bytes 344096 | tf_op jit(solution)/shard_map/ppermute | solution.py:21
  45.1 1.7 %collective-permute-start.19 = (bf16[48,3584]{1,0:T(8,128)(2,1)S(1)}, bf16[48,3584]{1,0:T(8,128)(2,1)S(1)}, u32[]{:S(2)}, u32[]{:S(2)}) collective-permute-start(bf16[48,3584]{1,0:T(8,128)(2,1)S(1)} %get-tuple-element.106), channel_id=1, source_target_pairs={{0,4},{1,3},{2,6},{3,1},{4,0},{5,7},{6,2},{7,5},{8,12},{9,11},{10,... | collective-permute-start | bytes 1032200 | tf_op jit(solution)/shard_map/ppermute | solution.py:21
  47.9 1.6 %collective-permute-start.13 = (bf16[24,3584]{1,0:T(8,128)(2,1)S(1)}, bf16[24,3584]{1,0:T(8,128)(2,1)S(1)}, u32[]{:S(2)}, u32[]{:S(2)}) collective-permute-start(bf16[24,3584]{1,0:T(8,128)(2,1)S(1)} %add_convert_fusion.7), channel_id=1, source_target_pairs={{0,2},{1,5},{2,0},{3,7},{4,6},{5,1},{6,4},{7,3},{8,10},{9,13},{10,... | collective-permute-start | bytes 516104 | tf_op jit(solution)/shard_map/ppermute | solution.py:21
  49.4 4.4 %collective-permute-done.12 = bf16[48,3584]{1,0:T(8,128)(2,1)S(1)} collective-permute-done((bf16[48,3584]{1,0:T(8,128)(2,1)S(1)}, bf16[48,3584]{1,0:T(8,128)(2,1)S(1)}, u32[]{:S(2)}, u32[]{:S(2)}) %collective-permute-start.12) | collective-permute-done | bytes 344096 | tf_op jit(solution)/shard_map/ppermute | solution.py:21
  53.9 1.8 %collective-permute-start.17 = (bf16[24,3584]{1,0:T(8,128)(2,1)S(1)}, bf16[24,3584]{1,0:T(8,128)(2,1)S(1)}, u32[]{:S(2)}, u32[]{:S(2)}) collective-permute-start(bf16[24,3584]{1,0:T(8,128)(2,1)S(1)} %add_convert_fusion.6), channel_id=1, source_target_pairs={{0,2},{1,5},{2,0},{3,7},{4,6},{5,1},{6,4},{7,3},{8,10},{9,13},{10,... | collective-permute-start | bytes 516104 | tf_op jit(solution)/shard_map/ppermute | solution.py:21
  55.8 1.4 %collective-permute-start.16 = (bf16[24,3584]{1,0:T(8,128)(2,1)S(1)}, bf16[24,3584]{1,0:T(8,128)(2,1)S(1)}, u32[]{:S(2)}, u32[]{:S(2)}) collective-permute-start(bf16[24,3584]{1,0:T(8,128)(2,1)S(1)} %add_convert_fusion.5), channel_id=1, source_target_pairs={{0,24},{1,25},{2,26},{3,27},{4,28},{5,29},{6,30},{7,31},{8,16},{9,... | collective-permute-start | bytes 516104 | tf_op jit(solution)/shard_map/ppermute | solution.py:21
  58.0 1.4 %collective-permute-done.19 = bf16[48,3584]{1,0:T(8,128)(2,1)S(1)} collective-permute-done((bf16[48,3584]{1,0:T(8,128)(2,1)S(1)}, bf16[48,3584]{1,0:T(8,128)(2,1)S(1)}, u32[]{:S(2)}, u32[]{:S(2)}) %collective-permute-start.19) | collective-permute-done | bytes 344096 | tf_op jit(solution)/shard_map/ppermute | solution.py:21
  59.4 1.8 %collective-permute-start.20 = (bf16[24,3584]{1,0:T(8,128)(2,1)S(1)}, bf16[24,3584]{1,0:T(8,128)(2,1)S(1)}, u32[]{:S(2)}, u32[]{:S(2)}) collective-permute-start(bf16[24,3584]{1,0:T(8,128)(2,1)S(1)} %add_convert_fusion.2), channel_id=1, source_target_pairs={{0,2},{1,5},{2,0},{3,7},{4,6},{5,1},{6,4},{7,3},{8,10},{9,13},{10,... | collective-permute-start | bytes 516104 | tf_op jit(solution)/shard_map/ppermute | solution.py:21
  61.4 3.5 %collective-permute-done.20 = bf16[24,3584]{1,0:T(8,128)(2,1)S(1)} collective-permute-done((bf16[24,3584]{1,0:T(8,128)(2,1)S(1)}, bf16[24,3584]{1,0:T(8,128)(2,1)S(1)}, u32[]{:S(2)}, u32[]{:S(2)}) %collective-permute-start.20) | collective-permute-done | bytes 172064 | tf_op jit(solution)/shard_map/ppermute | solution.py:21
  66.2 2.1 %collective-permute-start.15 = (bf16[24,3584]{1,0:T(8,128)(2,1)S(1)}, bf16[24,3584]{1,0:T(8,128)(2,1)S(1)}, u32[]{:S(2)}, u32[]{:S(2)}) collective-permute-start(bf16[24,3584]{1,0:T(8,128)(2,1)S(1)} %add_convert_fusion.4), channel_id=1, source_target_pairs={{0,2},{1,5},{2,0},{3,7},{4,6},{5,1},{6,4},{7,3},{8,10},{9,13},{10,... | collective-permute-start | bytes 516104 | tf_op jit(solution)/shard_map/ppermute | solution.py:21
  69.6 3.1 %collective-permute-done.18.refs_2_ = bf16[24,3584]{1,0:T(8,128)(2,1)S(1)} collective-permute-done((bf16[24,3584]{1,0:T(8,128)(2,1)S(1)}, bf16[24,3584]{1,0:T(8,128)(2,1)S(1)}, u32[]{:S(2)}, u32[]{:S(2)}) %collective-permute-start.18) | collective-permute-done | bytes 172064 | tf_op jit(solution)/shard_map/ppermute | solution.py:21
  (56 shorter events, 12.6 us)
Async XLA Ops:
  3.1 8.1 %collective-permute-start = (bf16[24,3584]{1,0:T(8,128)(2,1)}, bf16[24,3584]{1,0:T(8,128)(2,1)S(1)}, u32[]{:S(2)}, u32[]{:S(2)}) collective-permute-start(bf16[24,3584]{1,0:T(8,128)(2,1)} %get-tuple-element.64), channel_id=1, source_target_pairs={{0,2},{1,5},{2,0},{3,7},{4,6},{5,1},{6,4},{7,3},{8,10},{9,13},{10,... | collective-permute-start | bytes 516104 | tf_op jit(solution)/shard_map/ppermute | solution.py:21
  6.1 9.3 %collective-permute-start.2 = (bf16[24,3584]{1,0:T(8,128)(2,1)}, bf16[24,3584]{1,0:T(8,128)(2,1)S(1)}, u32[]{:S(2)}, u32[]{:S(2)}) collective-permute-start(bf16[24,3584]{1,0:T(8,128)(2,1)} %get-tuple-element.67), channel_id=1, source_target_pairs={{0,24},{1,25},{2,26},{3,27},{4,28},{5,29},{6,30},{7,31},{8,16},{9,... | collective-permute-start | bytes 516104 | tf_op jit(solution)/shard_map/ppermute | solution.py:21
  9.7 8.1 %collective-permute-start.3 = (bf16[24,3584]{1,0:T(8,128)(2,1)}, bf16[24,3584]{1,0:T(8,128)(2,1)S(1)}, u32[]{:S(2)}, u32[]{:S(2)}) collective-permute-start(bf16[24,3584]{1,0:T(8,128)(2,1)} %get-tuple-element.72), channel_id=1, source_target_pairs={{0,8},{1,9},{2,10},{3,11},{4,12},{5,13},{6,14},{7,15},{8,0},{9,1},... | collective-permute-start | bytes 516104 | tf_op jit(solution)/shard_map/ppermute | solution.py:21
  9.7 26.7 %collective-permute-start.7 = (bf16[3584,256]{1,0:T(8,128)(2,1)}, bf16[3584,256]{1,0:T(8,128)(2,1)S(1)}, u32[]{:S(2)}, u32[]{:S(2)}) collective-permute-start(bf16[3584,256]{1,0:T(8,128)(2,1)} %bitcast.7), channel_id=1, source_target_pairs={{0,1},{1,0},{2,3},{3,2},{4,5},{5,4},{6,7},{7,6},{8,9},{9,8},{10,11... | collective-permute-start | bytes 5505032 | tf_op jit(solution)/shard_map/ppermute | solution.py:21
  9.7 26.7 %collective-permute-start.8 = (bf16[128,3584]{1,0:T(8,128)(2,1)}, bf16[128,3584]{1,0:T(8,128)(2,1)S(1)}, u32[]{:S(2)}, u32[]{:S(2)}) collective-permute-start(bf16[128,3584]{1,0:T(8,128)(2,1)} %bitcast.10), channel_id=1, source_target_pairs={{0,1},{1,0},{2,3},{3,2},{4,5},{5,4},{6,7},{7,6},{8,9},{9,8},{10,11... | collective-permute-start | bytes 2752520 | tf_op jit(solution)/shard_map/ppermute | solution.py:21
  11.2 25.2 %collective-permute-start.1 = (bf16[48,3584]{1,0:T(8,128)(2,1)S(1)}, bf16[48,3584]{1,0:T(8,128)(2,1)S(1)}, u32[]{:S(2)}, u32[]{:S(2)}) collective-permute-start(bf16[48,3584]{1,0:T(8,128)(2,1)S(1)} %constant_dynamic-update-slice_fusion.refs_0_), channel_id=1, source_target_pairs={{0,4},{1,3},{2,6},{3,1},{4,0},{5,7},{6,2},{7,5},{8,12},{9,11},{10,... | collective-permute-start | bytes 1032200 | tf_op jit(solution)/shard_map/ppermute | solution.py:21
  17.9 7.3 %collective-permute-start.4 = (bf16[48,3584]{1,0:T(8,128)(2,1)S(1)}, bf16[48,3584]{1,0:T(8,128)(2,1)S(1)}, u32[]{:S(2)}, u32[]{:S(2)}) collective-permute-start(bf16[48,3584]{1,0:T(8,128)(2,1)S(1)} %pad_maximum_fusion), channel_id=1, source_target_pairs={{0,2},{1,5},{2,0},{3,7},{4,6},{5,1},{6,4},{7,3},{8,10},{9,13},{10,... | collective-permute-start | bytes 1032200 | tf_op jit(solution)/shard_map/ppermute | solution.py:21
  19.4 9.5 %collective-permute-start.5 = (bf16[24,3584]{1,0:T(8,128)(2,1)}, bf16[24,3584]{1,0:T(8,128)(2,1)S(1)}, u32[]{:S(2)}, u32[]{:S(2)}) collective-permute-start(bf16[24,3584]{1,0:T(8,128)(2,1)} %get-tuple-element.79), channel_id=1, source_target_pairs={{0,16},{1,17},{2,18},{3,19},{4,20},{5,21},{6,22},{7,23},{8,24},{9,... | collective-permute-start | bytes 516104 | tf_op jit(solution)/shard_map/ppermute | solution.py:21
  25.2 12.8 %collective-permute-start.6 = (bf16[96,3584]{1,0:T(8,128)(2,1)S(1)}, bf16[96,3584]{1,0:T(8,128)(2,1)S(1)}, u32[]{:S(2)}, u32[]{:S(2)}) collective-permute-start(bf16[96,3584]{1,0:T(8,128)(2,1)S(1)} %constant_dynamic-update-slice_fusion.2.refs_2_), channel_id=1, source_target_pairs={{0,4},{1,3},{2,6},{3,1},{4,0},{5,7},{6,2},{7,5},{8,12},{9,11},{10,... | collective-permute-start | bytes 2064392 | tf_op jit(solution)/shard_map/ppermute | solution.py:21
  28.9 7.1 %collective-permute-start.9 = (bf16[24,3584]{1,0:T(8,128)(2,1)S(1)}, bf16[24,3584]{1,0:T(8,128)(2,1)S(1)}, u32[]{:S(2)}, u32[]{:S(2)}) collective-permute-start(bf16[24,3584]{1,0:T(8,128)(2,1)S(1)} %collective-permute-done.5), channel_id=1, source_target_pairs={{0,2},{1,5},{2,0},{3,7},{4,6},{5,1},{6,4},{7,3},{8,10},{9,13},{10,... | collective-permute-start | bytes 516104 | tf_op jit(solution)/shard_map/ppermute | solution.py:21
  36.1 7.3 %collective-permute-start.11 = (bf16[48,3584]{1,0:T(8,128)(2,1)S(1)}, bf16[48,3584]{1,0:T(8,128)(2,1)S(1)}, u32[]{:S(2)}, u32[]{:S(2)}) collective-permute-start(bf16[48,3584]{1,0:T(8,128)(2,1)S(1)} %constant_dynamic-update-slice_fusion.5.refs_0_), channel_id=1, source_target_pairs={{0,4},{1,3},{2,6},{3,1},{4,0},{5,7},{6,2},{7,5},{8,12},{9,11},{10,... | collective-permute-start | bytes 1032200 | tf_op jit(solution)/shard_map/ppermute | solution.py:21
  40.5 7.3 %collective-permute-start.10 = (bf16[48,3584]{1,0:T(8,128)(2,1)S(1)}, bf16[48,3584]{1,0:T(8,128)(2,1)S(1)}, u32[]{:S(2)}, u32[]{:S(2)}) collective-permute-start(bf16[48,3584]{1,0:T(8,128)(2,1)S(1)} %get-tuple-element.88), channel_id=1, source_target_pairs={{0,4},{1,3},{2,6},{3,1},{4,0},{5,7},{6,2},{7,5},{8,12},{9,11},{10,... | collective-permute-start | bytes 1032200 | tf_op jit(solution)/shard_map/ppermute | solution.py:21
  44.6 2.2 %collective-permute-start.22 = (bf16[16,24,128]{2,1,0:T(8,128)(2,1)S(1)}, bf16[16,24,128]{2,1,0:T(8,128)(2,1)S(1)}, u32[]{:S(2)}, u32[]{:S(2)}) collective-permute-start(bf16[16,24,128]{2,1,0:T(8,128)(2,1)S(1)} %get-tuple-element.119), channel_id=1, source_target_pairs={{0,1},{1,0},{2,3},{3,2},{4,5},{5,4},{6,7},{7,6},{8,9},{9,8},{10,11... | collective-permute-start | bytes 294920 | tf_op jit(solution)/shard_map/ppermute | solution.py:21
  44.7 9.2 %collective-permute-start.12 = (bf16[48,3584]{1,0:T(8,128)(2,1)S(1)}, bf16[48,3584]{1,0:T(8,128)(2,1)S(1)}, u32[]{:S(2)}, u32[]{:S(2)}) collective-permute-start(bf16[48,3584]{1,0:T(8,128)(2,1)S(1)} %get-tuple-element.97), channel_id=1, source_target_pairs={{0,4},{1,3},{2,6},{3,1},{4,0},{5,7},{6,2},{7,5},{8,12},{9,11},{10,... | collective-permute-start | bytes 1032200 | tf_op jit(solution)/shard_map/ppermute | solution.py:21
  45.1 14.3 %collective-permute-start.19 = (bf16[48,3584]{1,0:T(8,128)(2,1)S(1)}, bf16[48,3584]{1,0:T(8,128)(2,1)S(1)}, u32[]{:S(2)}, u32[]{:S(2)}) collective-permute-start(bf16[48,3584]{1,0:T(8,128)(2,1)S(1)} %get-tuple-element.106), channel_id=1, source_target_pairs={{0,4},{1,3},{2,6},{3,1},{4,0},{5,7},{6,2},{7,5},{8,12},{9,11},{10,... | collective-permute-start | bytes 1032200 | tf_op jit(solution)/shard_map/ppermute | solution.py:21
  46.8 21.5 %collective-permute-start.23 = (bf16[16,2,24,128]{3,2,1,0:T(8,128)(2,1)S(1)}, bf16[16,2,24,128]{3,2,1,0:T(8,128)(2,1)S(1)}, u32[]{:S(2)}, u32[]{:S(2)}) collective-permute-start(bf16[16,2,24,128]{3,2,1,0:T(8,128)(2,1)S(1)} %shard_map.90.mine_ref), channel_id=1, source_target_pairs={{0,16},{1,17},{2,18},{3,19},{4,20},{5,21},{6,22},{7,23},{8,24},{9,... | collective-permute-start | bytes 589832 | tf_op jit(solution)/shard_map/ppermute | solution.py:21
  47.9 7.8 %collective-permute-start.13 = (bf16[24,3584]{1,0:T(8,128)(2,1)S(1)}, bf16[24,3584]{1,0:T(8,128)(2,1)S(1)}, u32[]{:S(2)}, u32[]{:S(2)}) collective-permute-start(bf16[24,3584]{1,0:T(8,128)(2,1)S(1)} %add_convert_fusion.7), channel_id=1, source_target_pairs={{0,2},{1,5},{2,0},{3,7},{4,6},{5,1},{6,4},{7,3},{8,10},{9,13},{10,... | collective-permute-start | bytes 516104 | tf_op jit(solution)/shard_map/ppermute | solution.py:21
  53.9 7.3 %collective-permute-start.17 = (bf16[24,3584]{1,0:T(8,128)(2,1)S(1)}, bf16[24,3584]{1,0:T(8,128)(2,1)S(1)}, u32[]{:S(2)}, u32[]{:S(2)}) collective-permute-start(bf16[24,3584]{1,0:T(8,128)(2,1)S(1)} %add_convert_fusion.6), channel_id=1, source_target_pairs={{0,2},{1,5},{2,0},{3,7},{4,6},{5,1},{6,4},{7,3},{8,10},{9,13},{10,... | collective-permute-start | bytes 516104 | tf_op jit(solution)/shard_map/ppermute | solution.py:21
  55.8 13.8 %collective-permute-start.16 = (bf16[24,3584]{1,0:T(8,128)(2,1)S(1)}, bf16[24,3584]{1,0:T(8,128)(2,1)S(1)}, u32[]{:S(2)}, u32[]{:S(2)}) collective-permute-start(bf16[24,3584]{1,0:T(8,128)(2,1)S(1)} %add_convert_fusion.5), channel_id=1, source_target_pairs={{0,24},{1,25},{2,26},{3,27},{4,28},{5,29},{6,30},{7,31},{8,16},{9,... | collective-permute-start | bytes 516104 | tf_op jit(solution)/shard_map/ppermute | solution.py:21
  57.2 8.9 %collective-permute-start.14 = (bf16[48,3584]{1,0:T(8,128)(2,1)S(1)}, bf16[48,3584]{1,0:T(8,128)(2,1)S(1)}, u32[]{:S(2)}, u32[]{:S(2)}) collective-permute-start(bf16[48,3584]{1,0:T(8,128)(2,1)S(1)} %get-tuple-element.102), channel_id=1, source_target_pairs={{0,4},{1,3},{2,6},{3,1},{4,0},{5,7},{6,2},{7,5},{8,12},{9,11},{10,... | collective-permute-start | bytes 1032200 | tf_op jit(solution)/shard_map/ppermute | solution.py:21
  59.4 5.5 %collective-permute-start.20 = (bf16[24,3584]{1,0:T(8,128)(2,1)S(1)}, bf16[24,3584]{1,0:T(8,128)(2,1)S(1)}, u32[]{:S(2)}, u32[]{:S(2)}) collective-permute-start(bf16[24,3584]{1,0:T(8,128)(2,1)S(1)} %add_convert_fusion.2), channel_id=1, source_target_pairs={{0,2},{1,5},{2,0},{3,7},{4,6},{5,1},{6,4},{7,3},{8,10},{9,13},{10,... | collective-permute-start | bytes 516104 | tf_op jit(solution)/shard_map/ppermute | solution.py:21
  61.3 11.3 %collective-permute-start.18 = (bf16[24,3584]{1,0:T(8,128)(2,1)S(1)}, bf16[24,3584]{1,0:T(8,128)(2,1)S(1)}, u32[]{:S(2)}, u32[]{:S(2)}) collective-permute-start(bf16[24,3584]{1,0:T(8,128)(2,1)S(1)} %add_convert_fusion.3), channel_id=1, source_target_pairs={{0,16},{1,17},{2,18},{3,19},{4,20},{5,21},{6,22},{7,23},{8,24},{9,... | collective-permute-start | bytes 516104 | tf_op jit(solution)/shard_map/ppermute | solution.py:21
  65.0 8.7 %collective-permute-start.21 = (bf16[24,3584]{1,0:T(8,128)(2,1)S(1)}, bf16[24,3584]{1,0:T(8,128)(2,1)S(1)}, u32[]{:S(2)}, u32[]{:S(2)}) collective-permute-start(bf16[24,3584]{1,0:T(8,128)(2,1)S(1)} %add_convert_fusion.1), channel_id=1, source_target_pairs={{0,8},{1,9},{2,10},{3,11},{4,12},{5,13},{6,14},{7,15},{8,0},{9,1},... | collective-permute-start | bytes 516104 | tf_op jit(solution)/shard_map/ppermute | solution.py:21
  66.2 7.5 %collective-permute-start.15 = (bf16[24,3584]{1,0:T(8,128)(2,1)S(1)}, bf16[24,3584]{1,0:T(8,128)(2,1)S(1)}, u32[]{:S(2)}, u32[]{:S(2)}) collective-permute-start(bf16[24,3584]{1,0:T(8,128)(2,1)S(1)} %add_convert_fusion.4), channel_id=1, source_target_pairs={{0,2},{1,5},{2,0},{3,7},{4,6},{5,1},{6,4},{7,3},{8,10},{9,13},{10,... | collective-permute-start | bytes 516104 | tf_op jit(solution)/shard_map/ppermute | solution.py:21
  (5 other events, 119.1 us)

commit v8 on v7

--- a/solution.py
+++ b/solution.py
@@ -215,7 +215,7 @@
 def mix_kernel(hi_ref, lo_ref, *refs):
     values, out, (stage_ref, sems) = refs[:-3], refs[-3], refs[-2:]
     width = stage_ref.shape[1]
-    tile = column_tile(width)
+    tile = width // sems.shape[0]
     copies = []
     for k in range(width // tile):
         cols = pl.ds(k * tile, tile)
@@ -376,7 +376,7 @@
         out_specs=ANY,
         scratch_shapes=[
             pltpu.VMEM((tok_count, width), jnp.bfloat16),
-            pltpu.SemaphoreType.DMA((width // column_tile(width),)),
+            pltpu.SemaphoreType.DMA((max(1, width // 896),)),
         ],
         compiler_params=small,
     )(gate_hi, gate_lo, *finals)

time: 75.3 us -> 75.3 us (level)
  no operation moved by 1% of the time
where the time goes in v8:
time: 75.3 us; the launch traced here: 75.1 us
  waiting for transfers between devices  37 us (49%)
  starting transfers between devices  27.1 us (36%)
  Pallas kernels  8.74 us (12%)
  local copies, waits for them, and re-layouts  1.04 us (1%)
  between operations  0.83 us (1%)
    ppermute x24, waiting for transfers between devices, swap(): lax.ppermute(value, 'ep', [(i, i ^ mask_of(i)) for i in range(count)])  37 us
    ppermute x24, starting transfers between devices, swap(): lax.ppermute(value, 'ep', [(i, i ^ mask_of(i)) for i in range(count)])  27.1 us
    pallas_call x2, Pallas kernels, run_expert(): pl.pallas_call(functools.partial(expert_kernel, chunks, backs, ahead, fin...  3.63 us
    pallas_call x1, Pallas kernels, run_route(): pl.pallas_call(functools.partial(route_kernel, experts, capacity), out_sh...  2.45 us
  transfers between devices with their start and end apart: 24, of which 13 were waited for; matrix products, arithmetic and copies ran while one was open for 2% of the time, Pallas kernels for 7%

profile of v8, /device:TPU:0, one launch (start us, length us, event | category | flops | bytes accessed | tf_op | source)
XLA Modules:
  0.0 75.1 jit_solution(14153499594149139161)
XLA Ops:
  0.6 2.5 %shard_map.86 = (bf16[24,3584]{1,0:T(8,128)(2,1)}, bf16[24,3584]{1,0:T(8,128)(2,1)}, bf16[24,3584]{1,0:T(8,128)(2,1)}, bf16[24,3584]{1,0:T(8,128)(2,1)}, bf16[12...) custom-call(s32[1]{0:T(128)} %bitcast.me_ref, s32[1,64]{1,0:T(1,128)} %bitcast.14, s32[1,64]{1,0:T(1,128)} %bitcast.15, ...), custom_call_target="tpu_custom_call" | custom-call | tf_op jit(solution)/shard_map/pallas_call | solution.py:107
  3.1 3.0 %collective-permute-start = (bf16[24,3584]{1,0:T(8,128)(2,1)}, bf16[24,3584]{1,0:T(8,128)(2,1)S(1)}, u32[]{:S(2)}, u32[]{:S(2)}) collective-permute-start(bf16[24,3584]{1,0:T(8,128)(2,1)} %get-tuple-element.64), channel_id=1, source_target_pairs={{0,2},{1,5},{2,0},{3,7},{4,6},{5,1},{6,4},{7,3},{8,10},{9,13},{10,... | collective-permute-start | bytes 516104 | tf_op jit(solution)/shard_map/ppermute | solution.py:21
  6.1 3.6 %collective-permute-start.2 = (bf16[24,3584]{1,0:T(8,128)(2,1)}, bf16[24,3584]{1,0:T(8,128)(2,1)S(1)}, u32[]{:S(2)}, u32[]{:S(2)}) collective-permute-start(bf16[24,3584]{1,0:T(8,128)(2,1)} %get-tuple-element.67), channel_id=1, source_target_pairs={{0,24},{1,25},{2,26},{3,27},{4,28},{5,29},{6,30},{7,31},{8,16},{9,... | collective-permute-start | bytes 516104 | tf_op jit(solution)/shard_map/ppermute | solution.py:21
  11.2 1.6 %collective-permute-start.1 = (bf16[48,3584]{1,0:T(8,128)(2,1)S(1)}, bf16[48,3584]{1,0:T(8,128)(2,1)S(1)}, u32[]{:S(2)}, u32[]{:S(2)}) collective-permute-start(bf16[48,3584]{1,0:T(8,128)(2,1)S(1)} %constant_dynamic-update-slice_fusion.refs_0_), channel_id=1, source_target_pairs={{0,4},{1,3},{2,6},{3,1},{4,0},{5,7},{6,2},{7,5},{8,12},{9,11},{10,... | collective-permute-start | bytes 1032200 | tf_op jit(solution)/shard_map/ppermute | solution.py:21
  12.8 2.6 %collective-permute-done.2 = bf16[24,3584]{1,0:T(8,128)(2,1)S(1)} collective-permute-done((bf16[24,3584]{1,0:T(8,128)(2,1)}, bf16[24,3584]{1,0:T(8,128)(2,1)S(1)}, u32[]{:S(2)}, u32[]{:S(2)}) %collective-permute-start.2) | collective-permute-done | bytes 172064 | tf_op jit(solution)/shard_map/ppermute | solution.py:21
  15.4 2.4 %collective-permute-done.3 = bf16[24,3584]{1,0:T(8,128)(2,1)S(1)} collective-permute-done((bf16[24,3584]{1,0:T(8,128)(2,1)}, bf16[24,3584]{1,0:T(8,128)(2,1)S(1)}, u32[]{:S(2)}, u32[]{:S(2)}) %collective-permute-start.3) | collective-permute-done | bytes 172064 | tf_op jit(solution)/shard_map/ppermute | solution.py:21
  17.9 1.6 %collective-permute-start.4 = (bf16[48,3584]{1,0:T(8,128)(2,1)S(1)}, bf16[48,3584]{1,0:T(8,128)(2,1)S(1)}, u32[]{:S(2)}, u32[]{:S(2)}) collective-permute-start(bf16[48,3584]{1,0:T(8,128)(2,1)S(1)} %pad_maximum_fusion), channel_id=1, source_target_pairs={{0,2},{1,5},{2,0},{3,7},{4,6},{5,1},{6,4},{7,3},{8,10},{9,13},{10,... | collective-permute-start | bytes 1032200 | tf_op jit(solution)/shard_map/ppermute | solution.py:21
  20.1 5.1 %collective-permute-done.4 = bf16[48,3584]{1,0:T(8,128)(2,1)S(1)} collective-permute-done((bf16[48,3584]{1,0:T(8,128)(2,1)S(1)}, bf16[48,3584]{1,0:T(8,128)(2,1)S(1)}, u32[]{:S(2)}, u32[]{:S(2)}) %collective-permute-start.4) | collective-permute-done | bytes 344096 | tf_op jit(solution)/shard_map/ppermute | solution.py:21
  25.8 3.1 %collective-permute-done.5 = bf16[24,3584]{1,0:T(8,128)(2,1)S(1)} collective-permute-done((bf16[24,3584]{1,0:T(8,128)(2,1)}, bf16[24,3584]{1,0:T(8,128)(2,1)S(1)}, u32[]{:S(2)}, u32[]{:S(2)}) %collective-permute-start.5) | collective-permute-done | bytes 172064 | tf_op jit(solution)/shard_map/ppermute | solution.py:21
  28.9 1.7 %collective-permute-start.9 = (bf16[24,3584]{1,0:T(8,128)(2,1)S(1)}, bf16[24,3584]{1,0:T(8,128)(2,1)S(1)}, u32[]{:S(2)}, u32[]{:S(2)}) collective-permute-start(bf16[24,3584]{1,0:T(8,128)(2,1)S(1)} %collective-permute-done.5), channel_id=1, source_target_pairs={{0,2},{1,5},{2,0},{3,7},{4,6},{5,1},{6,4},{7,3},{8,10},{9,13},{10,... | collective-permute-start | bytes 516104 | tf_op jit(solution)/shard_map/ppermute | solution.py:21
  30.7 5.4 %collective-permute-done.9 = bf16[24,3584]{1,0:T(8,128)(2,1)S(1)} collective-permute-done((bf16[24,3584]{1,0:T(8,128)(2,1)S(1)}, bf16[24,3584]{1,0:T(8,128)(2,1)S(1)}, u32[]{:S(2)}, u32[]{:S(2)}) %collective-permute-start.9) | collective-permute-done | bytes 172064 | tf_op jit(solution)/shard_map/ppermute | solution.py:21
  36.4 1.6 %collective-permute-done.6.refs_3_ = bf16[96,3584]{1,0:T(8,128)(2,1)S(1)} collective-permute-done((bf16[96,3584]{1,0:T(8,128)(2,1)S(1)}, bf16[96,3584]{1,0:T(8,128)(2,1)S(1)}, u32[]{:S(2)}, u32[]{:S(2)}) %collective-permute-start.6) | collective-permute-done | bytes 688160 | tf_op jit(solution)/shard_map/ppermute | solution.py:21
  38.1 2.4 %shard_map.87 = (bf16[48,3584]{1,0:T(8,128)(2,1)S(1)}, bf16[48,3584]{1,0:T(8,128)(2,1)S(1)}, bf16[48,3584]{1,0:T(8,128)(2,1)S(1)}, bf16[48,3584]{1,0:T(8,128)(2,...) custom-call(s32[1]{0:T(128)} %bitcast.me_ref, ...), custom_call_target="tpu_custom_call" | custom-call | flops 1 | bytes 1 | tf_op jit(solution)/shard_map/pallas_call | solution.py:190
  41.1 2.3 %collective-permute-done.11.refs_1_ = bf16[48,3584]{1,0:T(8,128)(2,1)S(1)} collective-permute-done((bf16[48,3584]{1,0:T(8,128)(2,1)S(1)}, bf16[48,3584]{1,0:T(8,128)(2,1)S(1)}, u32[]{:S(2)}, u32[]{:S(2)}) %collective-permute-start.11) | collective-permute-done | bytes 344096 | tf_op jit(solution)/shard_map/ppermute | solution.py:21
  45.1 1.7 %collective-permute-start.19 = (bf16[48,3584]{1,0:T(8,128)(2,1)S(1)}, bf16[48,3584]{1,0:T(8,128)(2,1)S(1)}, u32[]{:S(2)}, u32[]{:S(2)}) collective-permute-start(bf16[48,3584]{1,0:T(8,128)(2,1)S(1)} %get-tuple-element.106), channel_id=1, source_target_pairs={{0,4},{1,3},{2,6},{3,1},{4,0},{5,7},{6,2},{7,5},{8,12},{9,11},{10,... | collective-permute-start | bytes 1032200 | tf_op jit(solution)/shard_map/ppermute | solution.py:21
  47.9 1.6 %collective-permute-start.13 = (bf16[24,3584]{1,0:T(8,128)(2,1)S(1)}, bf16[24,3584]{1,0:T(8,128)(2,1)S(1)}, u32[]{:S(2)}, u32[]{:S(2)}) collective-permute-start(bf16[24,3584]{1,0:T(8,128)(2,1)S(1)} %add_convert_fusion.7), channel_id=1, source_target_pairs={{0,2},{1,5},{2,0},{3,7},{4,6},{5,1},{6,4},{7,3},{8,10},{9,13},{10,... | collective-permute-start | bytes 516104 | tf_op jit(solution)/shard_map/ppermute | solution.py:21
  49.4 4.4 %collective-permute-done.12 = bf16[48,3584]{1,0:T(8,128)(2,1)S(1)} collective-permute-done((bf16[48,3584]{1,0:T(8,128)(2,1)S(1)}, bf16[48,3584]{1,0:T(8,128)(2,1)S(1)}, u32[]{:S(2)}, u32[]{:S(2)}) %collective-permute-start.12) | collective-permute-done | bytes 344096 | tf_op jit(solution)/shard_map/ppermute | solution.py:21
  53.9 1.8 %collective-permute-start.17 = (bf16[24,3584]{1,0:T(8,128)(2,1)S(1)}, bf16[24,3584]{1,0:T(8,128)(2,1)S(1)}, u32[]{:S(2)}, u32[]{:S(2)}) collective-permute-start(bf16[24,3584]{1,0:T(8,128)(2,1)S(1)} %add_convert_fusion.6), channel_id=1, source_target_pairs={{0,2},{1,5},{2,0},{3,7},{4,6},{5,1},{6,4},{7,3},{8,10},{9,13},{10,... | collective-permute-start | bytes 516104 | tf_op jit(solution)/shard_map/ppermute | solution.py:21
  55.8 1.4 %collective-permute-start.16 = (bf16[24,3584]{1,0:T(8,128)(2,1)S(1)}, bf16[24,3584]{1,0:T(8,128)(2,1)S(1)}, u32[]{:S(2)}, u32[]{:S(2)}) collective-permute-start(bf16[24,3584]{1,0:T(8,128)(2,1)S(1)} %add_convert_fusion.5), channel_id=1, source_target_pairs={{0,24},{1,25},{2,26},{3,27},{4,28},{5,29},{6,30},{7,31},{8,16},{9,... | collective-permute-start | bytes 516104 | tf_op jit(solution)/shard_map/ppermute | solution.py:21
  58.0 1.4 %collective-permute-done.19 = bf16[48,3584]{1,0:T(8,128)(2,1)S(1)} collective-permute-done((bf16[48,3584]{1,0:T(8,128)(2,1)S(1)}, bf16[48,3584]{1,0:T(8,128)(2,1)S(1)}, u32[]{:S(2)}, u32[]{:S(2)}) %collective-permute-start.19) | collective-permute-done | bytes 344096 | tf_op jit(solution)/shard_map/ppermute | solution.py:21
  59.4 1.8 %collective-permute-start.20 = (bf16[24,3584]{1,0:T(8,128)(2,1)S(1)}, bf16[24,3584]{1,0:T(8,128)(2,1)S(1)}, u32[]{:S(2)}, u32[]{:S(2)}) collective-permute-start(bf16[24,3584]{1,0:T(8,128)(2,1)S(1)} %add_convert_fusion.2), channel_id=1, source_target_pairs={{0,2},{1,5},{2,0},{3,7},{4,6},{5,1},{6,4},{7,3},{8,10},{9,13},{10,... | collective-permute-start | bytes 516104 | tf_op jit(solution)/shard_map/ppermute | solution.py:21
  61.4 3.5 %collective-permute-done.20 = bf16[24,3584]{1,0:T(8,128)(2,1)S(1)} collective-permute-done((bf16[24,3584]{1,0:T(8,128)(2,1)S(1)}, bf16[24,3584]{1,0:T(8,128)(2,1)S(1)}, u32[]{:S(2)}, u32[]{:S(2)}) %collective-permute-start.20) | collective-permute-done | bytes 172064 | tf_op jit(solution)/shard_map/ppermute | solution.py:21
  66.2 2.1 %collective-permute-start.15 = (bf16[24,3584]{1,0:T(8,128)(2,1)S(1)}, bf16[24,3584]{1,0:T(8,128)(2,1)S(1)}, u32[]{:S(2)}, u32[]{:S(2)}) collective-permute-start(bf16[24,3584]{1,0:T(8,128)(2,1)S(1)} %add_convert_fusion.4), channel_id=1, source_target_pairs={{0,2},{1,5},{2,0},{3,7},{4,6},{5,1},{6,4},{7,3},{8,10},{9,13},{10,... | collective-permute-start | bytes 516104 | tf_op jit(solution)/shard_map/ppermute | solution.py:21
  69.6 3.1 %collective-permute-done.18.refs_2_ = bf16[24,3584]{1,0:T(8,128)(2,1)S(1)} collective-permute-done((bf16[24,3584]{1,0:T(8,128)(2,1)S(1)}, bf16[24,3584]{1,0:T(8,128)(2,1)S(1)}, u32[]{:S(2)}, u32[]{:S(2)}) %collective-permute-start.18) | collective-permute-done | bytes 172064 | tf_op jit(solution)/shard_map/ppermute | solution.py:21
  (56 shorter events, 12.5 us)
Async XLA Ops:
  3.1 8.1 %collective-permute-start = (bf16[24,3584]{1,0:T(8,128)(2,1)}, bf16[24,3584]{1,0:T(8,128)(2,1)S(1)}, u32[]{:S(2)}, u32[]{:S(2)}) collective-permute-start(bf16[24,3584]{1,0:T(8,128)(2,1)} %get-tuple-element.64), channel_id=1, source_target_pairs={{0,2},{1,5},{2,0},{3,7},{4,6},{5,1},{6,4},{7,3},{8,10},{9,13},{10,... | collective-permute-start | bytes 516104 | tf_op jit(solution)/shard_map/ppermute | solution.py:21
  6.1 9.3 %collective-permute-start.2 = (bf16[24,3584]{1,0:T(8,128)(2,1)}, bf16[24,3584]{1,0:T(8,128)(2,1)S(1)}, u32[]{:S(2)}, u32[]{:S(2)}) collective-permute-start(bf16[24,3584]{1,0:T(8,128)(2,1)} %get-tuple-element.67), channel_id=1, source_target_pairs={{0,24},{1,25},{2,26},{3,27},{4,28},{5,29},{6,30},{7,31},{8,16},{9,... | collective-permute-start | bytes 516104 | tf_op jit(solution)/shard_map/ppermute | solution.py:21
  9.7 8.1 %collective-permute-start.3 = (bf16[24,3584]{1,0:T(8,128)(2,1)}, bf16[24,3584]{1,0:T(8,128)(2,1)S(1)}, u32[]{:S(2)}, u32[]{:S(2)}) collective-permute-start(bf16[24,3584]{1,0:T(8,128)(2,1)} %get-tuple-element.72), channel_id=1, source_target_pairs={{0,8},{1,9},{2,10},{3,11},{4,12},{5,13},{6,14},{7,15},{8,0},{9,1},... | collective-permute-start | bytes 516104 | tf_op jit(solution)/shard_map/ppermute | solution.py:21
  9.7 26.7 %collective-permute-start.7 = (bf16[3584,256]{1,0:T(8,128)(2,1)}, bf16[3584,256]{1,0:T(8,128)(2,1)S(1)}, u32[]{:S(2)}, u32[]{:S(2)}) collective-permute-start(bf16[3584,256]{1,0:T(8,128)(2,1)} %bitcast.7), channel_id=1, source_target_pairs={{0,1},{1,0},{2,3},{3,2},{4,5},{5,4},{6,7},{7,6},{8,9},{9,8},{10,11... | collective-permute-start | bytes 5505032 | tf_op jit(solution)/shard_map/ppermute | solution.py:21
  9.7 26.7 %collective-permute-start.8 = (bf16[128,3584]{1,0:T(8,128)(2,1)}, bf16[128,3584]{1,0:T(8,128)(2,1)S(1)}, u32[]{:S(2)}, u32[]{:S(2)}) collective-permute-start(bf16[128,3584]{1,0:T(8,128)(2,1)} %bitcast.10), channel_id=1, source_target_pairs={{0,1},{1,0},{2,3},{3,2},{4,5},{5,4},{6,7},{7,6},{8,9},{9,8},{10,11... | collective-permute-start | bytes 2752520 | tf_op jit(solution)/shard_map/ppermute | solution.py:21
  11.2 25.2 %collective-permute-start.1 = (bf16[48,3584]{1,0:T(8,128)(2,1)S(1)}, bf16[48,3584]{1,0:T(8,128)(2,1)S(1)}, u32[]{:S(2)}, u32[]{:S(2)}) collective-permute-start(bf16[48,3584]{1,0:T(8,128)(2,1)S(1)} %constant_dynamic-update-slice_fusion.refs_0_), channel_id=1, source_target_pairs={{0,4},{1,3},{2,6},{3,1},{4,0},{5,7},{6,2},{7,5},{8,12},{9,11},{10,... | collective-permute-start | bytes 1032200 | tf_op jit(solution)/shard_map/ppermute | solution.py:21
  17.9 7.3 %collective-permute-start.4 = (bf16[48,3584]{1,0:T(8,128)(2,1)S(1)}, bf16[48,3584]{1,0:T(8,128)(2,1)S(1)}, u32[]{:S(2)}, u32[]{:S(2)}) collective-permute-start(bf16[48,3584]{1,0:T(8,128)(2,1)S(1)} %pad_maximum_fusion), channel_id=1, source_target_pairs={{0,2},{1,5},{2,0},{3,7},{4,6},{5,1},{6,4},{7,3},{8,10},{9,13},{10,... | collective-permute-start | bytes 1032200 | tf_op jit(solution)/shard_map/ppermute | solution.py:21
  19.4 9.5 %collective-permute-start.5 = (bf16[24,3584]{1,0:T(8,128)(2,1)}, bf16[24,3584]{1,0:T(8,128)(2,1)S(1)}, u32[]{:S(2)}, u32[]{:S(2)}) collective-permute-start(bf16[24,3584]{1,0:T(8,128)(2,1)} %get-tuple-element.79), channel_id=1, source_target_pairs={{0,16},{1,17},{2,18},{3,19},{4,20},{5,21},{6,22},{7,23},{8,24},{9,... | collective-permute-start | bytes 516104 | tf_op jit(solution)/shard_map/ppermute | solution.py:21
  25.2 12.8 %collective-permute-start.6 = (bf16[96,3584]{1,0:T(8,128)(2,1)S(1)}, bf16[96,3584]{1,0:T(8,128)(2,1)S(1)}, u32[]{:S(2)}, u32[]{:S(2)}) collective-permute-start(bf16[96,3584]{1,0:T(8,128)(2,1)S(1)} %constant_dynamic-update-slice_fusion.2.refs_2_), channel_id=1, source_target_pairs={{0,4},{1,3},{2,6},{3,1},{4,0},{5,7},{6,2},{7,5},{8,12},{9,11},{10,... | collective-permute-start | bytes 2064392 | tf_op jit(solution)/shard_map/ppermute | solution.py:21
  28.9 7.1 %collective-permute-start.9 = (bf16[24,3584]{1,0:T(8,128)(2,1)S(1)}, bf16[24,3584]{1,0:T(8,128)(2,1)S(1)}, u32[]{:S(2)}, u32[]{:S(2)}) collective-permute-start(bf16[24,3584]{1,0:T(8,128)(2,1)S(1)} %collective-permute-done.5), channel_id=1, source_target_pairs={{0,2},{1,5},{2,0},{3,7},{4,6},{5,1},{6,4},{7,3},{8,10},{9,13},{10,... | collective-permute-start | bytes 516104 | tf_op jit(solution)/shard_map/ppermute | solution.py:21
  36.1 7.3 %collective-permute-start.11 = (bf16[48,3584]{1,0:T(8,128)(2,1)S(1)}, bf16[48,3584]{1,0:T(8,128)(2,1)S(1)}, u32[]{:S(2)}, u32[]{:S(2)}) collective-permute-start(bf16[48,3584]{1,0:T(8,128)(2,1)S(1)} %constant_dynamic-update-slice_fusion.5.refs_0_), channel_id=1, source_target_pairs={{0,4},{1,3},{2,6},{3,1},{4,0},{5,7},{6,2},{7,5},{8,12},{9,11},{10,... | collective-permute-start | bytes 1032200 | tf_op jit(solution)/shard_map/ppermute | solution.py:21
  40.5 7.3 %collective-permute-start.10 = (bf16[48,3584]{1,0:T(8,128)(2,1)S(1)}, bf16[48,3584]{1,0:T(8,128)(2,1)S(1)}, u32[]{:S(2)}, u32[]{:S(2)}) collective-permute-start(bf16[48,3584]{1,0:T(8,128)(2,1)S(1)} %get-tuple-element.88), channel_id=1, source_target_pairs={{0,4},{1,3},{2,6},{3,1},{4,0},{5,7},{6,2},{7,5},{8,12},{9,11},{10,... | collective-permute-start | bytes 1032200 | tf_op jit(solution)/shard_map/ppermute | solution.py:21
  44.6 2.2 %collective-permute-start.22 = (bf16[16,24,128]{2,1,0:T(8,128)(2,1)S(1)}, bf16[16,24,128]{2,1,0:T(8,128)(2,1)S(1)}, u32[]{:S(2)}, u32[]{:S(2)}) collective-permute-start(bf16[16,24,128]{2,1,0:T(8,128)(2,1)S(1)} %get-tuple-element.119), channel_id=1, source_target_pairs={{0,1},{1,0},{2,3},{3,2},{4,5},{5,4},{6,7},{7,6},{8,9},{9,8},{10,11... | collective-permute-start | bytes 294920 | tf_op jit(solution)/shard_map/ppermute | solution.py:21
  44.7 9.2 %collective-permute-start.12 = (bf16[48,3584]{1,0:T(8,128)(2,1)S(1)}, bf16[48,3584]{1,0:T(8,128)(2,1)S(1)}, u32[]{:S(2)}, u32[]{:S(2)}) collective-permute-start(bf16[48,3584]{1,0:T(8,128)(2,1)S(1)} %get-tuple-element.97), channel_id=1, source_target_pairs={{0,4},{1,3},{2,6},{3,1},{4,0},{5,7},{6,2},{7,5},{8,12},{9,11},{10,... | collective-permute-start | bytes 1032200 | tf_op jit(solution)/shard_map/ppermute | solution.py:21
  45.1 14.3 %collective-permute-start.19 = (bf16[48,3584]{1,0:T(8,128)(2,1)S(1)}, bf16[48,3584]{1,0:T(8,128)(2,1)S(1)}, u32[]{:S(2)}, u32[]{:S(2)}) collective-permute-start(bf16[48,3584]{1,0:T(8,128)(2,1)S(1)} %get-tuple-element.106), channel_id=1, source_target_pairs={{0,4},{1,3},{2,6},{3,1},{4,0},{5,7},{6,2},{7,5},{8,12},{9,11},{10,... | collective-permute-start | bytes 1032200 | tf_op jit(solution)/shard_map/ppermute | solution.py:21
  46.8 21.5 %collective-permute-start.23 = (bf16[16,2,24,128]{3,2,1,0:T(8,128)(2,1)S(1)}, bf16[16,2,24,128]{3,2,1,0:T(8,128)(2,1)S(1)}, u32[]{:S(2)}, u32[]{:S(2)}) collective-permute-start(bf16[16,2,24,128]{3,2,1,0:T(8,128)(2,1)S(1)} %shard_map.90.mine_ref), channel_id=1, source_target_pairs={{0,16},{1,17},{2,18},{3,19},{4,20},{5,21},{6,22},{7,23},{8,24},{9,... | collective-permute-start | bytes 589832 | tf_op jit(solution)/shard_map/ppermute | solution.py:21
  47.9 7.8 %collective-permute-start.13 = (bf16[24,3584]{1,0:T(8,128)(2,1)S(1)}, bf16[24,3584]{1,0:T(8,128)(2,1)S(1)}, u32[]{:S(2)}, u32[]{:S(2)}) collective-permute-start(bf16[24,3584]{1,0:T(8,128)(2,1)S(1)} %add_convert_fusion.7), channel_id=1, source_target_pairs={{0,2},{1,5},{2,0},{3,7},{4,6},{5,1},{6,4},{7,3},{8,10},{9,13},{10,... | collective-permute-start | bytes 516104 | tf_op jit(solution)/shard_map/ppermute | solution.py:21
  53.9 7.3 %collective-permute-start.17 = (bf16[24,3584]{1,0:T(8,128)(2,1)S(1)}, bf16[24,3584]{1,0:T(8,128)(2,1)S(1)}, u32[]{:S(2)}, u32[]{:S(2)}) collective-permute-start(bf16[24,3584]{1,0:T(8,128)(2,1)S(1)} %add_convert_fusion.6), channel_id=1, source_target_pairs={{0,2},{1,5},{2,0},{3,7},{4,6},{5,1},{6,4},{7,3},{8,10},{9,13},{10,... | collective-permute-start | bytes 516104 | tf_op jit(solution)/shard_map/ppermute | solution.py:21
  55.8 13.8 %collective-permute-start.16 = (bf16[24,3584]{1,0:T(8,128)(2,1)S(1)}, bf16[24,3584]{1,0:T(8,128)(2,1)S(1)}, u32[]{:S(2)}, u32[]{:S(2)}) collective-permute-start(bf16[24,3584]{1,0:T(8,128)(2,1)S(1)} %add_convert_fusion.5), channel_id=1, source_target_pairs={{0,24},{1,25},{2,26},{3,27},{4,28},{5,29},{6,30},{7,31},{8,16},{9,... | collective-permute-start | bytes 516104 | tf_op jit(solution)/shard_map/ppermute | solution.py:21
  57.2 8.9 %collective-permute-start.14 = (bf16[48,3584]{1,0:T(8,128)(2,1)S(1)}, bf16[48,3584]{1,0:T(8,128)(2,1)S(1)}, u32[]{:S(2)}, u32[]{:S(2)}) collective-permute-start(bf16[48,3584]{1,0:T(8,128)(2,1)S(1)} %get-tuple-element.102), channel_id=1, source_target_pairs={{0,4},{1,3},{2,6},{3,1},{4,0},{5,7},{6,2},{7,5},{8,12},{9,11},{10,... | collective-permute-start | bytes 1032200 | tf_op jit(solution)/shard_map/ppermute | solution.py:21
  59.4 5.5 %collective-permute-start.20 = (bf16[24,3584]{1,0:T(8,128)(2,1)S(1)}, bf16[24,3584]{1,0:T(8,128)(2,1)S(1)}, u32[]{:S(2)}, u32[]{:S(2)}) collective-permute-start(bf16[24,3584]{1,0:T(8,128)(2,1)S(1)} %add_convert_fusion.2), channel_id=1, source_target_pairs={{0,2},{1,5},{2,0},{3,7},{4,6},{5,1},{6,4},{7,3},{8,10},{9,13},{10,... | collective-permute-start | bytes 516104 | tf_op jit(solution)/shard_map/ppermute | solution.py:21
  61.3 11.3 %collective-permute-start.18 = (bf16[24,3584]{1,0:T(8,128)(2,1)S(1)}, bf16[24,3584]{1,0:T(8,128)(2,1)S(1)}, u32[]{:S(2)}, u32[]{:S(2)}) collective-permute-start(bf16[24,3584]{1,0:T(8,128)(2,1)S(1)} %add_convert_fusion.3), channel_id=1, source_target_pairs={{0,16},{1,17},{2,18},{3,19},{4,20},{5,21},{6,22},{7,23},{8,24},{9,... | collective-permute-start | bytes 516104 | tf_op jit(solution)/shard_map/ppermute | solution.py:21
  65.0 8.7 %collective-permute-start.21 = (bf16[24,3584]{1,0:T(8,128)(2,1)S(1)}, bf16[24,3584]{1,0:T(8,128)(2,1)S(1)}, u32[]{:S(2)}, u32[]{:S(2)}) collective-permute-start(bf16[24,3584]{1,0:T(8,128)(2,1)S(1)} %add_convert_fusion.1), channel_id=1, source_target_pairs={{0,8},{1,9},{2,10},{3,11},{4,12},{5,13},{6,14},{7,15},{8,0},{9,1},... | collective-permute-start | bytes 516104 | tf_op jit(solution)/shard_map/ppermute | solution.py:21
  66.2 7.5 %collective-permute-start.15 = (bf16[24,3584]{1,0:T(8,128)(2,1)S(1)}, bf16[24,3584]{1,0:T(8,128)(2,1)S(1)}, u32[]{:S(2)}, u32[]{:S(2)}) collective-permute-start(bf16[24,3584]{1,0:T(8,128)(2,1)S(1)} %add_convert_fusion.4), channel_id=1, source_target_pairs={{0,2},{1,5},{2,0},{3,7},{4,6},{5,1},{6,4},{7,3},{8,10},{9,13},{10,... | collective-permute-start | bytes 516104 | tf_op jit(solution)/shard_map/ppermute | solution.py:21
  (5 other events, 119.1 us)
